TPU v7x, 512 devices: a whole 4x8x8 slice. The times are simulated.
512 devices in a mesh: sample: 8 (over z), ctx: 16 (over y, core), head: 4 (over x).
Axes of the slice: x: 4, y: 8, z: 8, core: 2. Of those that a mesh axis runs over, the one named last changes fastest.
Arguments:
- prompt_query: bfloat16 [2048, 32, 128], P(('sample', 'ctx'), 'head'), may hold values from -1.5 to 1.5
- prompt_key: bfloat16 [2048, 32, 128], P(('sample', 'ctx'), 'head'), may hold values from -1.5 to 1.5
- prompt_value: bfloat16 [2048, 32, 128], P(('sample', 'ctx'), 'head'), may hold values from -1.5 to 1.5
- prompt_grad: bfloat16 [2048, 32, 128], P(('sample', 'ctx'), 'head'), may hold values from -6 to 6
- prompt_decay: float32 [32, 2048], P('head', ('sample', 'ctx')), may hold values from -1 to 0, as said below
- reply_query: bfloat16 [8, 2048, 32, 128], P('sample', 'ctx', 'head'), may hold values from -1.5 to 1.5
- reply_key: bfloat16 [8, 2048, 32, 128], P('sample', 'ctx', 'head'), may hold values from -1.5 to 1.5
- reply_value: bfloat16 [8, 2048, 32, 128], P('sample', 'ctx', 'head'), may hold values from -1.5 to 1.5
- reply_grad: bfloat16 [8, 2048, 32, 128], P('sample', 'ctx', 'head'), may hold values from -6 to 6
- reply_decay: float32 [8, 32, 2048], P('sample', 'head', 'ctx'), may hold values from -1 to 0, as said below
- reply_lengths: int32 [8], P('sample'), may hold values from 1 to 2048, 10240 in all
- norm_gain: bfloat16 [32, 128], P('head'), may hold values from 0.099609375 to 1.8984375
Outputs:
- prompt_query_grad: bfloat16 [2048, 32, 128], P(('sample', 'ctx'), 'head')
- prompt_key_grad: bfloat16 [2048, 32, 128], P(('sample', 'ctx'), 'head')
- prompt_value_grad: bfloat16 [2048, 32, 128], P(('sample', 'ctx'), 'head')
- reply_query_grad: bfloat16 [8, 2048, 32, 128], P('sample', 'ctx', 'head')
- reply_key_grad: bfloat16 [8, 2048, 32, 128], P('sample', 'ctx', 'head')
- reply_value_grad: bfloat16 [8, 2048, 32, 128], P('sample', 'ctx', 'head')
Inputs may be any that keep to these rules, and one draw needn't show every extreme that they name: `reply_lengths`: each response's length in tokens; the longest is exactly 2048. `prompt_decay`: never positive. `reply_decay`: never positive.
All inputs are finite; a program needn't handle non-finite values. No bound on the sum of `reply_lengths` on one device may be relied on, other than what follows from the above.
Results may differ from a plain program's by a relative error of at most 0.0051.
Values sent between devices are 32-bit elements; how exact they have to be, the bound alone decides.
No kernel may reach another device: no remote copies, remote signals or barrier semaphores. Data moves between devices by JAX's collectives and lax.ppermute only.
A program may use at most 128 MiB of HBM per device.

v0:
```python
import jax
import jax.numpy as jnp
from jax import lax
from jax.sharding import PartitionSpec as P

HIGH = lax.Precision.HIGHEST
EPSILON = 1e-05


def prefix(x, axis, combine, identity, reverse):
    count, place = (lax.axis_size(axis), lax.axis_index(axis))
    everything = jax.tree.map(lambda part: lax.all_gather(part, axis), x)
    start = jax.tree.map(
        lambda part, zero: jnp.broadcast_to(jnp.asarray(zero, part.dtype), part.shape), x, identity
    )

    def turn(k, before):
        at = count - 1 - k if reverse else k
        reached = at > place if reverse else at < place
        new = combine(before, jax.tree.map(lambda part: part[at], everything))
        return jax.tree.map(lambda a, b: jnp.where(reached, a, b), new, before)

    return lax.fori_loop(0, count, turn, start)


def from_root(block, axis, owner):
    block = jnp.where(lax.axis_index(axis) == owner, block, jnp.zeros_like(block))
    return lax.psum(block, axis)


def decay_mask(running):
    extent = running.shape[1]
    row_ids = lax.broadcasted_iota(jnp.int32, (extent, extent), 0)
    col_ids = lax.broadcasted_iota(jnp.int32, (extent, extent), 1)
    causal = (row_ids >= col_ids)[None]
    spread = running[:, :, None] - running[:, None, :]
    return jnp.where(causal, jnp.exp(jnp.where(causal, spread, 0.0)), 0.0)


def front_pass(queries, key_rows, values, running, state_in):
    masking = decay_mask(running)
    scores = jnp.einsum("thd,shd->hts", queries, key_rows, preferred_element_type=jnp.float32)
    weights = (scores * masking).astype(jnp.bfloat16)
    carried = jnp.einsum("thd,hde->the", queries.astype(jnp.float32), state_in, precision=HIGH)
    local = jnp.einsum("hts,she->the", weights, values, preferred_element_type=jnp.float32)
    return (masking, weights, local + jnp.exp(running).T[:, :, None] * carried)


def forward_summary(key_rows, values, running):
    to_end = jnp.exp(running[:, -1:] - running)
    weighted = key_rows.astype(jnp.float32) * to_end.T[:, :, None]
    summary = jnp.einsum("thd,the->hde", weighted, values.astype(jnp.float32), precision=HIGH)
    return (jnp.exp(running[:, -1]), summary)


def norm_back(outputs, upstream, squares, intersection, features):
    inverse = lax.rsqrt(squares / features + EPSILON)
    project = intersection * inverse * inverse / features
    return ((upstream - outputs * project[:, None, None]) * inverse[:, None, None]).astype(
        jnp.bfloat16
    )


def back_left(queries, key_rows, values, out_grad, running, masking, state_in):
    inner = jnp.einsum("thd,shd->hts", out_grad, values, preferred_element_type=jnp.float32)
    grad_weights = (inner * masking).astype(jnp.bfloat16)
    carried = jnp.einsum("the,hde->thd", out_grad.astype(jnp.float32), state_in, precision=HIGH)
    local = jnp.einsum("hts,shd->thd", grad_weights, key_rows, preferred_element_type=jnp.float32)
    query_grad = (local + jnp.exp(running).T[:, :, None] * carried).astype(jnp.bfloat16)
    weighted = queries.astype(jnp.float32) * jnp.exp(running).T[:, :, None]
    back_state = jnp.einsum("thd,the->hde", weighted, out_grad.astype(jnp.float32), precision=HIGH)
    return (grad_weights, query_grad, back_state)


def back_right(queries, key_rows, values, out_grad, running, weights, grad_weights, adjoint):
    to_end = jnp.exp(running[:, -1:] - running).T[:, :, None]
    key_grad = jnp.einsum("hst,shd->thd", grad_weights, queries, preferred_element_type=jnp.float32)
    key_grad = key_grad + to_end * jnp.einsum(
        "the,hde->thd", values.astype(jnp.float32), adjoint, precision=HIGH
    )
    value_grad = jnp.einsum("hst,she->the", weights, out_grad, preferred_element_type=jnp.float32)
    value_grad = value_grad + to_end * jnp.einsum(
        "thd,hde->the", key_rows.astype(jnp.float32), adjoint, precision=HIGH
    )
    return (key_grad.astype(jnp.bfloat16), value_grad.astype(jnp.bfloat16))


def compose(earlier_a, earlier_b, later_a, later_b):
    return (earlier_a * later_a, later_a[..., None, None] * earlier_b + later_b)


def chain_link(earlier, later):
    prompt_a, prompt_b = compose(earlier[0], earlier[1], later[0], later[1])
    reply_a, reply_b = compose(earlier[2], earlier[3], later[2], later[3])
    return (prompt_a, prompt_b, reply_a, reply_b)


def fold_rows(every_a, every_b, reverse):
    start = (jnp.ones_like(every_a[0]), jnp.zeros_like(every_b[0]))

    def advance(carry, item):
        return (compose(carry[0], carry[1], item[0], item[1]), carry)

    final, prefixes = lax.scan(advance, start, (every_a, every_b), reverse=reverse)
    place = lax.axis_index("sample")
    mine_a = lax.dynamic_index_in_dim(prefixes[0], place, 0, keepdims=False)
    mine_b = lax.dynamic_index_in_dim(prefixes[1], place, 0, keepdims=False)
    return (mine_a, mine_b, final[1])


def shards(
    prompt_query,
    prompt_key,
    prompt_value,
    prompt_grad,
    prompt_decay,
    reply_query,
    reply_key,
    reply_value,
    reply_grad,
    reply_decay,
    reply_lengths,
    norm_gain,
):
    heads_here = prompt_query.shape[1]
    depth = prompt_query.shape[2]
    extent = reply_query.shape[1]
    features = float(heads_here * depth * lax.axis_size("head"))
    place = lax.axis_index("ctx")
    positions = place * extent + lax.iota(jnp.int32, extent)
    live = (positions[None, :] < reply_lengths[:, None])[:, :, None, None]
    nothing = jnp.zeros((), jnp.bfloat16)
    queries = jnp.where(live, reply_query, nothing)
    key_rows = jnp.where(live, reply_key, nothing)
    values = jnp.where(live, reply_value, nothing)
    upstream_raw = jnp.where(live, reply_grad, nothing)
    scale_gain = norm_gain.astype(jnp.float32)[None]
    prompt_run = jnp.cumsum(prompt_decay, axis=1)
    reply_run = jnp.cumsum(reply_decay, axis=2)
    prompt_factor, prompt_summary = forward_summary(prompt_key, prompt_value, prompt_run)
    reply_factor, reply_summary = jax.vmap(forward_summary)(key_rows, values, reply_run)
    identity = (
        jnp.ones_like(prompt_factor),
        jnp.zeros_like(prompt_summary),
        jnp.ones_like(reply_factor),
        jnp.zeros_like(reply_summary),
    )
    before = prefix(
        (prompt_factor, prompt_summary, reply_factor, reply_summary),
        "ctx",
        chain_link,
        identity,
        False,
    )
    reply_scale = before[2]
    reply_prior = before[3]
    row_a, row_b = compose(before[0], before[1], prompt_factor, prompt_summary)
    row_a, row_b = (
        from_root(row_a, "ctx", lax.axis_size("ctx") - 1),
        from_root(row_b, "ctx", lax.axis_size("ctx") - 1),
    )
    every_a, every_b = (
        lax.all_gather(row_a[None], "sample", axis=0, tiled=True),
        lax.all_gather(row_b[None], "sample", axis=0, tiled=True),
    )
    upper_a, upper_b, prompt_end = fold_rows(every_a, every_b, False)
    prompt_state = compose(upper_a, upper_b, before[0], before[1])[1]
    reply_state = reply_scale[:, :, None, None] * prompt_end[None] + reply_prior
    prompt_mask, prompt_weights, prompt_out = front_pass(
        prompt_query, prompt_key, prompt_value, prompt_run, prompt_state
    )
    reply_mask, reply_weights, reply_out = jax.vmap(front_pass)(
        queries, key_rows, values, reply_run, reply_state
    )
    prompt_up = prompt_grad.astype(jnp.float32) * scale_gain
    reply_up = upstream_raw.astype(jnp.float32) * scale_gain[None]
    totals = lax.psum(
        (
            jnp.sum(prompt_out * prompt_out, axis=(1, 2)),
            jnp.sum(prompt_up * prompt_out, axis=(1, 2)),
            jnp.sum(reply_out * reply_out, axis=(2, 3)),
            jnp.sum(reply_up * reply_out, axis=(2, 3)),
        ),
        "head",
    )
    prompt_ograd = norm_back(prompt_out, prompt_up, totals[0], totals[1], features)
    reply_ograd = jax.vmap(norm_back, in_axes=(0, 0, 0, 0, None))(
        reply_out, reply_up, totals[2], totals[3], features
    )
    prompt_gw, prompt_qgrad, prompt_back = back_left(
        prompt_query, prompt_key, prompt_value, prompt_ograd, prompt_run, prompt_mask, prompt_state
    )
    reply_gw, reply_qgrad, reply_back = jax.vmap(back_left)(
        queries, key_rows, values, reply_ograd, reply_run, reply_mask, reply_state
    )
    adjoint_term = jnp.sum(reply_scale[:, :, None, None] * reply_back, axis=0)
    total_adjoint = lax.psum(adjoint_term, ("sample", "ctx"))
    after = prefix(
        (prompt_factor, prompt_back, reply_factor, reply_back), "ctx", chain_link, identity, True
    )
    tail_a, tail_b = compose(after[0], after[1], prompt_factor, prompt_back)
    tail_a, tail_b = (from_root(tail_a, "ctx", 0), from_root(tail_b, "ctx", 0))
    every_a, every_b = (
        lax.all_gather(tail_a[None], "sample", axis=0, tiled=True),
        lax.all_gather(tail_b[None], "sample", axis=0, tiled=True),
    )
    lower_a, lower_b, unused = fold_rows(every_a, every_b, True)
    full_a, full_b = compose(lower_a, lower_b, after[0], after[1])
    prompt_adjoint = full_a[:, None, None] * total_adjoint + full_b
    reply_adjoint = after[3]
    prompt_kgrad, prompt_vgrad = back_right(
        prompt_query,
        prompt_key,
        prompt_value,
        prompt_ograd,
        prompt_run,
        prompt_weights,
        prompt_gw,
        prompt_adjoint,
    )
    reply_kgrad, reply_vgrad = jax.vmap(back_right)(
        queries, key_rows, values, reply_ograd, reply_run, reply_weights, reply_gw, reply_adjoint
    )
    return (prompt_qgrad, prompt_kgrad, prompt_vgrad, reply_qgrad, reply_kgrad, reply_vgrad)


def solution(mesh):
    in_specs = (
        P(("sample", "ctx"), "head", None),
        P(("sample", "ctx"), "head", None),
        P(("sample", "ctx"), "head", None),
        P(("sample", "ctx"), "head", None),
        P("head", ("sample", "ctx")),
        P("sample", "ctx", "head", None),
        P("sample", "ctx", "head", None),
        P("sample", "ctx", "head", None),
        P("sample", "ctx", "head", None),
        P("sample", "head", "ctx"),
        P("sample"),
        P("head", None),
    )
    out_specs = (
        P(("sample", "ctx"), "head", None),
        P(("sample", "ctx"), "head", None),
        P(("sample", "ctx"), "head", None),
        P("sample", "ctx", "head", None),
        P("sample", "ctx", "head", None),
        P("sample", "ctx", "head", None),
    )
    return jax.shard_map(shards, mesh=mesh, in_specs=in_specs, out_specs=out_specs, check_vma=False)
```

profile of v0, /device:TPU:1, one launch (start us, length us, event | category | flops | bytes accessed | tf_op | source)
XLA Modules:
  0.0 948.0 jit_solution(9210615028966658343)
XLA Ops:
  8.4 2.2 fusion.79
  14.9 1.5 fusion.47
  18.7 30.8 %all-reduce = f32[128]{0:T(128)S(1)} all-reduce(f32[128]{0:T(128)S(1)} %dynamic-update-slice), channel_id=2, replica_groups=mesh['sample'=8,'ctx'=16,'head'=4] {'ctx'}, use_global_device_ids=true, to_apply=%add | all-reduce | flops 128 | bytes 1024
  49.6 14.9 %all-gather.2 = f32[16,8,1]{1,2,0:T(1,128)S(1)} all-gather(f32[1,8,1]{1,2,0:T(1,128)S(1)} %copy.108), channel_id=4, replica_groups=mesh['sample'=8,'ctx'=16,'head'=4] {'ctx'}, dimensions={0}, use_global_device_ids=true | all-gather | bytes 544 | tf_op jit(solution)/shard_map/all_gather | solution.py:12
  64.6 10.6 %all-gather.19.cloned.1.call-done = f32[128,128,128]{2,1,0:T(8,128)} async-done(((f32[8,128,128]{2,1,0:T(8,128)}), f32[128,128,128]{2,1,0:T(8,128)}) %all-gather.19.cloned.1.call-update) | async-done | bytes 8388624 | tf_op jit(solution)/shard_map/all_gather | solution.py:12
  75.2 59.4 %all-gather.21.cloned.1.call-done = f32[128,128,128]{2,1,0:T(8,128)} async-done(((f32[8,128,128]{2,1,0:T(8,128)}), f32[128,128,128]{2,1,0:T(8,128)}) %all-gather.21.cloned.1.call-update) | async-done | bytes 8388624 | tf_op jit(solution)/shard_map/all_gather | solution.py:12
  134.6 39.1 %while.74 = (s32[]{:T(128)}, f32[8]{0:T(128)S(1)}, f32[8,128,128]{2,1,0:T(8,128)S(1)}, f32[1,8]{1,0:T(1,128)S(1)}, f32[1,8,128,128]{3,2,1,0:T(8,128)S(1)}, /*ind...) while((s32[]{:T(128)}, f32[8]{0:T(128)S(1)}, ...), condition=%wide.region_3.4_spmd.clone, body=%wide.region_2.3_spmd.clone.sunk | while | flops 1048628 | bytes 3146251 | solution.py:23
  174.8 113.6 %all-reduce.6.cloned.1.call-done = f32[1,8,128,128]{3,2,1,0:T(8,128)} async-done(((f32[1,8,128,128]{3,2,1,0:T(8,128)}), f32[1,8,128,128]{3,2,1,0:T(8,128)}) %all-reduce.6.cloned.1.call-update) | async-done | bytes 524304 | tf_op jit(solution)/shard_map/psum | solution.py:28
  289.6 24.1 %psum.63 = f32[1,8]{1,0:T(1,128)S(1)} all-reduce(f32[1,8]{1,0:T(1,128)S(1)} %get-tuple-element.851), channel_id=1, replica_groups=mesh['sample'=8,'ctx'=16,'head'=4] {'ctx'}, use_global_device_ids=true, to_apply=%region_4.5 | all-reduce | flops 8 | bytes 64 | tf_op jit(solution)/shard_map/psum | solution.py:28
  313.7 14.9 %all-gather.6 = f32[8,1,8]{2,1,0:T(1,128)S(1)} all-gather(f32[1,1,8]{2,1,0:T(1,128)S(1)} %bitcast.304), channel_id=1, replica_groups=mesh['sample'=8,'ctx'=16,'head'=4] {'sample'}, dimensions={0}, use_global_device_ids=true | all-gather | bytes 288 | tf_op jit(solution)/shard_map/all_gather | solution.py:163
  328.5 21.1 %all-gather.15.cloned.1.call-done = f32[8,8,128,128]{3,2,1,0:T(8,128)} async-done(((f32[1,8,128,128]{3,2,1,0:T(8,128)}), f32[8,8,128,128]{3,2,1,0:T(8,128)}) %all-gather.15.cloned.1.call-update) | async-done | bytes 4194320 | tf_op jit(solution)/shard_map/all_gather | solution.py:164
  349.7 2.5 broadcast.95.clone
  352.1 16.1 %while.75 = (s32[]{:T(128)}, f32[8,128,128]{2,1,0:T(8,128)S(1)}, f32[8,8,128,128]{3,2,1,0:T(8,128)}, f32[8,8]{1,0:T(8,128)S(1)}, f32[8,8,128,128]{3,2,1,0:T(8,128)}, /*index=5*/s32[]{:T(128)}, s32[]{:T(128)}) while((s32[]{:T(128)}, f32[8,128,128]{2,1,0:T(8,128)S(1)}, f32[8,8,128,128]{3,2,1,0:T(8,128)}, f32[8,8]{1,0:T(8,128)S(1)}, ...), condition=%wide.region_7.8_spmd.clone, body=%wide.region_6.7_spmd.clone.sunk | while | flops 524291 | bytes 2621644 | solution.py:104
  368.3 1.5 fusion.32
  369.8 1.4 multiply_reduce_fusion.3
  373.0 8.4 all-reduce.1
  382.4 1.5 fusion.76
  384.8 2.3 broadcast_multiply_fusion
  387.2 53.4 %all-gather.23.cloned.1.call-done = f32[128,128,128]{2,1,0:T(8,128)} async-done(((f32[8,128,128]{2,1,0:T(8,128)}), f32[128,128,128]{2,1,0:T(8,128)}) %all-gather.23.cloned.1.call-update) | async-done | bytes 8388624 | tf_op jit(solution)/shard_map/all_gather | solution.py:12
  440.6 59.5 %all-gather.25.cloned.1.call-done = f32[128,128,128]{2,1,0:T(8,128)} async-done(((f32[8,128,128]{2,1,0:T(8,128)}), f32[128,128,128]{2,1,0:T(8,128)}) %all-gather.25.cloned.1.call-update) | async-done | bytes 8388624 | tf_op jit(solution)/shard_map/all_gather | solution.py:12
  500.1 68.9 %while.76 = (s32[]{:T(128)}, f32[8]{0:T(128)}, f32[8,128,128]{2,1,0:T(8,128)S(1)}, f32[1,8,128,128]{3,2,1,0:T(8,128)S(1)}, s32[]{:T(128)}, /*index=5*/f32[16,8]{...) while((s32[]{:T(128)}, f32[8]{0:T(128)}, ...), condition=%wide.region_17.18_spmd.clone, body=%wide.region_16.17_spmd.clone.sunk | while | flops 1048608 | bytes 3146203 | solution.py:23
  500.1 1.3 broadcast_select_fusion.30
  504.5 1.3 broadcast_select_fusion.30
  508.8 1.3 broadcast_select_fusion.30
  513.1 1.3 broadcast_select_fusion.30
  517.4 1.3 broadcast_select_fusion.30
  521.7 1.3 broadcast_select_fusion.30
  526.0 1.3 broadcast_select_fusion.30
  530.3 1.3 broadcast_select_fusion.30
  534.6 1.3 broadcast_select_fusion.30
  538.9 1.3 broadcast_select_fusion.30
  543.2 1.3 broadcast_select_fusion.30
  547.5 1.3 broadcast_select_fusion.30
  551.8 1.3 broadcast_select_fusion.30
  556.1 1.3 broadcast_select_fusion.30
  569.1 1.5 select_bitcast_fusion
  570.6 113.6 %all-reduce.8.cloned.1.call-done = f32[1,8,128,128]{3,2,1,0:T(8,128)} async-done(((f32[1,8,128,128]{3,2,1,0:T(8,128)}), f32[1,8,128,128]{3,2,1,0:T(8,128)}) %all-reduce.8.cloned.1.call-update) | async-done | bytes 524304 | tf_op jit(solution)/shard_map/psum | solution.py:28
  685.2 1.6 fusion.31
  687.7 1.4 fusion.24
  689.1 1.5 fusion.17
  693.0 1.3 fusion.18
  695.0 25.1 %psum.69 = f32[1,8]{1,0:T(1,128)S(1)} all-reduce(f32[1,8]{1,0:T(1,128)} %fusion.105), channel_id=1, replica_groups=mesh['sample'=8,'ctx'=16,'head'=4] {'ctx'}, use_global_device_ids=true, to_apply=%region_18.19 | all-reduce | flops 8 | bytes 64 | tf_op jit(solution)/shard_map/psum | solution.py:28
  720.0 14.9 %all-gather.7 = f32[8,1,8]{2,1,0:T(1,128)S(1)} all-gather(f32[1,1,8]{2,1,0:T(1,128)S(1)} %bitcast.305), channel_id=1, replica_groups=mesh['sample'=8,'ctx'=16,'head'=4] {'sample'}, dimensions={0}, use_global_device_ids=true | all-gather | bytes 288 | tf_op jit(solution)/shard_map/all_gather | solution.py:204
  739.0 6.5 all-gather.17.cloned.1.call-done
  745.5 2.5 broadcast.95
  748.0 16.7 %while.77 = (s32[]{:T(128)}, f32[8]{0:T(128)S(1)}, f32[8,128,128]{2,1,0:T(8,128)S(1)}, f32[8,8]{1,0:T(8,128)S(1)}, f32[8,8,128,128]{3,2,1,0:T(8,128)}, /*index=5...) while((s32[]{:T(128)}, f32[8]{0:T(128)S(1)}, ...), condition=%wide.region_21.22_spmd.clone, body=%wide.region_20.21_spmd.clone.sunk | while | flops 524308 | bytes 2621845 | solution.py:104
  764.8 172.8 %all-reduce.10.cloned.1.call-done = f32[8,128,128]{2,1,0:T(8,128)} async-done(((f32[8,128,128]{2,1,0:T(8,128)}), f32[8,128,128]{2,1,0:T(8,128)}) %all-reduce.10.cloned.1.call-update) | async-done | bytes 524304 | tf_op jit(solution)/shard_map/psum | solution.py:197
  937.6 1.4 fusion.41
  (338 shorter events, 145.3 us)
Async XLA Ops:
  7.2 1.2 copy-start
  7.2 68.0 %all-gather.19.cloned.1.call-start = ((), (), s32[]{:S(2)}) async-start(), calls=%async_computation.5 | async-start | bytes 8912896 | tf_op jit(solution)/shard_map/all_gather | solution.py:12
  8.1 280.9 %copy-start.24 = (f32[8,16]{1,0:T(8,128)}, f32[8,16]{1,0:T(8,128)S(1)}, u32[]{:S(2)}) copy-start(f32[8,16]{1,0:T(8,128)S(1)} %reduce_window_sum.22) | copy-start | bytes 1540
  8.3 165.5 %copy-start.33 = (f32[8]{0:T(128)}, f32[8]{0:T(128)S(1)}, u32[]{:S(2)}) copy-start(f32[8]{0:T(128)S(1)} %get-tuple-element.765) | copy-start | bytes 100
  10.6 124.0 %all-gather.21.cloned.1.call-start = ((), (), s32[]{:S(2)}) async-start(), calls=%async_computation.6 | async-start | bytes 8912896 | tf_op jit(solution)/shard_map/all_gather | solution.py:12
  13.6 358.3 %copy-start.7 = (bf16[1,128,8,128]{1,3,2,0:T(8,128)(2,1)}, bf16[1,128,8,128]{1,3,2,0:T(8,128)(2,1)S(1)}, u32[]{:S(2)}) copy-start(bf16[1,128,8,128]{1,3,2,0:T(8,128)(2,1)S(1)} %copy.111) | copy-start | bytes 786436
  14.6 274.6 %copy-start.25 = (f32[1,8,128]{2,1,0:T(8,128)}, f32[1,8,128]{2,1,0:T(8,128)S(1)}, u32[]{:S(2)}) copy-start(f32[1,8,128]{2,1,0:T(8,128)S(1)} %reduce_window_sum.23) | copy-start | bytes 12292
  14.6 356.6 %copy-start.21 = (pred[128]{0:T(512)(128)(4,1)}, pred[128]{0:T(512)(128)(4,1)S(1)}, u32[]{:S(2)}) copy-start(pred[128]{0:T(512)(128)(4,1)S(1)} %add_compare_fusion) | copy-start | bytes 388
  14.9 356.4 %copy-start.19 = (f32[128,8]{0,1:T(8,128)}, f32[128,8]{0,1:T(8,128)S(1)}, u32[]{:S(2)}) copy-start(f32[128,8]{0,1:T(8,128)S(1)} %get-tuple-element.840) | copy-start | bytes 12292
  16.4 271.9 %all-reduce.6.cloned.1.call-start = ((), (), s32[]{:S(2)}) async-start(), calls=%async_computation | async-start | bytes 1048576 | tf_op jit(solution)/shard_map/psum | solution.py:28
  134.6 39.2 %copy-start.1 = (f32[8,128,128]{2,1,0:T(8,128)S(1)}, f32[8,128,128]{2,1,0:T(8,128)}, u32[]{:S(2)}) copy-start(f32[8,128,128]{2,1,0:T(8,128)} %fusion.79) | copy-start | bytes 1572868
  134.6 153.8 %copy-start.35 = (bf16[8,128]{1,0:T(8,128)(2,1)S(1)}, bf16[8,128]{1,0:T(8,128)(2,1)}, u32[]{:S(2)}) copy-start(bf16[8,128]{1,0:T(8,128)(2,1)} %param.31) | copy-start | bytes 6148
  134.6 153.9 %copy-start.12 = (bf16[1,128,8,128]{3,2,1,0:T(8,128)(2,1)S(1)}, bf16[1,128,8,128]{3,2,1,0:T(8,128)(2,1)}, u32[]{:S(2)}) copy-start(bf16[1,128,8,128]{3,2,1,0:T(8,128)(2,1)} %param.28) | copy-start | bytes 786436
  134.6 154.1 %copy-start.13 = (bf16[1,128,8,128]{3,2,1,0:T(8,128)(2,1)S(1)}, bf16[1,128,8,128]{3,2,1,0:T(8,128)(2,1)}, u32[]{:S(2)}) copy-start(bf16[1,128,8,128]{3,2,1,0:T(8,128)(2,1)} %param.25) | copy-start | bytes 786436
  134.6 154.4 %copy-start.10 = (bf16[16,8,128]{2,1,0:T(8,128)(2,1)S(1)}, bf16[16,8,128]{2,1,0:T(8,128)(2,1)}, u32[]{:S(2)}) copy-start(bf16[16,8,128]{2,1,0:T(8,128)(2,1)} %param.21) | copy-start | bytes 98308
  134.6 154.4 %copy-start.11 = (bf16[16,8,128]{2,1,0:T(8,128)(2,1)S(1)}, bf16[16,8,128]{2,1,0:T(8,128)(2,1)}, u32[]{:S(2)}) copy-start(bf16[16,8,128]{2,1,0:T(8,128)(2,1)} %param.20) | copy-start | bytes 98308
  173.7 114.8 %copy-start.29 = (f32[16,8]{1,0:T(8,128)}, f32[16,8]{1,0:T(8,128)S(1)}, u32[]{:S(2)}) copy-start(f32[16,8]{1,0:T(8,128)S(1)} %get-tuple-element.1222) | copy-start | bytes 1540
  173.7 114.8 %copy-start.31 = (f32[16,1,8]{2,1,0:T(1,128)}, f32[16,1,8]{2,1,0:T(1,128)S(1)}, u32[]{:S(2)}) copy-start(f32[16,1,8]{2,1,0:T(1,128)S(1)} %get-tuple-element.1223) | copy-start | bytes 1540
  173.7 194.6 %copy-start.26 = (f32[8]{0:T(128)}, f32[8]{0:T(128)S(1)}, u32[]{:S(2)}) copy-start(f32[8]{0:T(128)S(1)} %get-tuple-element.570) | copy-start | bytes 100
  173.7 197.6 %copy-start.28 = (f32[1,8]{1,0:T(1,128)}, f32[1,8]{1,0:T(1,128)S(1)}, u32[]{:S(2)}) copy-start(f32[1,8]{1,0:T(1,128)S(1)} %get-tuple-element.573) | copy-start | bytes 100
  173.8 114.7 %copy-start.34 = (f32[8]{0:T(128)}, f32[8]{0:T(128)S(1)}, u32[]{:S(2)}) copy-start(f32[8]{0:T(128)S(1)} %get-tuple-element.850) | copy-start | bytes 100
  174.7 174.9 %all-gather.15.cloned.1.call-start = ((), (), s32[]{:S(2)}) async-start(), calls=%async_computation.1 | async-start | bytes 4718592 | tf_op jit(solution)/shard_map/all_gather | solution.py:164
  288.4 152.3 %all-gather.23.cloned.1.call-start = ((), (), s32[]{:S(2)}) async-start(), calls=%async_computation.7 | async-start | bytes 8912896 | tf_op jit(solution)/shard_map/all_gather | solution.py:12
  289.0 95.8 %copy-start.3 = (bf16[1,128,8,128]{1,3,2,0:T(8,128)(2,1)}, bf16[1,128,8,128]{1,3,2,0:T(8,128)(2,1)S(1)}, u32[]{:S(2)}) copy-start(bf16[1,128,8,128]{1,3,2,0:T(8,128)(2,1)S(1)} %copy.121) | copy-start | bytes 786436
  289.0 63.2 %copy-start.36 = (pred[16,16]{1,0:T(8,128)(4,1)}, pred[16,16]{1,0:T(8,128)(4,1)S(1)}, u32[]{:S(2)}) copy-start(pred[16,16]{1,0:T(8,128)(4,1)S(1)} %iota_compare_fusion.1) | copy-start | bytes 772
  289.0 63.1 %copy-start.30 = (pred[128,128]{1,0:T(8,128)(4,1)}, pred[128,128]{1,0:T(8,128)(4,1)S(1)}, u32[]{:S(2)}) copy-start(pred[128,128]{1,0:T(8,128)(4,1)S(1)} %iota_compare_fusion) | copy-start | bytes 49156
  289.2 80.6 %copy-start.14 = (bf16[8,16,16]{2,1,0:T(8,128)(2,1)}, bf16[8,16,16]{2,1,0:T(8,128)(2,1)S(1)}, u32[]{:S(2)}) copy-start(bf16[8,16,16]{2,1,0:T(8,128)(2,1)S(1)} %fusion.33) | copy-start | bytes 12292
  289.6 82.4 %copy-start.9 = (bf16[8,128,128]{2,1,0:T(8,128)(2,1)}, bf16[8,128,128]{2,1,0:T(8,128)(2,1)S(1)}, u32[]{:S(2)}) copy-start(bf16[8,128,128]{2,1,0:T(8,128)(2,1)S(1)} %fusion.23) | copy-start | bytes 786436
  352.1 17.7 %copy-start.18 = (bf16[16,8,128]{2,1,0:T(8,128)(2,1)S(1)}, bf16[16,8,128]{2,1,0:T(8,128)(2,1)}, u32[]{:S(2)}) copy-start(bf16[16,8,128]{2,1,0:T(8,128)(2,1)} %param.23) | copy-start | bytes 98308
  383.9 116.2 %all-gather.25.cloned.1.call-start = ((), (), s32[]{:S(2)}) async-start(), calls=%async_computation.8 | async-start | bytes 8912896 | tf_op jit(solution)/shard_map/all_gather | solution.py:12
  384.8 2.3 copy-start.5
  387.2 297.0 %all-reduce.8.cloned.1.call-start = ((), (), s32[]{:S(2)}) async-start(), calls=%async_computation.2 | async-start | bytes 1048576 | tf_op jit(solution)/shard_map/psum | solution.py:28
  500.1 68.9 %copy-start.2 = (f32[8,128,128]{2,1,0:T(8,128)S(1)}, f32[8,128,128]{2,1,0:T(8,128)}, u32[]{:S(2)}) copy-start(f32[8,128,128]{2,1,0:T(8,128)} %fusion.76) | copy-start | bytes 1572868
  569.0 120.0 %copy-start.20 = (f32[128,8]{0,1:T(8,128)S(1)}, f32[128,8]{0,1:T(8,128)}, u32[]{:S(2)}) copy-start(f32[128,8]{0,1:T(8,128)} %copy-done.19) | copy-start | bytes 12292
  570.6 174.9 %all-gather.17.cloned.1.call-start = ((), (), s32[]{:S(2)}) async-start(), calls=%async_computation.3 | async-start | bytes 4718592 | tf_op jit(solution)/shard_map/all_gather | solution.py:205
  684.2 253.4 %all-reduce.10.cloned.1.call-start = ((), (), s32[]{:S(2)}) async-start(), calls=%async_computation.4 | async-start | bytes 1048576 | tf_op jit(solution)/shard_map/psum | solution.py:197
  684.3 6.3 copy-start.22
  685.2 2.4 copy-start.16
  686.9 6.2 copy-start.23
  687.7 47.3 %copy-start.4 = (bf16[1,128,8,128]{1,3,2,0:T(8,128)(2,1)S(1)}, bf16[1,128,8,128]{1,3,2,0:T(8,128)(2,1)}, u32[]{:S(2)}) copy-start(bf16[1,128,8,128]{1,3,2,0:T(8,128)(2,1)} %copy-done.3) | copy-start | bytes 786436
  689.1 1.5 copy-start.8
  689.1 47.9 %copy-start.6 = (bf16[128,8,128]{0,2,1:T(8,128)(2,1)S(1)}, bf16[128,8,128]{0,2,1:T(8,128)(2,1)}, u32[]{:S(2)}) copy-start(bf16[128,8,128]{0,2,1:T(8,128)(2,1)} %copy-done.5) | copy-start | bytes 786436
  695.0 53.0 %copy-start.32 = (f32[8]{0:T(128)S(1)}, f32[8]{0:T(128)}, u32[]{:S(2)}) copy-start(f32[8]{0:T(128)} %custom-call.8) | copy-start | bytes 100
  748.0 16.8 %copy-start.27 = (f32[8]{0:T(128)S(1)}, f32[8]{0:T(128)}, u32[]{:S(2)}) copy-start(f32[8]{0:T(128)} %get-tuple-element.576) | copy-start | bytes 100
  748.0 191.8 %copy-start.17 = (bf16[8,16,16]{2,1,0:T(8,128)(2,1)S(1)}, bf16[8,16,16]{2,1,0:T(8,128)(2,1)}, u32[]{:S(2)}) copy-start(bf16[8,16,16]{2,1,0:T(8,128)(2,1)} %copy-done.16) | copy-start | bytes 12292
  748.0 192.7 %copy-start.15 = (bf16[8,16,16]{2,1,0:T(8,128)(2,1)S(1)}, bf16[8,16,16]{2,1,0:T(8,128)(2,1)}, u32[]{:S(2)}) copy-start(bf16[8,16,16]{2,1,0:T(8,128)(2,1)} %copy-done.14) | copy-start | bytes 12292
Sparse Core Ops, SparseCore 0:
  10.7 64.4 all-gather.18
  77.3 57.2 all-gather.20
  174.8 113.4 all-reduce.5
  290.5 59.1 all-gather.14
  384.0 56.5 all-gather.22
  442.8 57.2 all-gather.24
  570.7 113.4 all-reduce.7
  686.3 59.1 all-gather.16
  748.7 188.8 all-reduce.9
where the time goes:
time: 954 us; the launch traced here: 948 us
  waiting for transfers between devices  611 us (64%)
  other arithmetic  137 us (14%)
  blocking collectives  133 us (14%)
  local copies, waits for them, and re-layouts  25.7 us (3%)
  matrix products  24.1 us (3%)
  between operations  15.9 us (2%)
    psum x2, waiting for transfers between devices, from_root(): return lax.psum(block, axis)  227 us
    all_gather x4, waiting for transfers between devices, prefix(): everything = jax.tree.map(lambda part: lax.all_gather(part, axis), x)  183 us
    psum x1, waiting for transfers between devices, shards(): total_adjoint = lax.psum(adjoint_term, ('sample', 'ctx'))  173 us
    select_n x112, other arithmetic, turn(): return jax.tree.map(lambda a, b: jnp.where(reached, a, b), new, before)  96 us
    psum x2, blocking collectives, from_root(): return lax.psum(block, axis)  49.2 us
    unnamed x1, blocking collectives  30.8 us
    all_gather x1, waiting for transfers between devices, shards(): lax.all_gather(row_b[None], 'sample', axis=0, tiled=True)  21.1 us
  transfers between devices with their start and end apart: 9, of which 9 were waited for; matrix products, arithmetic and copies ran while one was open for 5% of the time, Pallas kernels for 0%

commit v1 on v0

v1 whole, which is shorter than its diff:
```python
import jax
import jax.numpy as jnp
from jax import lax
from jax.experimental import pallas as pl
from jax.experimental.pallas import tpu as pltpu
from jax.sharding import PartitionSpec as P

EPSILON = 1e-05
F32 = jnp.float32
BF16 = jnp.bfloat16
HEADS = 8
D = 128
HALF = D // 2
T = 128
PT = 16
CTX = 16
SAMPLE = 8
HEAD_AXIS = 4
ROW = CTX * PT
FEATURES = float(HEADS * HEAD_AXIS * D)


def iota(shape, axis):
    return lax.broadcasted_iota(jnp.int32, shape, axis)


def dot(a, b, ca, cb):
    return lax.dot_general(a, b, (((ca,), (cb,)), ((), ())), preferred_element_type=F32)


def split(x):
    high = x.astype(BF16)
    return high, (x - high.astype(F32)).astype(BF16)


def split3(x):
    high, rest = x.astype(BF16), None
    rest = x - high.astype(F32)
    mid = rest.astype(BF16)
    return high, mid, (rest - mid.astype(F32)).astype(BF16)


def dot_right(a, x, ca, cb):
    return sum(dot(a, part, ca, cb) for part in split(x))


def dot_left(x, b, ca, cb):
    return sum(dot(part, b, ca, cb) for part in split(x))


def low_lanes(rows):
    return iota((rows, D), 1) < HALF


def pack(x, half):
    top, bottom, low = x[0:8], x[8:16], low_lanes(8)
    if half == 0:
        return jnp.where(low, top, pltpu.roll(bottom, HALF, 1))
    return jnp.where(low, pltpu.roll(top, HALF, 1), bottom)


def unpack(first, second):
    low = low_lanes(8)
    top = jnp.where(low, first, pltpu.roll(second, HALF, 1))
    bottom = jnp.where(low, pltpu.roll(first, HALF, 1), second)
    return jnp.concatenate([top, bottom], axis=0)


def rows_of_half(x):
    both = jnp.stack([x[:, :, :HALF], x[:, :, HALF:]], axis=1)
    return both.reshape(ROW, HALF)


def packed_half(x):
    both = x.reshape(CTX, 2, 8, HALF)
    return jnp.concatenate([both[:, 0], both[:, 1]], axis=-1)


def running_rows(decay):
    upper = (iota((T, T), 0) <= iota((T, T), 1)).astype(BF16)
    return sum(dot(part, upper, 1, 0) for part in split3(decay))


def running_columns(decay):
    lower = (iota((T, T), 1) <= iota((T, T), 0)).astype(BF16)
    return sum(dot(lower, part, 1, 1) for part in split3(decay))


def masking(column, row):
    extent = row.shape[1]
    causal = iota((extent, extent), 0) >= iota((extent, extent), 1)
    return jnp.where(causal, jnp.exp(jnp.where(causal, column - row, 0.0)), 0.0)


def column_to_row(column):
    extent = column.shape[0]
    eye = iota((extent, max(extent, D)), 0) == iota((extent, max(extent, D)), 1)
    return jnp.sum(jnp.where(eye, column, 0.0), axis=0, keepdims=True)


def row_to_column(row, extent):
    eye = iota((extent, row.shape[1]), 0) == iota((extent, row.shape[1]), 1)
    return jnp.sum(jnp.where(eye, row, 0.0), axis=1, keepdims=True)


def live_tokens(lengths):
    return lax.axis_index("ctx") * T + iota((T, 1), 0) < lengths[0]


def prompt_send_kernel(key, value, decay, reply_decay, out, rows_k, rows_v):
    rows_k[...] = key[...].astype(F32).reshape(PT * HEADS, D)
    rows_v[...] = value[...].astype(F32).reshape(PT * HEADS, D)
    wide = jnp.concatenate([decay[...], jnp.zeros((HEADS, D - PT), F32)], axis=1)
    totals = jnp.sum(reply_decay[0], axis=1, keepdims=True)
    at = iota((8, D), 0)
    for h in range(HEADS):
        k = rows_k[pl.ds(h, PT, HEADS), :]
        v = rows_v[pl.ds(h, PT, HEADS), :]
        tail = jnp.where(at == 0, wide[h : h + 1], jnp.where(at == 1, totals[h : h + 1], 0.0))
        for half in range(2):
            out[2 * h + half, 0:16, :] = k
            out[2 * h + half, 16:24, :] = pack(v, half)
            out[2 * h + half, 24:32, :] = tail


def reply_send_kernel(lengths, key, value, decay, prompt_query, out, key_out, value_out, rows_k, rows_v, rows_q):
    rows_k[...] = key[0].astype(F32).reshape(T * HEADS, D)
    rows_v[...] = value[0].astype(F32).reshape(T * HEADS, D)
    rows_q[...] = prompt_query[...].astype(F32).reshape(PT * HEADS, D)
    live = live_tokens(lengths)
    columns = running_columns(decay[0])
    to_end = jnp.exp(columns[T - 1 : T, :] - columns)
    for h in range(HEADS):
        k = jnp.where(live, rows_k[pl.ds(h, T, HEADS), :], 0.0)
        v = jnp.where(live, rows_v[pl.ds(h, T, HEADS), :], 0.0).astype(BF16)
        key_out[h] = k.astype(BF16)
        value_out[h] = v
        state = dot_right(v, k * to_end[:, h : h + 1], 0, 0)
        q = rows_q[pl.ds(h, PT, HEADS), :]
        for half in range(2):
            out[2 * h + half, 0:64, :] = state[half * HALF : (half + 1) * HALF]
            out[2 * h + half, 64:80, :] = q


def reply_local_kernel(lengths, query, grad, key, value, decay, query_out, grad_out, weights_out, local_out, rows):
    live = live_tokens(lengths)
    lines = running_rows(decay[0])
    columns = running_columns(decay[0])
    rows[...] = query[0].astype(F32).reshape(T * HEADS, D)
    for h in range(HEADS):
        q = jnp.where(live, rows[pl.ds(h, T, HEADS), :], 0.0).astype(BF16)
        query_out[h] = q
        mask = masking(columns[:, h : h + 1], lines[h : h + 1])
        weights = (dot(q, key[h], 1, 1) * mask).astype(BF16)
        weights_out[h] = weights
        local_out[h] = dot(weights, value[h], 1, 0)
    rows[...] = grad[0].astype(F32).reshape(T * HEADS, D)
    for h in range(HEADS):
        grad_out[h] = jnp.where(live, rows[pl.ds(h, T, HEADS), :], 0.0).astype(BF16)


def prompt_row_kernel(received, out, key_out, value_out, column_out, line_out):
    k = received[:, 0:16, :].reshape(ROW, D)
    v = rows_of_half(received[:, 16:24, :]).astype(BF16)
    decay = received[:, 24, :]
    token_block, token_place = iota((ROW, CTX), 0) // PT, iota((ROW, D), 0) % PT
    block = iota((ROW, CTX), 1)
    parts = split3(decay)
    own = sum(dot((block == token_block).astype(BF16), part, 1, 0) for part in parts)
    before = sum(dot((block < token_block).astype(BF16), part, 1, 0) for part in parts)
    running = jnp.sum(before + jnp.where(iota((ROW, D), 1) <= token_place, own, 0.0), axis=1, keepdims=True)
    last = running[ROW - 1 : ROW]
    state = dot_right(v, k * jnp.exp(last - running), 0, 0)
    total = jnp.broadcast_to(last, (8, D))
    for s in range(SAMPLE):
        out[s, 0:64, :] = state
        out[s, 64:72, :] = total
    key_out[...] = k.astype(BF16)
    value_out[...] = v
    column_out[...] = jnp.broadcast_to(running, (ROW, D))
    line_out[...] = jnp.broadcast_to(column_to_row(running), (8, ROW))


def same_block():
    return iota((ROW, ROW), 0) // PT == iota((ROW, ROW), 1) // PT


def prompt_weights(q, k, mask):
    scores = dot(q, k, 1, 1) * mask
    high = scores.astype(BF16)
    low = jnp.where(same_block(), 0.0, scores - high.astype(F32)).astype(BF16)
    return high, low


def fold_kernel(rows_received, received, first, key, value, column, line, out, start_out, total_out, query_out):
    place = lax.axis_index("sample")
    end = jnp.zeros((HALF, D), F32)
    start = end
    for s in range(SAMPLE):
        start = jnp.where(place == s, end, start)
        total = rows_received[s, 64:65, :]
        total_out[s : s + 1, :] = total
        end = jnp.exp(total) * end + rows_received[s, 0:64, :]
    start_out[...] = start
    state = end
    for b in range(CTX):
        out[b, 0:64, :] = state
        state = jnp.exp(first[b, 25:26, :]) * state + received[b, 0:64, :]
    q = received[:, 64:80, :].reshape(ROW, D).astype(BF16)
    query_out[...] = q
    running = column[:, 0:1]
    weights = prompt_weights(q, key[...], masking(running, line[0:1, :]))
    v = value[...]
    outputs = sum(dot(part, v, 1, 0) for part in weights)
    outputs = outputs + jnp.exp(running) * dot_right(q, start, 1, 1)
    out[:, 64:72, :] = packed_half(outputs)


def output_kernel(received, query, local, grad, decay, gain, prompt_grad, out, output_out, prompt_out, rows):
    columns = jnp.exp(running_columns(decay[0]))
    scale = gain[...].astype(F32)
    rows[...] = prompt_grad[...].astype(F32).reshape(PT * HEADS, D)
    squares = jnp.zeros((T, D), F32)
    crossed = jnp.zeros((T, D), F32)
    prompt_squares = jnp.zeros((PT, D), F32)
    prompt_crossed = jnp.zeros((PT, D), F32)
    for h in range(HEADS):
        state = jnp.concatenate([received[2 * h, 0:64, :], received[2 * h + 1, 0:64, :]], axis=0)
        outputs = local[h] + columns[:, h : h + 1] * dot_right(query[h], state, 1, 1)
        output_out[h] = outputs
        upstream = grad[h].astype(F32) * scale[h : h + 1]
        squares = squares + outputs * outputs
        crossed = crossed + upstream * outputs
        outputs = unpack(received[2 * h, 64:72, :], received[2 * h + 1, 64:72, :])
        prompt_out[h] = outputs
        upstream = rows[pl.ds(h, PT, HEADS), :] * scale[h : h + 1]
        prompt_squares = prompt_squares + outputs * outputs
        prompt_crossed = prompt_crossed + upstream * outputs
    sums = [
        column_to_row(jnp.sum(part, axis=1, keepdims=True))
        for part in (squares, crossed, prompt_squares, prompt_crossed)
    ]
    at = iota((8, D), 0)
    tile = jnp.zeros((8, D), F32)
    for i, part in enumerate(sums):
        tile = jnp.where(at == i, part, tile)
    for x in range(HEAD_AXIS):
        out[x] = tile


def norm_terms(squares, crossed):
    inverse = lax.rsqrt(squares / FEATURES + EPSILON)
    return inverse, crossed * inverse * inverse / FEATURES


def grad_kernel(
    sums, outputs, prompt_outputs, query, grad, decay, gain, prompt_grad, out, grad_out, rows
):
    columns = jnp.exp(running_columns(decay[0]))
    scale = gain[...].astype(F32)
    rows[...] = prompt_grad[...].astype(F32).reshape(PT * HEADS, D)
    total = sums[0] + sums[1] + sums[2] + sums[3]
    inverse, project = norm_terms(row_to_column(total[0:1], T), row_to_column(total[1:2], T))
    prompt_inverse, prompt_project = norm_terms(row_to_column(total[2:3], PT), row_to_column(total[3:4], PT))
    for h in range(HEADS):
        upstream = grad[h].astype(F32) * scale[h : h + 1]
        out_grad = ((upstream - outputs[h] * project) * inverse).astype(BF16)
        grad_out[h] = out_grad
        back = dot_right(out_grad, query[h].astype(F32) * columns[:, h : h + 1], 0, 0)
        upstream = rows[pl.ds(h, PT, HEADS), :] * scale[h : h + 1]
        prompt_out_grad = ((upstream - prompt_outputs[h] * prompt_project) * prompt_inverse).astype(BF16).astype(F32)
        for half in range(2):
            out[2 * h + half, 0:64, :] = back[half * HALF : (half + 1) * HALF]
            out[2 * h + half, 64:72, :] = pack(prompt_out_grad, half)


def reply_back_kernel(
    received, out_grad, query, key, value, weights, decay, query_grad, key_local, value_local, rows
):
    lines = running_rows(decay[0])
    columns = running_columns(decay[0])
    scales = jnp.exp(columns)
    for h in range(HEADS):
        state = jnp.concatenate([received[2 * h, 0:64, :], received[2 * h + 1, 0:64, :]], axis=0)
        og = out_grad[h]
        mask = masking(columns[:, h : h + 1], lines[h : h + 1])
        mix = (dot(og, value[h], 1, 1) * mask).astype(BF16)
        rows[pl.ds(h, T, HEADS), :] = dot(mix, key[h], 1, 0) + scales[:, h : h + 1] * dot_right(og, state, 1, 0)
        key_local[h] = dot(mix, query[h], 0, 0)
        value_local[h] = dot(weights[h], og, 0, 0)
    query_grad[0] = rows[...].reshape(T, HEADS, D).astype(BF16)


def prompt_mix(og, v, mask):
    return split(dot(og, v, 1, 1) * mask)


def back_fold_kernel(
    received, first, start, totals, query, key, value, column, line, out, rows_out, grad_out
):
    adjoint = jnp.zeros((HALF, D), F32)
    for b in range(CTX - 1, -1, -1):
        out[b, 0:64, :] = adjoint
        adjoint = jnp.exp(first[b, 25:26, :]) * adjoint + received[b, 0:64, :]
    og = rows_of_half(received[:, 64:72, :]).astype(BF16)
    grad_out[...] = og
    running = column[:, 0:1]
    scale = jnp.exp(running)
    q = query[...]
    back = dot_right(og, q.astype(F32) * scale, 0, 0)
    place = lax.axis_index("sample")
    for s in range(SAMPLE):
        after = jnp.zeros((1, D), F32)
        between = after
        for other in range(s + 1, SAMPLE):
            after = after + totals[other : other + 1, :]
            between = between + jnp.where(other < place, totals[other : other + 1, :], 0.0)
        rows_out[s] = jnp.exp(after) * adjoint + jnp.where(place > s, jnp.exp(between), 0.0) * back
    mix = prompt_mix(og, value[...], masking(running, line[0:1, :]))
    k = key[...]
    query_grad = sum(dot(part, k, 1, 0) for part in mix) + scale * dot_right(og, start[...], 1, 0)
    out[:, 64:80, :] = query_grad.reshape(CTX, PT, D)


def prompt_back_kernel(rows_received, out_grad, query, key, value, column, line, out):
    adjoint = rows_received[0]
    for s in range(1, SAMPLE):
        adjoint = adjoint + rows_received[s]
    running = column[:, 0:1]
    to_end = jnp.exp(running[ROW - 1 : ROW] - running)
    mask = masking(running, line[0:1, :])
    q, k, v, og = query[...], key[...], value[...], out_grad[...]
    mix = prompt_mix(og, v, mask)
    key_grad = sum(dot(part, q, 0, 0) for part in mix) + to_end * dot_right(v, adjoint, 1, 0)
    weights = prompt_weights(q, k, mask)
    value_grad = sum(dot(part, og, 0, 0) for part in weights) + to_end * dot_right(k, adjoint, 1, 1)
    out[:, 0:16, :] = key_grad.reshape(CTX, PT, D)
    out[:, 16:24, :] = packed_half(value_grad)


def reply_end_kernel(received, key, value, key_local, value_local, decay, key_grad, value_grad, rows_k, rows_v):
    columns = running_columns(decay[0])
    to_end = jnp.exp(columns[T - 1 : T, :] - columns)
    for h in range(HEADS):
        adjoint = jnp.concatenate([received[2 * h, 0:64, :], received[2 * h + 1, 0:64, :]], axis=0)
        scale = to_end[:, h : h + 1]
        rows_k[pl.ds(h, T, HEADS), :] = key_local[h] + scale * dot_right(value[h], adjoint, 1, 0)
        rows_v[pl.ds(h, T, HEADS), :] = value_local[h] + scale * dot_right(key[h], adjoint, 1, 1)
    key_grad[0] = rows_k[...].reshape(T, HEADS, D).astype(BF16)
    value_grad[0] = rows_v[...].reshape(T, HEADS, D).astype(BF16)


def prompt_end_kernel(received, last, query_grad, key_grad, value_grad, rows_q, rows_k, rows_v):
    for h in range(HEADS):
        rows_q[pl.ds(h, PT, HEADS), :] = received[2 * h, 64:80, :] + received[2 * h + 1, 64:80, :]
        rows_k[pl.ds(h, PT, HEADS), :] = last[2 * h, 0:16, :] + last[2 * h + 1, 0:16, :]
        rows_v[pl.ds(h, PT, HEADS), :] = unpack(last[2 * h, 16:24, :], last[2 * h + 1, 16:24, :])
    query_grad[...] = rows_q[...].reshape(PT, HEADS, D).astype(BF16)
    key_grad[...] = rows_k[...].reshape(PT, HEADS, D).astype(BF16)
    value_grad[...] = rows_v[...].reshape(PT, HEADS, D).astype(BF16)


VMEM = pl.BlockSpec(memory_space=pltpu.VMEM)
SMEM = pl.BlockSpec(memory_space=pltpu.SMEM)
REPLY_ROWS = pltpu.VMEM((T * HEADS, D), F32)
PROMPT_ROWS = pltpu.VMEM((PT * HEADS, D), F32)
BY_HEAD = ((HEADS, T, D), BF16)
BY_HEAD_WIDE = ((HEADS, T, D), F32)
REPLY = ((1, T, HEADS, D), BF16)
PROMPT = ((PT, HEADS, D), BF16)


def run(kernel, outs, scratch, *operands, flops=0):
    specs = [SMEM if operand.dtype == jnp.int32 else VMEM for operand in operands]
    moved = sum(operand.size * operand.dtype.itemsize for operand in operands)
    return pl.pallas_call(
        kernel,
        out_shape=[jax.ShapeDtypeStruct(shape, kind) for shape, kind in outs],
        in_specs=specs,
        out_specs=[VMEM] * len(outs),
        scratch_shapes=scratch,
        compiler_params=pltpu.CompilerParams(vmem_limit_bytes=24 * 1024 * 1024),
        cost_estimate=pl.CostEstimate(flops=flops, bytes_accessed=2 * moved, transcendentals=0),
        name=kernel.__name__,
    )(*operands)


def exchange(x, axis):
    return lax.all_to_all(x, axis, 0, 0, tiled=True)


def shards(
    prompt_query,
    prompt_key,
    prompt_value,
    prompt_grad,
    prompt_decay,
    reply_query,
    reply_key,
    reply_value,
    reply_grad,
    reply_decay,
    reply_lengths,
    norm_gain,
):
    work = 8 * 2 * T * D * D
    (sent,) = run(
        prompt_send_kernel,
        [((CTX, 32, D), F32)],
        [PROMPT_ROWS, PROMPT_ROWS],
        prompt_key,
        prompt_value,
        prompt_decay,
        reply_decay,
    )
    first = exchange(sent, "ctx")
    sent, key, value = run(
        reply_send_kernel,
        [((CTX, 80, D), F32), BY_HEAD, BY_HEAD],
        [REPLY_ROWS, REPLY_ROWS, PROMPT_ROWS],
        reply_lengths,
        reply_key,
        reply_value,
        reply_decay,
        prompt_query,
        flops=2 * work,
    )
    blocks = exchange(sent, "ctx")
    sent, row_key, row_value, column, line = run(
        prompt_row_kernel,
        [
            ((SAMPLE, 72, D), F32),
            ((ROW, D), BF16),
            ((ROW, HALF), BF16),
            ((ROW, D), F32),
            ((8, ROW), F32),
        ],
        [],
        first,
    )
    rows = exchange(sent, "sample")
    query, grad, weights, local = run(
        reply_local_kernel,
        [BY_HEAD, BY_HEAD, BY_HEAD, BY_HEAD_WIDE],
        [REPLY_ROWS],
        reply_lengths,
        reply_query,
        reply_grad,
        key,
        value,
        reply_decay,
        flops=2 * work,
    )
    sent, start, totals, row_query = run(
        fold_kernel,
        [((CTX, 72, D), F32), ((HALF, D), F32), ((SAMPLE, D), F32), ((ROW, D), BF16)],
        [],
        rows,
        blocks,
        first,
        row_key,
        row_value,
        column,
        line,
    )
    states = exchange(sent, "ctx")
    sent, outputs, prompt_outputs = run(
        output_kernel,
        [((HEAD_AXIS, 8, D), F32), BY_HEAD_WIDE, ((HEADS, PT, D), F32)],
        [PROMPT_ROWS],
        states,
        query,
        local,
        grad,
        reply_decay,
        norm_gain,
        prompt_grad,
        flops=2 * work,
    )
    sums = exchange(sent, "head")
    sent, out_grad = run(
        grad_kernel,
        [((CTX, 72, D), F32), BY_HEAD],
        [PROMPT_ROWS],
        sums,
        outputs,
        prompt_outputs,
        query,
        grad,
        reply_decay,
        norm_gain,
        prompt_grad,
        flops=2 * work,
    )
    backs = exchange(sent, "ctx")
    reply_query_grad, key_local, value_local = run(
        reply_back_kernel,
        [REPLY, BY_HEAD_WIDE, BY_HEAD_WIDE],
        [REPLY_ROWS],
        states,
        out_grad,
        query,
        key,
        value,
        weights,
        reply_decay,
        flops=6 * work,
    )
    sent, sent_rows, row_grad = run(
        back_fold_kernel,
        [((CTX, 80, D), F32), ((SAMPLE, HALF, D), F32), ((ROW, HALF), BF16)],
        [],
        backs,
        first,
        start,
        totals,
        row_query,
        row_key,
        row_value,
        column,
        line,
    )
    rows = exchange(sent_rows, "sample")
    adjoints = exchange(sent, "ctx")
    (sent,) = run(
        prompt_back_kernel,
        [((CTX, 24, D), F32)],
        [],
        rows,
        row_grad,
        row_query,
        row_key,
        row_value,
        column,
        line,
    )
    last = exchange(sent, "ctx")
    reply_key_grad, reply_value_grad = run(
        reply_end_kernel,
        [REPLY, REPLY],
        [REPLY_ROWS, REPLY_ROWS],
        adjoints,
        key,
        value,
        key_local,
        value_local,
        reply_decay,
        flops=4 * work,
    )
    prompt_query_grad, prompt_key_grad, prompt_value_grad = run(
        prompt_end_kernel, [PROMPT, PROMPT, PROMPT], [PROMPT_ROWS] * 3, adjoints, last
    )
    return (
        prompt_query_grad,
        prompt_key_grad,
        prompt_value_grad,
        reply_query_grad,
        reply_key_grad,
        reply_value_grad,
    )


def solution(mesh):
    prompt = P(("sample", "ctx"), "head", None)
    reply = P("sample", "ctx", "head", None)
    in_specs = (
        (prompt,) * 4
        + (P("head", ("sample", "ctx")),)
        + (reply,) * 4
        + (P("sample", "head", "ctx"), P("sample"), P("head", None))
    )
    out_specs = (prompt,) * 3 + (reply,) * 3
    return jax.shard_map(shards, mesh=mesh, in_specs=in_specs, out_specs=out_specs, check_vma=False)
```

time: 954 us -> 184 us (0.19)
  waiting for transfers between devices: 611 us -> 43.6 us
  other arithmetic: 137 us -> 0 us
  blocking collectives: 133 us -> 104 us
  matrix products: 24.1 us -> 0 us
  local copies, waits for them, and re-layouts: 25.7 us -> 5.25 us
  starting transfers between devices: 0.36 us -> 16.4 us
  between operations: 15.9 us -> 1.43 us
  Pallas kernels: 0 us -> 13.1 us
    psum x3 -> x0, waiting for transfers between devices: 400 us -> none  [the longest x2 227 us: from_root(): return lax.psum(block, axis)]
    all_gather x6 -> x0, waiting for transfers between devices: 210 us -> none  [the longest x4 183 us: prefix(): everything = jax.tree.map(lambda part: lax.all_gather(part, axis), x)]
    all_to_all x0 -> x6, blocking collectives: none -> 104 us  [exchange(): return lax.all_to_all(x, axis, 0, 0, tiled=True)]
    select_n x112 -> x0, other arithmetic: 96 us -> none  [turn(): return jax.tree.map(lambda a, b: jnp.where(reached, a, b), new, before)]
    psum x3 -> x0, blocking collectives: 57.6 us -> none  [the longest x2 49.2 us: from_root(): return lax.psum(block, axis)]
    all_gather x3 -> x0, blocking collectives: 44.6 us -> none  [the longest x1 14.9 us: prefix(): everything = jax.tree.map(lambda part: lax.all_gather(part, axis), x)]
    all_to_all x0 -> x3, waiting for transfers between devices: none -> 43.6 us  [exchange(): return lax.all_to_all(x, axis, 0, 0, tiled=True)]
    unnamed x1 -> x0, blocking collectives: 30.8 us -> none
  transfers between devices with their start and end apart: 9 -> 3, of which waited for: 9 -> 3; matrix products, arithmetic and copies ran while one was open for 5% -> 0% of each run, Pallas kernels for 0% -> 3%
where the time goes in v1:
time: 184 us; the launch traced here: 183 us
  blocking collectives  104 us (57%)
  waiting for transfers between devices  43.6 us (24%)
  starting transfers between devices  16.4 us (9%)
  Pallas kernels  13.1 us (7%)
  local copies, waits for them, and re-layouts  5.25 us (3%)
    all_to_all x6, blocking collectives, exchange(): return lax.all_to_all(x, axis, 0, 0, tiled=True)  104 us
    all_to_all x3, waiting for transfers between devices, exchange(): return lax.all_to_all(x, axis, 0, 0, tiled=True)  43.6 us
    all_to_all x3, starting transfers between devices, exchange(): return lax.all_to_all(x, axis, 0, 0, tiled=True)  16.4 us
    pallas_call x12, Pallas kernels, run(): pl.pallas_call(kernel, out_shape=[jax.ShapeDtypeStruct(shape, kind) for s...  13.1 us
    unnamed x32, local copies, waits for them, and re-layouts  5.25 us
  transfers between devices with their start and end apart: 3, of which 3 were waited for; matrix products, arithmetic and copies ran while one was open for 0% of the time, Pallas kernels for 3%

profile of v1, /device:TPU:1, one launch (start us, length us, event | category | flops | bytes accessed | tf_op | source)
XLA Modules:
  0.0 183.3 jit_solution(14768988661693839292)
XLA Ops:
  0.6 0.0 copy-start.8
  0.6 0.7 copy-done.8
  1.3 0.0 copy-start.12
  1.3 0.8 copy-done.12
  2.1 0.0 copy-start.13
  2.1 0.8 copy-done.13
  2.8 0.0 copy-start.15
  2.8 0.7 copy-done.15
  3.5 0.1 prompt_send_kernel.1
  3.6 21.2 %all_to_all.45.received.first = f32[16,32,128]{2,1,0:T(8,128)S(1)} all-to-all(f32[16,32,128]{2,1,0:T(8,128)S(1)} %prompt_send_kernel.1), channel_id=1, replica_groups=mesh['sample'=8,'ctx'=16,'head'=4] {'ctx'}, dimensions={0} | all-to-all | bytes 524288 | tf_op jit(solution)/shard_map/all_to_all | solution.py:389
  24.8 1.2 prompt_row_kernel.1
  26.0 0.0 copy-start
  26.0 9.2 %all-to-all-start.1 = ((f32[8,72,128]{2,1,0:T(8,128)}), f32[8,72,128]{2,1,0:T(8,128)S(1)}, u32[]{:S(2)}, u32[]{:S(2)}) async-start(f32[8,72,128]{2,1,0:T(8,128)} %get-tuple-element.38), calls=%async_computation.1 | async-start | bytes 589824 | tf_op jit(solution)/shard_map/all_to_all | solution.py:389
  35.8 0.0 copy-done
  35.8 0.0 copy-done.1
  35.8 0.0 copy-done.9
  35.9 0.0 copy-done.11
  35.9 0.7 reply_send_kernel.1
  36.5 11.7 %all-to-all-done.1.rows_received = f32[8,72,128]{2,1,0:T(8,128)S(1)} async-done(((f32[8,72,128]{2,1,0:T(8,128)}), f32[8,72,128]{2,1,0:T(8,128)S(1)}, u32[]{:S(2)}, u32[]{:S(2)}) %all-to-all-start.1) | async-done | bytes 294944 | tf_op jit(solution)/shard_map/all_to_all | solution.py:389
  48.3 23.2 %all_to_all.46.received = f32[16,80,128]{2,1,0:T(8,128)S(1)} all-to-all(f32[16,80,128]{2,1,0:T(8,128)S(1)} %get-tuple-element.39), channel_id=1, replica_groups=mesh['sample'=8,'ctx'=16,'head'=4] {'ctx'}, dimensions={0} | all-to-all | bytes 1310720 | tf_op jit(solution)/shard_map/all_to_all | solution.py:389
  71.5 1.3 fold_kernel.1
  72.8 3.6 %all-to-all-start.3 = ((f32[16,72,128]{2,1,0:T(8,128)}), f32[16,72,128]{2,1,0:T(8,128)S(1)}, u32[]{:S(2)}, u32[]{:S(2)}) async-start(f32[16,72,128]{2,1,0:T(8,128)} %get-tuple-element.44), calls=%async_computation.3 | async-start | bytes 1179648 | tf_op jit(solution)/shard_map/all_to_all | solution.py:389
  76.4 0.0 copy-done.2
  76.4 0.0 copy-done.3
  76.5 0.0 copy-start.10
  76.5 1.5 reply_local_kernel.1
  78.0 0.7 copy-done.4
  78.7 15.9 %all-to-all-done.3.received = f32[16,72,128]{2,1,0:T(8,128)S(1)} async-done(((f32[16,72,128]{2,1,0:T(8,128)}), f32[16,72,128]{2,1,0:T(8,128)S(1)}, u32[]{:S(2)}, u32[]{:S(2)}) %all-to-all-start.3) | async-done | bytes 589856 | tf_op jit(solution)/shard_map/all_to_all | solution.py:389
  94.6 0.0 copy-done.10
  94.6 0.7 copy-done.14
  95.3 0.6 output_kernel.1
  95.8 8.0 %all_to_all.47.sums = f32[4,8,128]{2,1,0:T(8,128)S(1)} all-to-all(f32[4,8,128]{2,1,0:T(8,128)S(1)} %get-tuple-element.50), channel_id=1, replica_groups=mesh['sample'=8,'ctx'=16,'head'=4] {'head'}, dimensions={0} | all-to-all | bytes 32768 | tf_op jit(solution)/shard_map/all_to_all | solution.py:389
  103.8 0.6 grad_kernel.1
  104.5 0.0 copy-start.6
  104.5 23.2 %all_to_all.48.received = f32[16,72,128]{2,1,0:T(8,128)S(1)} all-to-all(f32[16,72,128]{2,1,0:T(8,128)S(1)} %get-tuple-element.53), channel_id=1, replica_groups=mesh['sample'=8,'ctx'=16,'head'=4] {'ctx'}, dimensions={0} | all-to-all | bytes 1179648 | tf_op jit(solution)/shard_map/all_to_all | solution.py:389
  127.7 0.0 copy-done.6
  127.7 1.4 back_fold_kernel.1
  129.1 14.8 %all_to_all.49.rows_received = f32[8,64,128]{2,1,0:T(8,128)S(1)} all-to-all(f32[8,64,128]{2,1,0:T(8,128)S(1)} %get-tuple-element.58), channel_id=1, replica_groups=mesh['sample'=8,'ctx'=16,'head'=4] {'sample'}, dimensions={0} | all-to-all | bytes 524288 | tf_op jit(solution)/shard_map/all_to_all | solution.py:389
  143.9 1.0 prompt_back_kernel.1
  144.8 13.3 %all_to_all.50.last = f32[16,24,128]{2,1,0:T(8,128)S(1)} all-to-all(f32[16,24,128]{2,1,0:T(8,128)S(1)} %prompt_back_kernel.1), channel_id=1, replica_groups=mesh['sample'=8,'ctx'=16,'head'=4] {'ctx'}, dimensions={0} | all-to-all | bytes 393216 | tf_op jit(solution)/shard_map/all_to_all | solution.py:389
  158.1 3.6 %all-to-all-start.6 = ((f32[16,80,128]{2,1,0:T(8,128)}), f32[16,80,128]{2,1,0:T(8,128)S(1)}, u32[]{:S(2)}, u32[]{:S(2)}) async-start(f32[16,80,128]{2,1,0:T(8,128)} %get-tuple-element.57), calls=%async_computation.6 | async-start | bytes 1310720 | tf_op jit(solution)/shard_map/all_to_all | solution.py:389
  161.7 0.0 copy-done.5
  161.7 0.0 copy-start.7
  161.7 0.9 copy-done.7
  162.7 2.6 %reply_back_kernel.1 = (bf16[1,128,8,128]{3,2,1,0:T(8,128)(2,1)}, f32[8,128,128]{2,1,0:T(8,128)S(1)}, f32[8,128,128]{2,1,0:T(8,128)S(1)}) custom-call(f32[16,72,128]{2,1,0:T(8,128)S(1)} %all-to-all-done.3.received, bf16[8,128,128]{2,1,0:T(8,128)(2,1)S(1)} %copy-done.7, bf16[8,128,128]{2,1,0:T(8,128)(2,1)S(1)} %get-tuple-element.47.query, ...), custom_call_target="tpu_custom_call" | custom-call | flops 201326592 | bytes 3809280 | tf_op jit(solution)/shard_map/reply_back_kernel/pallas_call | solution.py:376
  165.3 15.9 %all-to-all-done.6.received = f32[16,80,128]{2,1,0:T(8,128)S(1)} async-done(((f32[16,80,128]{2,1,0:T(8,128)}), f32[16,80,128]{2,1,0:T(8,128)S(1)}, u32[]{:S(2)}, u32[]{:S(2)}) %all-to-all-start.6) | async-done | bytes 655392 | tf_op jit(solution)/shard_map/all_to_all | solution.py:389
  181.2 0.7 prompt_end_kernel.1
  181.9 1.4 reply_end_kernel.1
  (8 shorter events, 0.0 us)
Async XLA Ops:
  0.6 0.7 copy-start.8
  1.3 0.8 copy-start.12
  2.1 0.8 copy-start.13
  2.8 0.7 copy-start.15
  26.0 9.8 %copy-start = (bf16[1,128,8,128]{3,2,1,0:T(8,128)(2,1)S(1)}, bf16[1,128,8,128]{3,2,1,0:T(8,128)(2,1)}, u32[]{:S(2)}) copy-start(bf16[1,128,8,128]{3,2,1,0:T(8,128)(2,1)} %key.3) | copy-start | bytes 786436
  26.0 9.8 %copy-start.1 = (bf16[1,128,8,128]{3,2,1,0:T(8,128)(2,1)S(1)}, bf16[1,128,8,128]{3,2,1,0:T(8,128)(2,1)}, u32[]{:S(2)}) copy-start(bf16[1,128,8,128]{3,2,1,0:T(8,128)(2,1)} %value.3) | copy-start | bytes 786436
  26.0 9.8 %copy-start.9 = (f32[1,8,128]{2,1,0:T(8,128)S(1)}, f32[1,8,128]{2,1,0:T(8,128)}, u32[]{:S(2)}) copy-start(f32[1,8,128]{2,1,0:T(8,128)} %decay.13) | copy-start | bytes 12292
  26.0 9.8 %copy-start.11 = (bf16[16,8,128]{2,1,0:T(8,128)(2,1)S(1)}, bf16[16,8,128]{2,1,0:T(8,128)(2,1)}, u32[]{:S(2)}) copy-start(bf16[16,8,128]{2,1,0:T(8,128)(2,1)} %prompt_query.1) | copy-start | bytes 98308
  26.0 22.3 %all-to-all-start.1 = ((f32[8,72,128]{2,1,0:T(8,128)}), f32[8,72,128]{2,1,0:T(8,128)S(1)}, u32[]{:S(2)}, u32[]{:S(2)}) async-start(f32[8,72,128]{2,1,0:T(8,128)} %get-tuple-element.38), calls=%async_computation.1 | async-start | bytes 589824 | tf_op jit(solution)/shard_map/all_to_all | solution.py:389
  72.8 3.6 %copy-start.2 = (bf16[1,128,8,128]{3,2,1,0:T(8,128)(2,1)S(1)}, bf16[1,128,8,128]{3,2,1,0:T(8,128)(2,1)}, u32[]{:S(2)}) copy-start(bf16[1,128,8,128]{3,2,1,0:T(8,128)(2,1)} %query.1) | copy-start | bytes 786436
  72.8 3.6 %copy-start.3 = (bf16[1,128,8,128]{3,2,1,0:T(8,128)(2,1)S(1)}, bf16[1,128,8,128]{3,2,1,0:T(8,128)(2,1)}, u32[]{:S(2)}) copy-start(bf16[1,128,8,128]{3,2,1,0:T(8,128)(2,1)} %grad.1) | copy-start | bytes 786436
  72.8 21.8 %all-to-all-start.3 = ((f32[16,72,128]{2,1,0:T(8,128)}), f32[16,72,128]{2,1,0:T(8,128)S(1)}, u32[]{:S(2)}, u32[]{:S(2)}) async-start(f32[16,72,128]{2,1,0:T(8,128)} %get-tuple-element.44), calls=%async_computation.3 | async-start | bytes 1179648 | tf_op jit(solution)/shard_map/all_to_all | solution.py:389
  76.5 18.1 %copy-start.10 = (bf16[16,8,128]{2,1,0:T(8,128)(2,1)S(1)}, bf16[16,8,128]{2,1,0:T(8,128)(2,1)}, u32[]{:S(2)}) copy-start(bf16[16,8,128]{2,1,0:T(8,128)(2,1)} %prompt_grad.3) | copy-start | bytes 98308
  78.0 0.7 copy-start.4
  94.6 0.7 copy-start.14
  104.5 23.2 %copy-start.6 = (bf16[8,128,128]{2,1,0:T(8,128)(2,1)}, bf16[8,128,128]{2,1,0:T(8,128)(2,1)S(1)}, u32[]{:S(2)}) copy-start(bf16[8,128,128]{2,1,0:T(8,128)(2,1)S(1)} %get-tuple-element.63.out_grad) | copy-start | bytes 786436
  158.1 3.6 %copy-start.5 = (bf16[8,128,128]{2,1,0:T(8,128)(2,1)S(1)}, bf16[8,128,128]{2,1,0:T(8,128)(2,1)}, u32[]{:S(2)}) copy-start(bf16[8,128,128]{2,1,0:T(8,128)(2,1)} %copy-done.4) | copy-start | bytes 786436
  158.1 23.1 %all-to-all-start.6 = ((f32[16,80,128]{2,1,0:T(8,128)}), f32[16,80,128]{2,1,0:T(8,128)S(1)}, u32[]{:S(2)}, u32[]{:S(2)}) async-start(f32[16,80,128]{2,1,0:T(8,128)} %get-tuple-element.57), calls=%async_computation.6 | async-start | bytes 1310720 | tf_op jit(solution)/shard_map/all_to_all | solution.py:389
  161.7 1.0 copy-start.7

commit v2 on v1

--- a/solution.py
+++ b/solution.py
@@ -107,39 +107,37 @@
     return lax.axis_index("ctx") * T + iota((T, 1), 0) < lengths[0]
 
 
-def prompt_send_kernel(key, value, decay, reply_decay, out, rows_k, rows_v):
-    rows_k[...] = key[...].astype(F32).reshape(PT * HEADS, D)
-    rows_v[...] = value[...].astype(F32).reshape(PT * HEADS, D)
-    wide = jnp.concatenate([decay[...], jnp.zeros((HEADS, D - PT), F32)], axis=1)
-    totals = jnp.sum(reply_decay[0], axis=1, keepdims=True)
-    at = iota((8, D), 0)
-    for h in range(HEADS):
-        k = rows_k[pl.ds(h, PT, HEADS), :]
-        v = rows_v[pl.ds(h, PT, HEADS), :]
-        tail = jnp.where(at == 0, wide[h : h + 1], jnp.where(at == 1, totals[h : h + 1], 0.0))
-        for half in range(2):
-            out[2 * h + half, 0:16, :] = k
-            out[2 * h + half, 16:24, :] = pack(v, half)
-            out[2 * h + half, 24:32, :] = tail
-
-
-def reply_send_kernel(lengths, key, value, decay, prompt_query, out, key_out, value_out, rows_k, rows_v, rows_q):
+def send_kernel(
+    lengths, key, value, decay, prompt_query, prompt_key, prompt_value, prompt_decay, out, key_out, value_out,
+    rows_k, rows_v, prompt_q, prompt_k, prompt_v,
+):
     rows_k[...] = key[0].astype(F32).reshape(T * HEADS, D)
     rows_v[...] = value[0].astype(F32).reshape(T * HEADS, D)
-    rows_q[...] = prompt_query[...].astype(F32).reshape(PT * HEADS, D)
+    prompt_q[...] = prompt_query[...].astype(F32).reshape(PT * HEADS, D)
+    prompt_k[...] = prompt_key[...].astype(F32).reshape(PT * HEADS, D)
+    prompt_v[...] = prompt_value[...].astype(F32).reshape(PT * HEADS, D)
     live = live_tokens(lengths)
     columns = running_columns(decay[0])
     to_end = jnp.exp(columns[T - 1 : T, :] - columns)
+    wide = jnp.concatenate([prompt_decay[...], jnp.zeros((HEADS, D - PT), F32)], axis=1)
+    totals = jnp.sum(decay[0], axis=1, keepdims=True)
+    at = iota((8, D), 0)
     for h in range(HEADS):
         k = jnp.where(live, rows_k[pl.ds(h, T, HEADS), :], 0.0)
         v = jnp.where(live, rows_v[pl.ds(h, T, HEADS), :], 0.0).astype(BF16)
         key_out[h] = k.astype(BF16)
         value_out[h] = v
         state = dot_right(v, k * to_end[:, h : h + 1], 0, 0)
-        q = rows_q[pl.ds(h, PT, HEADS), :]
+        tail = jnp.where(at == 0, wide[h : h + 1], jnp.where(at == 1, totals[h : h + 1], 0.0))
+        q = prompt_q[pl.ds(h, PT, HEADS), :]
+        k = prompt_k[pl.ds(h, PT, HEADS), :]
+        v = prompt_v[pl.ds(h, PT, HEADS), :]
         for half in range(2):
             out[2 * h + half, 0:64, :] = state[half * HALF : (half + 1) * HALF]
-            out[2 * h + half, 64:80, :] = q
+            out[2 * h + half, 64:80, :] = k
+            out[2 * h + half, 80:88, :] = pack(v, half)
+            out[2 * h + half, 88:96, :] = tail
+            out[2 * h + half, 96:104, :] = q[8 * half : 8 * half + 8]
 
 
 def reply_local_kernel(lengths, query, grad, key, value, decay, query_out, grad_out, weights_out, local_out, rows):
@@ -159,10 +157,10 @@
         grad_out[h] = jnp.where(live, rows[pl.ds(h, T, HEADS), :], 0.0).astype(BF16)
 
 
-def prompt_row_kernel(received, out, key_out, value_out, column_out, line_out):
-    k = received[:, 0:16, :].reshape(ROW, D)
-    v = rows_of_half(received[:, 16:24, :]).astype(BF16)
-    decay = received[:, 24, :]
+def prompt_row_kernel(received, out, key_out, value_out, column_out, line_out, query_out):
+    k = received[:, 64:80, :].reshape(ROW, D)
+    v = rows_of_half(received[:, 80:88, :]).astype(BF16)
+    decay = received[:, 88, :]
     token_block, token_place = iota((ROW, CTX), 0) // PT, iota((ROW, D), 0) % PT
     block = iota((ROW, CTX), 1)
     parts = split3(decay)
@@ -179,6 +177,7 @@
     value_out[...] = v
     column_out[...] = jnp.broadcast_to(running, (ROW, D))
     line_out[...] = jnp.broadcast_to(column_to_row(running), (8, ROW))
+    query_out[...] = received[:, 96:104, :]
 
 
 def same_block():
@@ -192,7 +191,23 @@
     return high, low
 
 
-def fold_kernel(rows_received, received, first, key, value, column, line, out, start_out, total_out, query_out):
+def second_core():
+    return lax.axis_index("ctx") % 2 == 1
+
+
+def prompt_local_kernel(own, other, key, value, column, line, query_out, local_out, high_out, low_out):
+    second = second_core()
+    first_half = jnp.where(second, other[...], own[...])
+    second_half = jnp.where(second, own[...], other[...])
+    q = jnp.concatenate([first_half, second_half], axis=1).reshape(ROW, D).astype(BF16)
+    query_out[...] = q
+    weights = prompt_weights(q, key[...], masking(column[:, 0:1], line[0:1, :]))
+    v = value[...]
+    local_out[...] = sum(dot(part, v, 1, 0) for part in weights)
+    high_out[...], low_out[...] = weights
+
+
+def fold_kernel(rows_received, received, query, local, column, out, start_out, total_out):
     place = lax.axis_index("sample")
     end = jnp.zeros((HALF, D), F32)
     start = end
@@ -205,14 +220,8 @@
     state = end
     for b in range(CTX):
         out[b, 0:64, :] = state
-        state = jnp.exp(first[b, 25:26, :]) * state + received[b, 0:64, :]
-    q = received[:, 64:80, :].reshape(ROW, D).astype(BF16)
-    query_out[...] = q
-    running = column[:, 0:1]
-    weights = prompt_weights(q, key[...], masking(running, line[0:1, :]))
-    v = value[...]
-    outputs = sum(dot(part, v, 1, 0) for part in weights)
-    outputs = outputs + jnp.exp(running) * dot_right(q, start, 1, 1)
+        state = jnp.exp(received[b, 89:90, :]) * state + received[b, 0:64, :]
+    outputs = local[...] + jnp.exp(column[:, 0:1]) * dot_right(query[...], start, 1, 1)
     out[:, 64:72, :] = packed_half(outputs)
 
 
@@ -253,9 +262,7 @@
     return inverse, crossed * inverse * inverse / FEATURES
 
 
-def grad_kernel(
-    sums, outputs, prompt_outputs, query, grad, decay, gain, prompt_grad, out, grad_out, rows
-):
+def grad_kernel(sums, outputs, prompt_outputs, query, grad, decay, gain, prompt_grad, out, grad_out, rows):
     columns = jnp.exp(running_columns(decay[0]))
     scale = gain[...].astype(F32)
     rows[...] = prompt_grad[...].astype(F32).reshape(PT * HEADS, D)
@@ -291,23 +298,12 @@
     query_grad[0] = rows[...].reshape(T, HEADS, D).astype(BF16)
 
 
-def prompt_mix(og, v, mask):
-    return split(dot(og, v, 1, 1) * mask)
-
-
-def back_fold_kernel(
-    received, first, start, totals, query, key, value, column, line, out, rows_out, grad_out
-):
+def back_fold_kernel(received, first, totals, query, column, rows_out):
     adjoint = jnp.zeros((HALF, D), F32)
     for b in range(CTX - 1, -1, -1):
-        out[b, 0:64, :] = adjoint
-        adjoint = jnp.exp(first[b, 25:26, :]) * adjoint + received[b, 0:64, :]
+        adjoint = jnp.exp(first[b, 89:90, :]) * adjoint + received[b, 0:64, :]
     og = rows_of_half(received[:, 64:72, :]).astype(BF16)
-    grad_out[...] = og
-    running = column[:, 0:1]
-    scale = jnp.exp(running)
-    q = query[...]
-    back = dot_right(og, q.astype(F32) * scale, 0, 0)
+    back = dot_right(og, query[...].astype(F32) * jnp.exp(column[:, 0:1]), 0, 0)
     place = lax.axis_index("sample")
     for s in range(SAMPLE):
         after = jnp.zeros((1, D), F32)
@@ -316,48 +312,64 @@
             after = after + totals[other : other + 1, :]
             between = between + jnp.where(other < place, totals[other : other + 1, :], 0.0)
         rows_out[s] = jnp.exp(after) * adjoint + jnp.where(place > s, jnp.exp(between), 0.0) * back
-    mix = prompt_mix(og, value[...], masking(running, line[0:1, :]))
-    k = key[...]
-    query_grad = sum(dot(part, k, 1, 0) for part in mix) + scale * dot_right(og, start[...], 1, 0)
-    out[:, 64:80, :] = query_grad.reshape(CTX, PT, D)
-
-
-def prompt_back_kernel(rows_received, out_grad, query, key, value, column, line, out):
+
+
+def prompt_mid_kernel(
+    received, first, start, query, key, value, high, low, column, line,
+    out, keep_out, swap_out, key_local, value_local,
+):
+    adjoint = jnp.zeros((HALF, D), F32)
+    for b in range(CTX - 1, -1, -1):
+        out[b] = adjoint
+        adjoint = jnp.exp(first[b, 89:90, :]) * adjoint + received[b, 0:64, :]
+    og = rows_of_half(received[:, 64:72, :]).astype(BF16)
+    running = column[:, 0:1]
+    mix = split(dot(og, value[...], 1, 1) * masking(running, line[0:1, :]))
+    k, q = key[...], query[...]
+    query_grad = sum(dot(part, k, 1, 0) for part in mix) + jnp.exp(running) * dot_right(og, start[...], 1, 0)
+    query_grad = query_grad.reshape(CTX, PT, D)
+    second = second_core()
+    keep_out[...] = jnp.where(second, query_grad[:, 8:16], query_grad[:, 0:8])
+    swap_out[...] = jnp.where(second, query_grad[:, 0:8], query_grad[:, 8:16])
+    key_local[...] = sum(dot(part, q, 0, 0) for part in mix)
+    value_local[...] = dot(high[...], og, 0, 0) + dot(low[...], og, 0, 0)
+
+
+def prompt_back_kernel(rows_received, adjoints, keep, swapped, key_local, value_local, key, value, column, out):
     adjoint = rows_received[0]
     for s in range(1, SAMPLE):
         adjoint = adjoint + rows_received[s]
     running = column[:, 0:1]
     to_end = jnp.exp(running[ROW - 1 : ROW] - running)
-    mask = masking(running, line[0:1, :])
-    q, k, v, og = query[...], key[...], value[...], out_grad[...]
-    mix = prompt_mix(og, v, mask)
-    key_grad = sum(dot(part, q, 0, 0) for part in mix) + to_end * dot_right(v, adjoint, 1, 0)
-    weights = prompt_weights(q, k, mask)
-    value_grad = sum(dot(part, og, 0, 0) for part in weights) + to_end * dot_right(k, adjoint, 1, 1)
-    out[:, 0:16, :] = key_grad.reshape(CTX, PT, D)
-    out[:, 16:24, :] = packed_half(value_grad)
-
-
-def reply_end_kernel(received, key, value, key_local, value_local, decay, key_grad, value_grad, rows_k, rows_v):
+    key_grad = key_local[...] + to_end * dot_right(value[...], adjoint, 1, 0)
+    value_grad = value_local[...] + to_end * dot_right(key[...], adjoint, 1, 1)
+    out[:, 0:64, :] = adjoints[...]
+    out[:, 64:80, :] = key_grad.reshape(CTX, PT, D)
+    out[:, 80:88, :] = packed_half(value_grad)
+    out[:, 88:96, :] = keep[...] + swapped[...]
+
+
+def end_kernel(
+    received, key, value, key_local, value_local, decay,
+    key_grad, value_grad, prompt_query_grad, prompt_key_grad, prompt_value_grad,
+    rows_k, rows_v, prompt_q, prompt_k, prompt_v,
+):
     columns = running_columns(decay[0])
     to_end = jnp.exp(columns[T - 1 : T, :] - columns)
     for h in range(HEADS):
-        adjoint = jnp.concatenate([received[2 * h, 0:64, :], received[2 * h + 1, 0:64, :]], axis=0)
+        low, high = received[2 * h], received[2 * h + 1]
+        adjoint = jnp.concatenate([low[0:64], high[0:64]], axis=0)
         scale = to_end[:, h : h + 1]
         rows_k[pl.ds(h, T, HEADS), :] = key_local[h] + scale * dot_right(value[h], adjoint, 1, 0)
         rows_v[pl.ds(h, T, HEADS), :] = value_local[h] + scale * dot_right(key[h], adjoint, 1, 1)
+        prompt_k[pl.ds(h, PT, HEADS), :] = low[64:80] + high[64:80]
+        prompt_v[pl.ds(h, PT, HEADS), :] = unpack(low[80:88], high[80:88])
+        prompt_q[pl.ds(h, PT, HEADS), :] = jnp.concatenate([low[88:96], high[88:96]], axis=0)
     key_grad[0] = rows_k[...].reshape(T, HEADS, D).astype(BF16)
     value_grad[0] = rows_v[...].reshape(T, HEADS, D).astype(BF16)
-
-
-def prompt_end_kernel(received, last, query_grad, key_grad, value_grad, rows_q, rows_k, rows_v):
-    for h in range(HEADS):
-        rows_q[pl.ds(h, PT, HEADS), :] = received[2 * h, 64:80, :] + received[2 * h + 1, 64:80, :]
-        rows_k[pl.ds(h, PT, HEADS), :] = last[2 * h, 0:16, :] + last[2 * h + 1, 0:16, :]
-        rows_v[pl.ds(h, PT, HEADS), :] = unpack(last[2 * h, 16:24, :], last[2 * h + 1, 16:24, :])
-    query_grad[...] = rows_q[...].reshape(PT, HEADS, D).astype(BF16)
-    key_grad[...] = rows_k[...].reshape(PT, HEADS, D).astype(BF16)
-    value_grad[...] = rows_v[...].reshape(PT, HEADS, D).astype(BF16)
+    prompt_query_grad[...] = prompt_q[...].reshape(PT, HEADS, D).astype(BF16)
+    prompt_key_grad[...] = prompt_k[...].reshape(PT, HEADS, D).astype(BF16)
+    prompt_value_grad[...] = prompt_v[...].reshape(PT, HEADS, D).astype(BF16)
 
 
 VMEM = pl.BlockSpec(memory_space=pltpu.VMEM)
@@ -379,7 +391,7 @@
         in_specs=specs,
         out_specs=[VMEM] * len(outs),
         scratch_shapes=scratch,
-        compiler_params=pltpu.CompilerParams(vmem_limit_bytes=24 * 1024 * 1024),
+        compiler_params=pltpu.CompilerParams(vmem_limit_bytes=8 * 1024 * 1024),
         cost_estimate=pl.CostEstimate(flops=flops, bytes_accessed=2 * moved, transcendentals=0),
         name=kernel.__name__,
     )(*operands)
@@ -387,6 +399,10 @@
 
 def exchange(x, axis):
     return lax.all_to_all(x, axis, 0, 0, tiled=True)
+
+
+def swap_cores(x):
+    return lax.ppermute(x, "ctx", [(i, i ^ 1) for i in range(CTX)])
 
 
 def shards(
@@ -404,29 +420,22 @@
     norm_gain,
 ):
     work = 8 * 2 * T * D * D
-    (sent,) = run(
-        prompt_send_kernel,
-        [((CTX, 32, D), F32)],
-        [PROMPT_ROWS, PROMPT_ROWS],
-        prompt_key,
-        prompt_value,
-        prompt_decay,
-        reply_decay,
-    )
-    first = exchange(sent, "ctx")
     sent, key, value = run(
-        reply_send_kernel,
-        [((CTX, 80, D), F32), BY_HEAD, BY_HEAD],
-        [REPLY_ROWS, REPLY_ROWS, PROMPT_ROWS],
+        send_kernel,
+        [((CTX, 104, D), F32), BY_HEAD, BY_HEAD],
+        [REPLY_ROWS] * 2 + [PROMPT_ROWS] * 3,
         reply_lengths,
         reply_key,
         reply_value,
         reply_decay,
         prompt_query,
+        prompt_key,
+        prompt_value,
+        prompt_decay,
         flops=2 * work,
     )
-    blocks = exchange(sent, "ctx")
-    sent, row_key, row_value, column, line = run(
+    first = exchange(sent, "ctx")
+    sent, row_key, row_value, column, line, half_query = run(
         prompt_row_kernel,
         [
             ((SAMPLE, 72, D), F32),
@@ -434,6 +443,7 @@
             ((ROW, HALF), BF16),
             ((ROW, D), F32),
             ((8, ROW), F32),
+            ((CTX, 8, D), F32),
         ],
         [],
         first,
@@ -451,17 +461,27 @@
         reply_decay,
         flops=2 * work,
     )
-    sent, start, totals, row_query = run(
-        fold_kernel,
-        [((CTX, 72, D), F32), ((HALF, D), F32), ((SAMPLE, D), F32), ((ROW, D), BF16)],
+    row_query, row_local, row_high, row_low = run(
+        prompt_local_kernel,
+        [((ROW, D), BF16), ((ROW, HALF), F32), ((ROW, ROW), BF16), ((ROW, ROW), BF16)],
         [],
-        rows,
-        blocks,
-        first,
+        half_query,
+        swap_cores(half_query),
         row_key,
         row_value,
         column,
         line,
+        flops=work,
+    )
+    sent, start, totals = run(
+        fold_kernel,
+        [((CTX, 72, D), F32), ((HALF, D), F32), ((SAMPLE, D), F32)],
+        [],
+        rows,
+        first,
+        row_query,
+        row_local,
+        column,
     )
     states = exchange(sent, "ctx")
     sent, outputs, prompt_outputs = run(
@@ -506,49 +526,56 @@
         reply_decay,
         flops=6 * work,
     )
-    sent, sent_rows, row_grad = run(
-        back_fold_kernel,
-        [((CTX, 80, D), F32), ((SAMPLE, HALF, D), F32), ((ROW, HALF), BF16)],
+    (sent,) = run(back_fold_kernel, [((SAMPLE, HALF, D), F32)], [], backs, first, totals, row_query, column)
+    rows = exchange(sent, "sample")
+    adjoints, keep, swap, row_key_local, row_value_local = run(
+        prompt_mid_kernel,
+        [
+            ((CTX, HALF, D), F32),
+            ((CTX, 8, D), F32),
+            ((CTX, 8, D), F32),
+            ((ROW, D), F32),
+            ((ROW, HALF), F32),
+        ],
         [],
         backs,
         first,
         start,
-        totals,
         row_query,
         row_key,
         row_value,
+        row_high,
+        row_low,
         column,
         line,
-    )
-    rows = exchange(sent_rows, "sample")
-    adjoints = exchange(sent, "ctx")
+        flops=work,
+    )
     (sent,) = run(
         prompt_back_kernel,
-        [((CTX, 24, D), F32)],
+        [((CTX, 96, D), F32)],
         [],
         rows,
-        row_grad,
-        row_query,
+        adjoints,
+        keep,
+        swap_cores(swap),
+        row_key_local,
+        row_value_local,
         row_key,
         row_value,
         column,
-        line,
-    )
-    last = exchange(sent, "ctx")
-    reply_key_grad, reply_value_grad = run(
-        reply_end_kernel,
-        [REPLY, REPLY],
-        [REPLY_ROWS, REPLY_ROWS],
-        adjoints,
+    )
+    received = exchange(sent, "ctx")
+    reply_key_grad, reply_value_grad, prompt_query_grad, prompt_key_grad, prompt_value_grad = run(
+        end_kernel,
+        [REPLY, REPLY, PROMPT, PROMPT, PROMPT],
+        [REPLY_ROWS] * 2 + [PROMPT_ROWS] * 3,
+        received,
         key,
         value,
         key_local,
         value_local,
         reply_decay,
         flops=4 * work,
-    )
-    prompt_query_grad, prompt_key_grad, prompt_value_grad = run(
-        prompt_end_kernel, [PROMPT, PROMPT, PROMPT], [PROMPT_ROWS] * 3, adjoints, last
     )
     return (
         prompt_query_grad,

time: 184 us -> 173 us (0.940)
  blocking collectives: 104 us -> 65.1 us
  local copies, waits for them, and re-layouts: 5.25 us -> 18.7 us
  starting transfers between devices: 16.4 us -> 24.1 us
  waiting for transfers between devices: 43.6 us -> 48.9 us
    all_to_all x6 -> x3, blocking collectives: 104 us -> 65.1 us  [exchange(): return lax.all_to_all(x, axis, 0, 0, tiled=True)]
    unnamed x32 -> x56, local copies, waits for them, and re-layouts: 5.25 us -> 18.7 us
    ppermute x0 -> x2, starting transfers between devices: none -> 4 us  [swap_cores(): return lax.ppermute(x, 'ctx', [(i, i ^ 1) for i in range(CTX)])]
    all_to_all x3 -> x4, starting transfers between devices: 16.4 us -> 20.1 us  [exchange(): return lax.all_to_all(x, axis, 0, 0, tiled=True)]
    all_to_all x3 -> x4, waiting for transfers between devices: 43.6 us -> 46.6 us  [exchange(): return lax.all_to_all(x, axis, 0, 0, tiled=True)]
    ppermute x0 -> x2, waiting for transfers between devices: none -> 2.26 us  [swap_cores(): return lax.ppermute(x, 'ctx', [(i, i ^ 1) for i in range(CTX)])]
  transfers between devices with their start and end apart: 3 -> 6, of which waited for: 3 -> 6; matrix products, arithmetic and copies ran while one was open for 0% -> 0% of each run, Pallas kernels for 3% -> 3%
where the time goes in v2:
time: 173 us; the launch traced here: 171 us
  blocking collectives  65.1 us (38%)
  waiting for transfers between devices  48.9 us (28%)
  starting transfers between devices  24.1 us (14%)
  local copies, waits for them, and re-layouts  18.7 us (11%)
  Pallas kernels  13 us (8%)
    all_to_all x3, blocking collectives, exchange(): return lax.all_to_all(x, axis, 0, 0, tiled=True)  65.1 us
    all_to_all x4, waiting for transfers between devices, exchange(): return lax.all_to_all(x, axis, 0, 0, tiled=True)  46.6 us
    all_to_all x4, starting transfers between devices, exchange(): return lax.all_to_all(x, axis, 0, 0, tiled=True)  20.1 us
    unnamed x56, local copies, waits for them, and re-layouts  18.7 us
    pallas_call x12, Pallas kernels, run(): pl.pallas_call(kernel, out_shape=[jax.ShapeDtypeStruct(shape, kind) for s...  13 us
    ppermute x2, starting transfers between devices, swap_cores(): return lax.ppermute(x, 'ctx', [(i, i ^ 1) for i in range(CTX)])  4 us
  transfers between devices with their start and end apart: 6, of which 6 were waited for; matrix products, arithmetic and copies ran while one was open for 0% of the time, Pallas kernels for 3%

profile of v2, /device:TPU:1, one launch (start us, length us, event | category | flops | bytes accessed | tf_op | source)
XLA Modules:
  0.0 171.3 jit_solution(2156522100947335442)
XLA Ops:
  1.3 0.9 copy-done.4
  2.2 0.9 copy-done.5
  3.2 0.7 copy-done.12
  3.9 0.8 copy-done.23
  4.6 0.8 copy-done.24
  5.4 0.8 copy-done.25
  6.1 0.7 copy-done.27
  6.8 0.7 send_kernel.1
  7.5 33.8 %all_to_all.35.received.first = f32[16,104,128]{2,1,0:T(8,128)S(1)} all-to-all(f32[16,104,128]{2,1,0:T(8,128)S(1)} %get-tuple-element.44), channel_id=1, replica_groups=mesh['sample'=8,'ctx'=16,'head'=4] {'ctx'}, dimensions={0} | all-to-all | bytes 1703936 | tf_op jit(solution)/shard_map/all_to_all | solution.py:401
  41.4 1.2 prompt_row_kernel.1
  42.6 9.0 %all-to-all-start.1 = ((f32[8,72,128]{2,1,0:T(8,128)}), f32[8,72,128]{2,1,0:T(8,128)S(1)}, u32[]{:S(2)}, u32[]{:S(2)}) async-start(f32[8,72,128]{2,1,0:T(8,128)} %get-tuple-element.45), calls=%async_computation.1 | async-start | bytes 589824 | tf_op jit(solution)/shard_map/all_to_all | solution.py:401
  51.5 1.9 %collective-permute-start = (f32[16,8,128]{2,1,0:T(8,128)S(1)}, f32[16,8,128]{2,1,0:T(8,128)S(1)}, u32[]{:S(2)}, u32[]{:S(2)}) collective-permute-start(f32[16,8,128]{2,1,0:T(8,128)S(1)} %get-tuple-element.46.own), channel_id=1, source_target_pairs={{0,4},{4,0},{8,12},{12,8},{16,20},{20,16},{24,28},{28,24},{32,36},... | collective-permute-start | bytes 196616 | tf_op jit(solution)/shard_map/ppermute | solution.py:405
  53.5 1.2 collective-permute-done.other
  55.1 0.6 copy-done.14
  55.8 0.6 copy-done.16
  56.4 8.3 %all-to-all-done.1.rows_received = f32[8,72,128]{2,1,0:T(8,128)S(1)} async-done(((f32[8,72,128]{2,1,0:T(8,128)}), f32[8,72,128]{2,1,0:T(8,128)S(1)}, u32[]{:S(2)}, u32[]{:S(2)}) %all-to-all-start.1) | async-done | bytes 294944 | tf_op jit(solution)/shard_map/all_to_all | solution.py:401
  64.7 1.1 fold_kernel.1
  65.8 3.9 %all-to-all-start.2 = ((f32[16,72,128]{2,1,0:T(8,128)}), f32[16,72,128]{2,1,0:T(8,128)S(1)}, u32[]{:S(2)}, u32[]{:S(2)}) async-start(f32[16,72,128]{2,1,0:T(8,128)} %get-tuple-element.53), calls=%async_computation.2 | async-start | bytes 1179648 | tf_op jit(solution)/shard_map/all_to_all | solution.py:401
  69.7 1.5 reply_local_kernel.1
  71.2 0.8 copy-done.2
  72.1 0.7 copy-done.8
  72.8 15.6 %all-to-all-done.2.received = f32[16,72,128]{2,1,0:T(8,128)S(1)} async-done(((f32[16,72,128]{2,1,0:T(8,128)}), f32[16,72,128]{2,1,0:T(8,128)S(1)}, u32[]{:S(2)}, u32[]{:S(2)}) %all-to-all-start.2) | async-done | bytes 589856 | tf_op jit(solution)/shard_map/all_to_all | solution.py:401
  88.4 0.7 copy-done.26
  89.0 1.0 copy-done.3
  90.6 8.0 %all_to_all.36.sums = f32[4,8,128]{2,1,0:T(8,128)S(1)} all-to-all(f32[4,8,128]{2,1,0:T(8,128)S(1)} %get-tuple-element.59), channel_id=1, replica_groups=mesh['sample'=8,'ctx'=16,'head'=4] {'head'}, dimensions={0} | all-to-all | bytes 32768 | tf_op jit(solution)/shard_map/all_to_all | solution.py:401
  98.7 0.6 grad_kernel.1
  99.3 23.2 %all_to_all.37.received = f32[16,72,128]{2,1,0:T(8,128)S(1)} all-to-all(f32[16,72,128]{2,1,0:T(8,128)S(1)} %get-tuple-element.62), channel_id=1, replica_groups=mesh['sample'=8,'ctx'=16,'head'=4] {'ctx'}, dimensions={0} | all-to-all | bytes 1179648 | tf_op jit(solution)/shard_map/all_to_all | solution.py:401
  122.5 1.0 back_fold_kernel.1
  123.5 3.4 %all-to-all-start.5 = ((f32[8,64,128]{2,1,0:T(8,128)}), f32[8,64,128]{2,1,0:T(8,128)S(1)}, u32[]{:S(2)}, u32[]{:S(2)}) async-start(f32[8,64,128]{2,1,0:T(8,128)} %back_fold_kernel.1), calls=%async_computation.5 | async-start | bytes 524288 | tf_op jit(solution)/shard_map/all_to_all | solution.py:401
  126.9 0.9 copy-done.15
  127.8 0.9 copy-done.17
  128.7 0.6 prompt_mid_kernel.1
  129.4 0.8 copy-done
  130.2 0.6 copy-done.18
  130.8 0.7 copy-done.20
  131.5 2.1 %collective-permute-start.1 = (f32[16,8,128]{2,1,0:T(8,128)S(1)}, f32[16,8,128]{2,1,0:T(8,128)S(1)}, u32[]{:S(2)}, u32[]{:S(2)}) collective-permute-start(f32[16,8,128]{2,1,0:T(8,128)S(1)} %get-tuple-element.69), channel_id=1, source_target_pairs={{0,4},{4,0},{8,12},{12,8},{16,20},{20,16},{24,28},{28,24},{32,36},... | collective-permute-start | bytes 196616 | tf_op jit(solution)/shard_map/ppermute | solution.py:405
  133.6 1.0 collective-permute-done.1.swapped
  134.6 4.6 %all-to-all-done.5.rows_received = f32[8,64,128]{2,1,0:T(8,128)S(1)} async-done(((f32[8,64,128]{2,1,0:T(8,128)}), f32[8,64,128]{2,1,0:T(8,128)S(1)}, u32[]{:S(2)}, u32[]{:S(2)}) %all-to-all-start.5) | async-done | bytes 262176 | tf_op jit(solution)/shard_map/all_to_all | solution.py:401
  139.2 1.0 copy-done.1
  140.3 0.9 copy-done.19
  141.2 0.9 copy-done.21
  142.1 1.2 prompt_back_kernel.1
  143.3 3.9 %all-to-all-start.6 = ((f32[16,96,128]{2,1,0:T(8,128)}), f32[16,96,128]{2,1,0:T(8,128)S(1)}, u32[]{:S(2)}, u32[]{:S(2)}) async-start(f32[16,96,128]{2,1,0:T(8,128)} %prompt_back_kernel.1), calls=%async_computation.6 | async-start | bytes 1572864 | tf_op jit(solution)/shard_map/all_to_all | solution.py:401
  147.2 0.9 copy-done.9
  148.1 0.9 copy-done.11
  149.0 2.6 %reply_back_kernel.1 = (bf16[1,128,8,128]{3,2,1,0:T(8,128)(2,1)}, f32[8,128,128]{2,1,0:T(8,128)S(1)}, f32[8,128,128]{2,1,0:T(8,128)S(1)}) custom-call(f32[16,72,128]{2,1,0:T(8,128)S(1)} %all-to-all-done.2.received, bf16[8,128,128]{2,1,0:T(8,128)(2,1)S(1)} %copy-done.11, bf16[8,128,128]{2,1,0:T(8,128)(2,1)S(1)} %get-tuple-element.56.query, ...), custom_call_target="tpu_custom_call" | custom-call | flops 201326592 | bytes 3809280 | tf_op jit(solution)/shard_map/reply_back_kernel/pallas_call | solution.py:388
  151.7 18.2 %all-to-all-done.6.received = f32[16,96,128]{2,1,0:T(8,128)S(1)} async-done(((f32[16,96,128]{2,1,0:T(8,128)}), f32[16,96,128]{2,1,0:T(8,128)S(1)}, u32[]{:S(2)}, u32[]{:S(2)}) %all-to-all-start.6) | async-done | bytes 786464 | tf_op jit(solution)/shard_map/all_to_all | solution.py:401
  169.9 1.5 end_kernel.1
  (35 shorter events, 1.0 us)
Async XLA Ops:
  1.3 1.0 copy-start.4
  2.2 0.9 copy-start.5
  3.2 0.7 copy-start.12
  3.9 0.8 copy-start.23
  4.6 0.8 copy-start.24
  5.4 0.8 copy-start.25
  6.1 0.7 copy-start.27
  42.6 22.1 %all-to-all-start.1 = ((f32[8,72,128]{2,1,0:T(8,128)}), f32[8,72,128]{2,1,0:T(8,128)S(1)}, u32[]{:S(2)}, u32[]{:S(2)}) async-start(f32[8,72,128]{2,1,0:T(8,128)} %get-tuple-element.45), calls=%async_computation.1 | async-start | bytes 589824 | tf_op jit(solution)/shard_map/all_to_all | solution.py:401
  51.5 3.1 %collective-permute-start = (f32[16,8,128]{2,1,0:T(8,128)S(1)}, f32[16,8,128]{2,1,0:T(8,128)S(1)}, u32[]{:S(2)}, u32[]{:S(2)}) collective-permute-start(f32[16,8,128]{2,1,0:T(8,128)S(1)} %get-tuple-element.46.own), channel_id=1, source_target_pairs={{0,4},{4,0},{8,12},{12,8},{16,20},{20,16},{24,28},{28,24},{32,36},... | collective-permute-start | bytes 196616 | tf_op jit(solution)/shard_map/ppermute | solution.py:405
  55.1 0.7 copy-start.14
  55.8 0.7 copy-start.16
  65.8 3.9 %copy-start.6 = (bf16[1,128,8,128]{3,2,1,0:T(8,128)(2,1)S(1)}, bf16[1,128,8,128]{3,2,1,0:T(8,128)(2,1)}, u32[]{:S(2)}) copy-start(bf16[1,128,8,128]{3,2,1,0:T(8,128)(2,1)} %query.1) | copy-start | bytes 786436
  65.8 3.9 %copy-start.7 = (bf16[1,128,8,128]{3,2,1,0:T(8,128)(2,1)S(1)}, bf16[1,128,8,128]{3,2,1,0:T(8,128)(2,1)}, u32[]{:S(2)}) copy-start(bf16[1,128,8,128]{3,2,1,0:T(8,128)(2,1)} %grad.1) | copy-start | bytes 786436
  65.8 3.9 %copy-start.13 = (f32[1,8,128]{2,1,0:T(8,128)S(1)}, f32[1,8,128]{2,1,0:T(8,128)}, u32[]{:S(2)}) copy-start(f32[1,8,128]{2,1,0:T(8,128)} %decay.11) | copy-start | bytes 12292
  65.8 22.5 %all-to-all-start.2 = ((f32[16,72,128]{2,1,0:T(8,128)}), f32[16,72,128]{2,1,0:T(8,128)S(1)}, u32[]{:S(2)}, u32[]{:S(2)}) async-start(f32[16,72,128]{2,1,0:T(8,128)} %get-tuple-element.53), calls=%async_computation.2 | async-start | bytes 1179648 | tf_op jit(solution)/shard_map/all_to_all | solution.py:401
  69.7 18.6 %copy-start.22 = (bf16[16,8,128]{2,1,0:T(8,128)(2,1)S(1)}, bf16[16,8,128]{2,1,0:T(8,128)(2,1)}, u32[]{:S(2)}) copy-start(bf16[16,8,128]{2,1,0:T(8,128)(2,1)} %prompt_grad.3) | copy-start | bytes 98308
  71.2 0.8 copy-start.2
  72.1 0.7 copy-start.8
  88.4 0.7 copy-start.26
  89.0 1.0 copy-start.3
  99.3 23.2 %copy-start.10 = (bf16[8,128,128]{2,1,0:T(8,128)(2,1)}, bf16[8,128,128]{2,1,0:T(8,128)(2,1)S(1)}, u32[]{:S(2)}) copy-start(bf16[8,128,128]{2,1,0:T(8,128)(2,1)S(1)} %get-tuple-element.72.out_grad) | copy-start | bytes 786436
  123.5 15.7 %all-to-all-start.5 = ((f32[8,64,128]{2,1,0:T(8,128)}), f32[8,64,128]{2,1,0:T(8,128)S(1)}, u32[]{:S(2)}, u32[]{:S(2)}) async-start(f32[8,64,128]{2,1,0:T(8,128)} %back_fold_kernel.1), calls=%async_computation.5 | async-start | bytes 524288 | tf_op jit(solution)/shard_map/all_to_all | solution.py:401
  126.9 0.9 copy-start.15
  127.8 0.9 copy-start.17
  129.4 0.8 copy-start
  130.2 0.6 copy-start.18
  130.8 0.7 copy-start.20
  131.5 3.1 %collective-permute-start.1 = (f32[16,8,128]{2,1,0:T(8,128)S(1)}, f32[16,8,128]{2,1,0:T(8,128)S(1)}, u32[]{:S(2)}, u32[]{:S(2)}) collective-permute-start(f32[16,8,128]{2,1,0:T(8,128)S(1)} %get-tuple-element.69), channel_id=1, source_target_pairs={{0,4},{4,0},{8,12},{12,8},{16,20},{20,16},{24,28},{28,24},{32,36},... | collective-permute-start | bytes 196616 | tf_op jit(solution)/shard_map/ppermute | solution.py:405
  139.2 1.0 copy-start.1
  140.3 0.9 copy-start.19
  141.2 0.9 copy-start.21
  143.3 26.6 %all-to-all-start.6 = ((f32[16,96,128]{2,1,0:T(8,128)}), f32[16,96,128]{2,1,0:T(8,128)S(1)}, u32[]{:S(2)}, u32[]{:S(2)}) async-start(f32[16,96,128]{2,1,0:T(8,128)} %prompt_back_kernel.1), calls=%async_computation.6 | async-start | bytes 1572864 | tf_op jit(solution)/shard_map/all_to_all | solution.py:401
  147.1 0.9 copy-start.9
  148.1 0.9 copy-start.11

commit v3 on v2

v3 whole, which is shorter than its diff:
```python
import jax
import jax.numpy as jnp
from jax import lax
from jax.experimental import pallas as pl
from jax.experimental.pallas import tpu as pltpu
from jax.sharding import PartitionSpec as P

EPSILON = 1e-05
F32 = jnp.float32
BF16 = jnp.bfloat16
HEADS = 8
D = 128
HALF = D // 2
T = 128
PT = 16
CTX = 16
SAMPLE = 8
HEAD_AXIS = 4
ROW = CTX * PT
FEATURES = float(HEADS * HEAD_AXIS * D)


def iota(shape, axis):
    return lax.broadcasted_iota(jnp.int32, shape, axis)


def dot(a, b, ca, cb):
    return lax.dot_general(a, b, (((ca,), (cb,)), ((), ())), preferred_element_type=F32)


def split(x):
    high = x.astype(BF16)
    return high, (x - high.astype(F32)).astype(BF16)


def split3(x):
    high, rest = x.astype(BF16), None
    rest = x - high.astype(F32)
    mid = rest.astype(BF16)
    return high, mid, (rest - mid.astype(F32)).astype(BF16)


def dot_right(a, x, ca, cb):
    return sum(dot(a, part, ca, cb) for part in split(x))


def dot_left(x, b, ca, cb):
    return sum(dot(part, b, ca, cb) for part in split(x))


def low_lanes(rows):
    return iota((rows, D), 1) < HALF


def pack(x, half):
    top, bottom, low = x[0:8], x[8:16], low_lanes(8)
    if half == 0:
        return jnp.where(low, top, pltpu.roll(bottom, HALF, 1))
    return jnp.where(low, pltpu.roll(top, HALF, 1), bottom)


def unpack(first, second):
    low = low_lanes(8)
    top = jnp.where(low, first, pltpu.roll(second, HALF, 1))
    bottom = jnp.where(low, pltpu.roll(first, HALF, 1), second)
    return jnp.concatenate([top, bottom], axis=0)


def rows_of_half(x):
    both = jnp.stack([x[:, :, :HALF], x[:, :, HALF:]], axis=1)
    return both.reshape(ROW, HALF)


def packed_half(x):
    both = x.reshape(CTX, 2, 8, HALF)
    return jnp.concatenate([both[:, 0], both[:, 1]], axis=-1)


def running_rows(decay):
    upper = (iota((T, T), 0) <= iota((T, T), 1)).astype(BF16)
    return sum(dot(part, upper, 1, 0) for part in split3(decay))


def running_columns(decay):
    lower = (iota((T, T), 1) <= iota((T, T), 0)).astype(BF16)
    return sum(dot(lower, part, 1, 1) for part in split3(decay))


def masking(column, row):
    extent = row.shape[1]
    causal = iota((extent, extent), 0) >= iota((extent, extent), 1)
    return jnp.where(causal, jnp.exp(jnp.where(causal, column - row, 0.0)), 0.0)


def column_to_row(column):
    extent = column.shape[0]
    eye = iota((extent, max(extent, D)), 0) == iota((extent, max(extent, D)), 1)
    return jnp.sum(jnp.where(eye, column, 0.0), axis=0, keepdims=True)


def row_to_column(row, extent):
    eye = iota((extent, row.shape[1]), 0) == iota((extent, row.shape[1]), 1)
    return jnp.sum(jnp.where(eye, row, 0.0), axis=1, keepdims=True)


def live_tokens(lengths):
    return lax.axis_index("ctx") * T + iota((T, 1), 0) < lengths[0]


def start_copies(pairs, sems):
    copies = [pltpu.make_async_copy(source, target, sems.at[i]) for i, (source, target) in enumerate(pairs)]
    for copy in copies:
        copy.start()
    return copies


def send_kernel(
    lengths, key, value, decay, prompt_query, prompt_key, prompt_value, prompt_decay, out, key_out, value_out,
    key_in, value_in, decay_in, query_in, prompt_key_in, prompt_value_in, prompt_decay_in,
    rows_k, rows_v, prompt_q, prompt_k, prompt_v, sems,
):
    copies = start_copies(
        [
            (decay, decay_in),
            (prompt_decay, prompt_decay_in),
            (prompt_query, query_in),
            (prompt_key, prompt_key_in),
            (prompt_value, prompt_value_in),
            (value, value_in),
            (key, key_in),
        ],
        sems,
    )
    live = live_tokens(lengths)
    for copy in copies[:5]:
        copy.wait()
    columns = running_columns(decay_in[0])
    to_end = jnp.exp(columns[T - 1 : T, :] - columns)
    wide = jnp.concatenate([prompt_decay_in[...], jnp.zeros((HEADS, D - PT), F32)], axis=1)
    totals = jnp.sum(decay_in[0], axis=1, keepdims=True)
    at = iota((8, D), 0)
    prompt_q[...] = query_in[...].astype(F32).reshape(PT * HEADS, D)
    prompt_k[...] = prompt_key_in[...].astype(F32).reshape(PT * HEADS, D)
    prompt_v[...] = prompt_value_in[...].astype(F32).reshape(PT * HEADS, D)
    for h in range(HEADS):
        tail = jnp.where(at == 0, wide[h : h + 1], jnp.where(at == 1, totals[h : h + 1], 0.0))
        q = prompt_q[pl.ds(h, PT, HEADS), :]
        k = prompt_k[pl.ds(h, PT, HEADS), :]
        v = prompt_v[pl.ds(h, PT, HEADS), :]
        for half in range(2):
            out[2 * h + half, 64:80, :] = k
            out[2 * h + half, 80:88, :] = pack(v, half)
            out[2 * h + half, 88:96, :] = tail
            out[2 * h + half, 96:104, :] = q[8 * half : 8 * half + 8]
    for copy in copies[5:]:
        copy.wait()
    rows_v[...] = value_in[0].astype(F32).reshape(T * HEADS, D)
    rows_k[...] = key_in[0].astype(F32).reshape(T * HEADS, D)
    for h in range(HEADS):
        k = jnp.where(live, rows_k[pl.ds(h, T, HEADS), :], 0.0)
        v = jnp.where(live, rows_v[pl.ds(h, T, HEADS), :], 0.0).astype(BF16)
        key_out[h] = k.astype(BF16)
        value_out[h] = v
        state = dot_right(v, k * to_end[:, h : h + 1], 0, 0)
        for half in range(2):
            out[2 * h + half, 0:64, :] = state[half * HALF : (half + 1) * HALF]


def wide_columns(columns):
    return jnp.concatenate([columns, jnp.zeros((T, D - HEADS), F32)], axis=1)


def reply_local_kernel(
    lengths, query, grad, key, decay, gain, prompt_grad,
    query_out, grad_out, weights_out, growth_out, scale_out, upstream_out,
    query_in, grad_in, rows, rows_g, prompt_rows, sems,
):
    copies = start_copies([(query, query_in), (grad, grad_in)], sems)
    live = live_tokens(lengths)
    lines = running_rows(decay[0])
    columns = running_columns(decay[0])
    growth_out[...] = wide_columns(jnp.exp(columns))
    scale = gain[...].astype(F32)
    scale_out[...] = scale
    prompt_rows[...] = prompt_grad[...].astype(F32).reshape(PT * HEADS, D)
    for h in range(HEADS):
        upstream_out[h] = prompt_rows[pl.ds(h, PT, HEADS), :] * scale[h : h + 1]
    for copy in copies:
        copy.wait()
    rows[...] = query_in[0].astype(F32).reshape(T * HEADS, D)
    rows_g[...] = grad_in[0].astype(F32).reshape(T * HEADS, D)
    for h in range(HEADS):
        q = jnp.where(live, rows[pl.ds(h, T, HEADS), :], 0.0).astype(BF16)
        query_out[h] = q
        mask = masking(columns[:, h : h + 1], lines[h : h + 1])
        weights_out[h] = (dot(q, key[h], 1, 1) * mask).astype(BF16)
        grad_out[h] = jnp.where(live, rows_g[pl.ds(h, T, HEADS), :], 0.0).astype(BF16)


def prompt_row_kernel(received, out, column_out, query_out, blocks_out):
    decay = received[:, 88, :]
    token_block, token_place = iota((ROW, CTX), 0) // PT, iota((ROW, D), 0) % PT
    block = iota((ROW, CTX), 1)
    parts = split3(decay)
    own = sum(dot((block == token_block).astype(BF16), part, 1, 0) for part in parts)
    before = sum(dot((block < token_block).astype(BF16), part, 1, 0) for part in parts)
    running = jnp.sum(before + jnp.where(iota((ROW, D), 1) <= token_place, own, 0.0), axis=1, keepdims=True)
    last = running[ROW - 1 : ROW]
    k = received[:, 64:80, :].reshape(ROW, D)
    v = rows_of_half(received[:, 80:88, :]).astype(BF16)
    state = dot_right(v, k * jnp.exp(last - running), 0, 0)
    total = jnp.broadcast_to(last, (8, D))
    for s in range(SAMPLE):
        out[s, 0:64, :] = state
        out[s, 64:72, :] = total
    column_out[...] = jnp.broadcast_to(running, (ROW, D))
    query_out[...] = received[:, 96:104, :]
    blocks_out[...] = received[:, 89, :]


def same_block():
    return iota((ROW, ROW), 0) // PT == iota((ROW, ROW), 1) // PT


def prompt_weights(q, k, mask):
    scores = dot(q, k, 1, 1) * mask
    high = scores.astype(BF16)
    low = jnp.where(same_block(), 0.0, scores - high.astype(F32)).astype(BF16)
    return high, low


def second_core():
    return lax.axis_index("ctx") % 2 == 1


def prompt_local_kernel(
    received, other, column, query_out, key_out, value_out, line_out, local_out
):
    own = received[:, 96:104, :]
    second = second_core()
    first_half = jnp.where(second, other[...], own)
    second_half = jnp.where(second, own, other[...])
    q = jnp.concatenate([first_half, second_half], axis=1).reshape(ROW, D).astype(BF16)
    k = received[:, 64:80, :].reshape(ROW, D).astype(BF16)
    v = rows_of_half(received[:, 80:88, :]).astype(BF16)
    running = column[:, 0:1]
    line = column_to_row(running)
    query_out[...] = q
    key_out[...] = k
    value_out[...] = v
    line_out[...] = jnp.broadcast_to(line, (8, ROW))
    weights = prompt_weights(q, k, masking(running, line))
    local_out[...] = sum(dot(part, v, 1, 0) for part in weights)


def fold_kernel(rows_received, received, query, local, column, out, start_out, total_out):
    place = lax.axis_index("sample")
    end = jnp.zeros((HALF, D), F32)
    start = end
    for s in range(SAMPLE):
        start = jnp.where(place == s, end, start)
        total = rows_received[s, 64:65, :]
        total_out[s : s + 1, :] = total
        end = jnp.exp(total) * end + rows_received[s, 0:64, :]
    start_out[...] = start
    state = end
    for b in range(CTX):
        out[b, 0:64, :] = state
        state = jnp.exp(received[b, 89:90, :]) * state + received[b, 0:64, :]
    outputs = local[...] + jnp.exp(column[:, 0:1]) * dot_right(query[...], start, 1, 1)
    out[:, 64:72, :] = packed_half(outputs)


def output_kernel(
    received, query, weights, value, grad, growth, scale, prompt_upstream, out, output_out, prompt_out
):
    squares = jnp.zeros((T, D), F32)
    crossed = jnp.zeros((T, D), F32)
    prompt_squares = jnp.zeros((PT, D), F32)
    prompt_crossed = jnp.zeros((PT, D), F32)
    for h in range(HEADS):
        state = jnp.concatenate([received[2 * h, 0:64, :], received[2 * h + 1, 0:64, :]], axis=0)
        outputs = dot(weights[h], value[h], 1, 0) + growth[:, h : h + 1] * dot_right(query[h], state, 1, 1)
        output_out[h] = outputs
        upstream = grad[h].astype(F32) * scale[h : h + 1, :]
        squares = squares + outputs * outputs
        crossed = crossed + upstream * outputs
        outputs = unpack(received[2 * h, 64:72, :], received[2 * h + 1, 64:72, :])
        prompt_out[h] = outputs
        prompt_squares = prompt_squares + outputs * outputs
        prompt_crossed = prompt_crossed + prompt_upstream[h] * outputs
    sums = [
        column_to_row(jnp.sum(part, axis=1, keepdims=True))
        for part in (squares, crossed, prompt_squares, prompt_crossed)
    ]
    at = iota((8, D), 0)
    tile = jnp.zeros((8, D), F32)
    for i, part in enumerate(sums):
        tile = jnp.where(at == i, part, tile)
    for x in range(HEAD_AXIS):
        out[x] = tile


def norm_terms(squares, crossed):
    inverse = lax.rsqrt(squares / FEATURES + EPSILON)
    return inverse, crossed * inverse * inverse / FEATURES


def grad_kernel(
    sums, outputs, prompt_outputs, query, grad, growth, scale, prompt_upstream, out, grad_out
):
    total = sums[0] + sums[1] + sums[2] + sums[3]
    inverse, project = norm_terms(row_to_column(total[0:1], T), row_to_column(total[1:2], T))
    prompt_inverse, prompt_project = norm_terms(row_to_column(total[2:3], PT), row_to_column(total[3:4], PT))
    for h in range(HEADS):
        upstream = grad[h].astype(F32) * scale[h : h + 1, :]
        out_grad = ((upstream - outputs[h] * project) * inverse).astype(BF16)
        grad_out[h] = out_grad
        back = dot_right(out_grad, query[h].astype(F32) * growth[:, h : h + 1], 0, 0)
        prompt_out_grad = (prompt_upstream[h] - prompt_outputs[h] * prompt_project) * prompt_inverse
        prompt_out_grad = prompt_out_grad.astype(BF16).astype(F32)
        for half in range(2):
            out[2 * h + half, 0:64, :] = back[half * HALF : (half + 1) * HALF]
            out[2 * h + half, 64:72, :] = pack(prompt_out_grad, half)


def reply_back_kernel(
    received, out_grad, query, key, value, weights, decay, totals,
    query_grad, key_local, value_local, to_end_out, factors_out, rows,
):
    lines = running_rows(decay[0])
    columns = running_columns(decay[0])
    scales = jnp.exp(columns)
    to_end_out[...] = wide_columns(jnp.exp(columns[T - 1 : T, :] - columns))
    place = lax.axis_index("sample")
    for s in range(SAMPLE):
        after = jnp.zeros((1, D), F32)
        between = after
        for other in range(s + 1, SAMPLE):
            after = after + totals[other : other + 1, :]
            between = between + jnp.where(other < place, totals[other : other + 1, :], 0.0)
        factors_out[s : s + 1, :] = jnp.exp(after)
        factors_out[SAMPLE + s : SAMPLE + s + 1, :] = jnp.where(place > s, jnp.exp(between), 0.0)
    for h in range(HEADS):
        state = jnp.concatenate([received[2 * h, 0:64, :], received[2 * h + 1, 0:64, :]], axis=0)
        og = out_grad[h]
        mask = masking(columns[:, h : h + 1], lines[h : h + 1])
        mix = (dot(og, value[h], 1, 1) * mask).astype(BF16)
        rows[pl.ds(h, T, HEADS), :] = dot(mix, key[h], 1, 0) + scales[:, h : h + 1] * dot_right(og, state, 1, 0)
        key_local[h] = dot(mix, query[h], 0, 0)
        value_local[h] = dot(weights[h], og, 0, 0)
    query_grad[0] = rows[...].reshape(T, HEADS, D).astype(BF16)


def back_fold_kernel(received, blocks, factors, query, column, rows_out):
    adjoint = jnp.zeros((HALF, D), F32)
    for b in range(CTX - 1, -1, -1):
        adjoint = jnp.exp(blocks[b : b + 1, :]) * adjoint + received[b, 0:64, :]
    og = rows_of_half(received[:, 64:72, :]).astype(BF16)
    back = dot_right(og, query[...].astype(F32) * jnp.exp(column[:, 0:1]), 0, 0)
    for s in range(SAMPLE):
        rows_out[s] = factors[s : s + 1, :] * adjoint + factors[SAMPLE + s : SAMPLE + s + 1, :] * back


def prompt_mid_kernel(received, blocks, start, query, key, value, column, line, out, swap_out):
    adjoint = jnp.zeros((HALF, D), F32)
    for b in range(CTX - 1, -1, -1):
        out[b, 0:64, :] = adjoint
        adjoint = jnp.exp(blocks[b : b + 1, :]) * adjoint + received[b, 0:64, :]
    og = rows_of_half(received[:, 64:72, :]).astype(BF16)
    running = column[:, 0:1]
    mask = masking(running, line[0:1, :])
    mix = split(dot(og, value[...], 1, 1) * mask)
    k, q = key[...], query[...]
    query_grad = sum(dot(part, k, 1, 0) for part in mix) + jnp.exp(running) * dot_right(og, start[...], 1, 0)
    query_grad = query_grad.reshape(CTX, PT, D)
    second = second_core()
    swap_out[...] = jnp.where(second, query_grad[:, 0:8], query_grad[:, 8:16])
    key_local = sum(dot(part, q, 0, 0) for part in mix)
    value_local = sum(dot(part, og, 0, 0) for part in prompt_weights(q, k, mask))
    out[:, 64:80, :] = key_local.reshape(CTX, PT, D)
    out[:, 80:88, :] = packed_half(value_local)
    out[:, 88:96, :] = jnp.where(second, query_grad[:, 8:16], query_grad[:, 0:8])


def prompt_back_kernel(rows_received, swapped, key, value, column, message, out, part, sems):
    arrive = pltpu.make_async_copy(message.at[:, 64:96, :], part, sems.at[0])
    arrive.start()
    adjoint = rows_received[0]
    for s in range(1, SAMPLE):
        adjoint = adjoint + rows_received[s]
    running = column[:, 0:1]
    to_end = jnp.exp(running[ROW - 1 : ROW] - running)
    key_grad = to_end * dot_right(value[...], adjoint, 1, 0)
    value_grad = to_end * dot_right(key[...], adjoint, 1, 1)
    arrive.wait()
    part[:, 0:16, :] += key_grad.reshape(CTX, PT, D)
    part[:, 16:24, :] += packed_half(value_grad)
    part[:, 24:32, :] += swapped[...]
    leave = pltpu.make_async_copy(part, out.at[:, 64:96, :], sems.at[1])
    leave.start()
    leave.wait()


def end_kernel(
    received, key, value, key_local, value_local, to_end,
    key_grad, value_grad, prompt_query_grad, prompt_key_grad, prompt_value_grad,
    rows_k, rows_v, prompt_q, prompt_k, prompt_v,
):
    for h in range(HEADS):
        low, high = received[2 * h], received[2 * h + 1]
        adjoint = jnp.concatenate([low[0:64], high[0:64]], axis=0)
        scale = to_end[:, h : h + 1]
        rows_k[pl.ds(h, T, HEADS), :] = key_local[h] + scale * dot_right(value[h], adjoint, 1, 0)
        rows_v[pl.ds(h, T, HEADS), :] = value_local[h] + scale * dot_right(key[h], adjoint, 1, 1)
        prompt_k[pl.ds(h, PT, HEADS), :] = low[64:80] + high[64:80]
        prompt_v[pl.ds(h, PT, HEADS), :] = unpack(low[80:88], high[80:88])
        prompt_q[pl.ds(h, PT, HEADS), :] = jnp.concatenate([low[88:96], high[88:96]], axis=0)
    key_grad[0] = rows_k[...].reshape(T, HEADS, D).astype(BF16)
    value_grad[0] = rows_v[...].reshape(T, HEADS, D).astype(BF16)
    prompt_query_grad[...] = prompt_q[...].reshape(PT, HEADS, D).astype(BF16)
    prompt_key_grad[...] = prompt_k[...].reshape(PT, HEADS, D).astype(BF16)
    prompt_value_grad[...] = prompt_v[...].reshape(PT, HEADS, D).astype(BF16)


VMEM = pl.BlockSpec(memory_space=pltpu.VMEM)
SMEM = pl.BlockSpec(memory_space=pltpu.SMEM)
HBM = pl.BlockSpec(memory_space=pltpu.HBM)
REPLY_ROWS = pltpu.VMEM((T * HEADS, D), F32)
PROMPT_ROWS = pltpu.VMEM((PT * HEADS, D), F32)
BY_HEAD = ((HEADS, T, D), BF16)
BY_HEAD_WIDE = ((HEADS, T, D), F32)
REPLY = ((1, T, HEADS, D), BF16)
PROMPT = ((PT, HEADS, D), BF16)


def run(kernel, outs, scratch, *operands, hbm=(), hbm_outs=(), kept=(), far=(), aliases=None, flops=0):
    operands = [
        pltpu.with_memory_space_constraint(operand, pltpu.HBM) if i in hbm else operand
        for i, operand in enumerate(operands)
    ]
    specs = [
        SMEM if operand.dtype == jnp.int32 else HBM if i in hbm else VMEM for i, operand in enumerate(operands)
    ]
    moved = sum(operand.size * operand.dtype.itemsize for operand in operands)
    return pl.pallas_call(
        kernel,
        out_shape=[
            pltpu.VMEM(shape, kind)
            if i in kept
            else pltpu.HBM(shape, kind)
            if i in far
            else jax.ShapeDtypeStruct(shape, kind)
            for i, (shape, kind) in enumerate(outs)
        ],
        in_specs=specs,
        out_specs=[HBM if i in hbm_outs else VMEM for i in range(len(outs))],
        scratch_shapes=scratch,
        input_output_aliases=aliases or {},
        compiler_params=pltpu.CompilerParams(vmem_limit_bytes=8 * 1024 * 1024),
        cost_estimate=pl.CostEstimate(flops=flops, bytes_accessed=2 * moved, transcendentals=0),
        name=kernel.__name__,
    )(*operands)


def exchange(x, axis):
    return lax.all_to_all(x, axis, 0, 0, tiled=True)


def swap_cores(x):
    return lax.ppermute(x, "ctx", [(i, i ^ 1) for i in range(CTX)])


def shards(
    prompt_query,
    prompt_key,
    prompt_value,
    prompt_grad,
    prompt_decay,
    reply_query,
    reply_key,
    reply_value,
    reply_grad,
    reply_decay,
    reply_lengths,
    norm_gain,
):
    work = 8 * 2 * T * D * D
    reply_in, prompt_in = pltpu.VMEM(*REPLY), pltpu.VMEM(*PROMPT)
    sent, key, value = run(
        send_kernel,
        [((CTX, 104, D), F32), BY_HEAD, BY_HEAD],
        [reply_in, reply_in, pltpu.VMEM((1, HEADS, T), F32)]
        + [prompt_in] * 3
        + [pltpu.VMEM((HEADS, PT), F32)]
        + [REPLY_ROWS] * 2
        + [PROMPT_ROWS] * 3
        + [pltpu.SemaphoreType.DMA((7,))],
        reply_lengths,
        reply_key,
        reply_value,
        reply_decay,
        prompt_query,
        prompt_key,
        prompt_value,
        prompt_decay,
        hbm=range(1, 8),
        flops=2 * work,
        kept=(1, 2),
    )
    first = exchange(sent, "ctx")
    sent, column, half_query, blocks = run(
        prompt_row_kernel,
        [((SAMPLE, 72, D), F32), ((ROW, D), F32), ((CTX, 8, D), F32), ((CTX, D), F32)],
        [],
        first,
        kept=(1, 3),
    )
    rows = exchange(sent, "sample")
    query, grad, weights, growth, scale, prompt_upstream = run(
        reply_local_kernel,
        [BY_HEAD, BY_HEAD, BY_HEAD, ((T, D), F32), ((HEADS, D), F32), ((HEADS, PT, D), F32)],
        [reply_in, reply_in, REPLY_ROWS, REPLY_ROWS, PROMPT_ROWS, pltpu.SemaphoreType.DMA((2,))],
        reply_lengths,
        reply_query,
        reply_grad,
        key,
        reply_decay,
        norm_gain,
        prompt_grad,
        hbm=(1, 2),
        flops=2 * work,
        kept=range(6),
    )
    row_query, row_key, row_value, line, row_local = run(
        prompt_local_kernel,
        [
            ((ROW, D), BF16),
            ((ROW, D), BF16),
            ((ROW, HALF), BF16),
            ((8, ROW), F32),
            ((ROW, HALF), F32),
        ],
        [],
        first,
        swap_cores(half_query),
        column,
        flops=work,
        kept=range(5),
    )
    sent, start, totals = run(
        fold_kernel,
        [((CTX, 72, D), F32), ((HALF, D), F32), ((SAMPLE, D), F32)],
        [],
        rows,
        first,
        row_query,
        row_local,
        column,
        far=(1, 2),
    )
    states = exchange(sent, "ctx")
    sent, outputs, prompt_outputs = run(
        output_kernel,
        [((HEAD_AXIS, 8, D), F32), BY_HEAD_WIDE, ((HEADS, PT, D), F32)],
        [],
        states,
        query,
        weights,
        value,
        grad,
        growth,
        scale,
        prompt_upstream,
        flops=2 * work,
        kept=(1, 2),
    )
    sums = exchange(sent, "head")
    sent, out_grad = run(
        grad_kernel,
        [((CTX, 72, D), F32), BY_HEAD],
        [],
        sums,
        outputs,
        prompt_outputs,
        query,
        grad,
        growth,
        scale,
        prompt_upstream,
        flops=2 * work,
        far=(1,),
    )
    backs = exchange(sent, "ctx")
    reply_query_grad, key_local, value_local, to_end, factors = run(
        reply_back_kernel,
        [REPLY, BY_HEAD_WIDE, BY_HEAD_WIDE, ((T, D), F32), ((2 * SAMPLE, D), F32)],
        [REPLY_ROWS],
        states,
        out_grad,
        query,
        key,
        value,
        weights,
        reply_decay,
        totals,
        flops=6 * work,
        kept=(1, 2, 3, 4),
    )
    (sent,) = run(
        back_fold_kernel, [((SAMPLE, HALF, D), F32)], [], backs, blocks, factors, row_query, column
    )
    rows = exchange(sent, "sample")
    message, swap = run(
        prompt_mid_kernel,
        [((CTX, 96, D), F32), ((CTX, 8, D), F32)],
        [],
        backs,
        blocks,
        start,
        row_query,
        row_key,
        row_value,
        column,
        line,
        flops=work,
    )
    (sent,) = run(
        prompt_back_kernel,
        [((CTX, 96, D), F32)],
        [pltpu.VMEM((CTX, 32, D), F32), pltpu.SemaphoreType.DMA((2,))],
        rows,
        swap_cores(swap),
        row_key,
        row_value,
        column,
        message,
        hbm=(5,),
        hbm_outs=(0,),
        aliases={5: 0},
    )
    received = exchange(sent, "ctx")
    reply_key_grad, reply_value_grad, prompt_query_grad, prompt_key_grad, prompt_value_grad = run(
        end_kernel,
        [REPLY, REPLY, PROMPT, PROMPT, PROMPT],
        [REPLY_ROWS] * 2 + [PROMPT_ROWS] * 3,
        received,
        key,
        value,
        key_local,
        value_local,
        to_end,
        flops=4 * work,
    )
    return (
        prompt_query_grad,
        prompt_key_grad,
        prompt_value_grad,
        reply_query_grad,
        reply_key_grad,
        reply_value_grad,
    )


def solution(mesh):
    prompt = P(("sample", "ctx"), "head", None)
    reply = P("sample", "ctx", "head", None)
    in_specs = (
        (prompt,) * 4
        + (P("head", ("sample", "ctx")),)
        + (reply,) * 4
        + (P("sample", "head", "ctx"), P("sample"), P("head", None))
    )
    out_specs = (prompt,) * 3 + (reply,) * 3
    return jax.shard_map(shards, mesh=mesh, in_specs=in_specs, out_specs=out_specs, check_vma=False)
```

time: 173 us -> 165 us (0.954)
  local copies, waits for them, and re-layouts: 18.7 us -> 4.44 us
  blocking collectives: 65.1 us -> 69.1 us
  Pallas kernels: 13 us -> 16 us
    unnamed x56 -> x30, local copies, waits for them, and re-layouts: 18.7 us -> 4.44 us
    all_to_all x3, blocking collectives: 65.1 us -> 69.1 us  [exchange(): return lax.all_to_all(x, axis, 0, 0, tiled=True)]
    pallas_call x12, Pallas kernels: 13 us -> 16 us  [run(): pl.pallas_call(kernel, out_shape=[pltpu.VMEM(shape, kind) if i in kept el...]
where the time goes in v3:
time: 165 us; the launch traced here: 164 us
  blocking collectives  69.1 us (42%)
  waiting for transfers between devices  48.5 us (29%)
  starting transfers between devices  24.8 us (15%)
  Pallas kernels  16 us (10%)
  local copies, waits for them, and re-layouts  4.44 us (3%)
    all_to_all x3, blocking collectives, exchange(): return lax.all_to_all(x, axis, 0, 0, tiled=True)  69.1 us
    all_to_all x4, waiting for transfers between devices, exchange(): return lax.all_to_all(x, axis, 0, 0, tiled=True)  46 us
    all_to_all x4, starting transfers between devices, exchange(): return lax.all_to_all(x, axis, 0, 0, tiled=True)  21 us
    pallas_call x12, Pallas kernels, run(): pl.pallas_call(kernel, out_shape=[pltpu.VMEM(shape, kind) if i in kept el...  16 us
    unnamed x30, local copies, waits for them, and re-layouts  4.44 us
    ppermute x2, starting transfers between devices, swap_cores(): return lax.ppermute(x, 'ctx', [(i, i ^ 1) for i in range(CTX)])  3.82 us
  transfers between devices with their start and end apart: 6, of which 6 were waited for; matrix products, arithmetic and copies ran while one was open for 0% of the time, Pallas kernels for 3%

profile of v3, /device:TPU:1, one launch (start us, length us, event | category | flops | bytes accessed | tf_op | source)
XLA Modules:
  0.0 164.2 jit_solution(6871976682968683262)
XLA Ops:
  1.3 1.8 %send_kernel.1 = (f32[16,104,128]{2,1,0:T(8,128)S(1)}, bf16[8,128,128]{2,1,0:T(8,128)(2,1)S(1)}, bf16[8,128,128]{2,1,0:T(8,128)(2,1)S(1)}) custom-call(s32[1]{0:T(128)S(6)} %copy.20.lengths, bf16[1,128,8,128]{3,2,1,0:T(8,128)(2,1)} %key.1, bf16[1,128,8,128]{3,2,1,0:T(8,128)(2,1)} %value.1, f32[1,8,128]{2,1,0:T(8,128)} %decay.5, ...), custom_call_target="tpu_custom_call" | custom-call | flops 67108864 | bytes 1254408 | tf_op jit(solution)/shard_map/send_kernel/pallas_call | solution.py:446
  3.0 33.8 %all_to_all.35.received = f32[16,104,128]{2,1,0:T(8,128)S(1)} all-to-all(f32[16,104,128]{2,1,0:T(8,128)S(1)} %get-tuple-element.44), channel_id=1, replica_groups=mesh['sample'=8,'ctx'=16,'head'=4] {'ctx'}, dimensions={0} | all-to-all | bytes 1703936 | tf_op jit(solution)/shard_map/all_to_all | solution.py:467
  36.9 1.2 prompt_row_kernel.1
  38.1 9.0 %all-to-all-start.1 = ((f32[8,72,128]{2,1,0:T(8,128)}), f32[8,72,128]{2,1,0:T(8,128)S(1)}, u32[]{:S(2)}, u32[]{:S(2)}) async-start(f32[8,72,128]{2,1,0:T(8,128)} %get-tuple-element.45), calls=%async_computation.1 | async-start | bytes 589824 | tf_op jit(solution)/shard_map/all_to_all | solution.py:467
  47.1 1.9 %collective-permute-start = (f32[16,8,128]{2,1,0:T(8,128)S(1)}, f32[16,8,128]{2,1,0:T(8,128)S(1)}, u32[]{:S(2)}, u32[]{:S(2)}) collective-permute-start(f32[16,8,128]{2,1,0:T(8,128)S(1)} %get-tuple-element.46), channel_id=1, source_target_pairs={{0,4},{4,0},{8,12},{12,8},{16,20},{20,16},{24,28},{28,24},{32,36},... | collective-permute-start | bytes 196616 | tf_op jit(solution)/shard_map/ppermute | solution.py:471
  49.0 1.2 collective-permute-done.other
  50.2 0.4 prompt_local_kernel.1
  50.6 0.0 copy-start.2
  50.6 0.6 copy-done.2
  51.3 0.0 copy-start.9
  51.3 8.9 %all-to-all-done.1.rows_received = f32[8,72,128]{2,1,0:T(8,128)S(1)} async-done(((f32[8,72,128]{2,1,0:T(8,128)}), f32[8,72,128]{2,1,0:T(8,128)S(1)}, u32[]{:S(2)}, u32[]{:S(2)}) %all-to-all-start.1) | async-done | bytes 294944 | tf_op jit(solution)/shard_map/all_to_all | solution.py:467
  60.2 1.1 fold_kernel.1
  61.3 0.0 copy-done.9
  61.3 0.0 copy-start.6
  61.3 0.0 copy-start.14
  61.3 3.9 %all-to-all-start.2 = ((f32[16,72,128]{2,1,0:T(8,128)}), f32[16,72,128]{2,1,0:T(8,128)S(1)}, u32[]{:S(2)}, u32[]{:S(2)}) async-start(f32[16,72,128]{2,1,0:T(8,128)} %get-tuple-element.50), calls=%async_computation.2 | async-start | bytes 1179648 | tf_op jit(solution)/shard_map/all_to_all | solution.py:467
  65.3 0.0 copy-done.6
  65.3 0.0 copy-done.7
  65.3 0.0 copy-done.14
  65.3 1.5 reply_local_kernel.1
  66.8 17.1 %all-to-all-done.2.received = f32[16,72,128]{2,1,0:T(8,128)S(1)} async-done(((f32[16,72,128]{2,1,0:T(8,128)}), f32[16,72,128]{2,1,0:T(8,128)S(1)}, u32[]{:S(2)}, u32[]{:S(2)}) %all-to-all-start.2) | async-done | bytes 589856 | tf_op jit(solution)/shard_map/all_to_all | solution.py:467
  83.9 0.6 output_kernel.1
  84.5 8.0 %all_to_all.36.sums = f32[4,8,128]{2,1,0:T(8,128)S(1)} all-to-all(f32[4,8,128]{2,1,0:T(8,128)S(1)} %get-tuple-element.59), channel_id=1, replica_groups=mesh['sample'=8,'ctx'=16,'head'=4] {'head'}, dimensions={0} | all-to-all | bytes 32768 | tf_op jit(solution)/shard_map/all_to_all | solution.py:467
  92.6 1.5 grad_kernel.1
  94.0 4.6 %all-to-all-start.4 = ((f32[16,72,128]{2,1,0:T(8,128)}), f32[16,72,128]{2,1,0:T(8,128)S(1)}, u32[]{:S(2)}, u32[]{:S(2)}) async-start(f32[16,72,128]{2,1,0:T(8,128)} %get-tuple-element.62), calls=%async_computation.4 | async-start | bytes 1179648 | tf_op jit(solution)/shard_map/all_to_all | solution.py:467
  98.6 0.0 copy-done.13
  98.6 0.0 copy-start.1
  98.6 0.9 copy-done.1
  99.6 2.6 %reply_back_kernel.1 = (bf16[1,128,8,128]{3,2,1,0:T(8,128)(2,1)}, f32[8,128,128]{2,1,0:T(8,128)S(1)}, f32[8,128,128]{2,1,0:T(8,128)S(1)}, f32[128,128]{1,0:T(8,128)S(1)}, f32[16,128]{1,0:T(8,128)S(1)}) custom-call(f32[16,72,128]{2,1,0:T(8,128)S(1)} %all-to-all-done.2.received, bf16[8,128,128]{2,1,0:T(8,128)(2,1)S(1)} %copy-done.1, ...), custom_call_target="tpu_custom_call" | custom-call | flops 201326592 | bytes 3817472 | tf_op jit(solution)/shard_map/reply_back_kernel/pallas_call | solution.py:446
  102.2 0.6 copy-done.4
  102.9 0.6 copy-done.11
  103.5 13.8 %all-to-all-done.4.received = f32[16,72,128]{2,1,0:T(8,128)S(1)} async-done(((f32[16,72,128]{2,1,0:T(8,128)}), f32[16,72,128]{2,1,0:T(8,128)S(1)}, u32[]{:S(2)}, u32[]{:S(2)}) %all-to-all-start.4) | async-done | bytes 589856 | tf_op jit(solution)/shard_map/all_to_all | solution.py:467
  117.3 0.7 copy-done.12
  118.0 1.0 back_fold_kernel.1
  119.0 3.5 %all-to-all-start.5 = ((f32[8,64,128]{2,1,0:T(8,128)}), f32[8,64,128]{2,1,0:T(8,128)S(1)}, u32[]{:S(2)}, u32[]{:S(2)}) async-start(f32[8,64,128]{2,1,0:T(8,128)} %back_fold_kernel.1), calls=%async_computation.5 | async-start | bytes 524288 | tf_op jit(solution)/shard_map/all_to_all | solution.py:467
  122.5 0.0 copy-done.3
  122.5 0.0 copy-done.8
  122.5 0.0 copy-done.10
  122.6 0.9 prompt_mid_kernel.1
  123.5 0.9 copy-done
  124.4 1.9 %collective-permute-start.1 = (f32[16,8,128]{2,1,0:T(8,128)S(1)}, f32[16,8,128]{2,1,0:T(8,128)S(1)}, u32[]{:S(2)}, u32[]{:S(2)}) collective-permute-start(f32[16,8,128]{2,1,0:T(8,128)S(1)} %get-tuple-element.71), channel_id=1, source_target_pairs={{0,4},{4,0},{8,12},{12,8},{16,20},{20,16},{24,28},{28,24},{32,36},... | collective-permute-start | bytes 196616 | tf_op jit(solution)/shard_map/ppermute | solution.py:471
  126.3 1.2 collective-permute-done.1.swapped
  127.5 6.1 %all-to-all-done.5.rows_received = f32[8,64,128]{2,1,0:T(8,128)S(1)} async-done(((f32[8,64,128]{2,1,0:T(8,128)}), f32[8,64,128]{2,1,0:T(8,128)S(1)}, u32[]{:S(2)}, u32[]{:S(2)}) %all-to-all-start.5) | async-done | bytes 262176 | tf_op jit(solution)/shard_map/all_to_all | solution.py:467
  133.7 1.8 %prompt_back_kernel.1 = f32[16,96,128]{2,1,0:T(8,128)} custom-call(f32[8,64,128]{2,1,0:T(8,128)S(1)} %all-to-all-done.5.rows_received, f32[16,8,128]{2,1,0:T(8,128)S(1)} %collective-permute-done.1.swapped, bf16[256,128]{1,0:T(8,128)(2,1)S(1)} %get-tuple-element.68.key, bf16[256,64]{1,0:T(8,128)(2,1)S(1)} %copy-done.3, ...), custom_call_target="tpu_custom_call", output_to_operand_aliasing={{}: (5, {})} | custom-call | bytes 2686976 | tf_op jit(solution)/shard_map/prompt_back_kernel/pallas_call | solution.py:446
  135.5 0.0 copy-start.5
  135.5 27.2 %all_to_all.37.received = f32[16,96,128]{2,1,0:T(8,128)S(1)} all-to-all(f32[16,96,128]{2,1,0:T(8,128)} %prompt_back_kernel.1), channel_id=1, replica_groups=mesh['sample'=8,'ctx'=16,'head'=4] {'ctx'}, dimensions={0} | all-to-all | bytes 1572864 | tf_op jit(solution)/shard_map/all_to_all | solution.py:467
  162.8 0.0 copy-done.5
  162.8 1.5 end_kernel.1
  (9 shorter events, 0.0 us)
Async XLA Ops:
  38.1 22.1 %all-to-all-start.1 = ((f32[8,72,128]{2,1,0:T(8,128)}), f32[8,72,128]{2,1,0:T(8,128)S(1)}, u32[]{:S(2)}, u32[]{:S(2)}) async-start(f32[8,72,128]{2,1,0:T(8,128)} %get-tuple-element.45), calls=%async_computation.1 | async-start | bytes 589824 | tf_op jit(solution)/shard_map/all_to_all | solution.py:467
  47.1 3.1 %collective-permute-start = (f32[16,8,128]{2,1,0:T(8,128)S(1)}, f32[16,8,128]{2,1,0:T(8,128)S(1)}, u32[]{:S(2)}, u32[]{:S(2)}) collective-permute-start(f32[16,8,128]{2,1,0:T(8,128)S(1)} %get-tuple-element.46), channel_id=1, source_target_pairs={{0,4},{4,0},{8,12},{12,8},{16,20},{20,16},{24,28},{28,24},{32,36},... | collective-permute-start | bytes 196616 | tf_op jit(solution)/shard_map/ppermute | solution.py:471
  50.6 0.6 copy-start.2
  51.3 10.1 %copy-start.9 = (f32[8,256]{1,0:T(8,128)}, f32[8,256]{1,0:T(8,128)S(1)}, u32[]{:S(2)}) copy-start(f32[8,256]{1,0:T(8,128)S(1)} %get-tuple-element.70.line) | copy-start | bytes 24580
  61.3 3.9 %copy-start.6 = (f32[1,8,128]{2,1,0:T(8,128)S(1)}, f32[1,8,128]{2,1,0:T(8,128)}, u32[]{:S(2)}) copy-start(f32[1,8,128]{2,1,0:T(8,128)} %decay.5) | copy-start | bytes 12292
  61.3 3.9 %copy-start.7 = (bf16[16,8,128]{2,1,0:T(8,128)(2,1)S(1)}, bf16[16,8,128]{2,1,0:T(8,128)(2,1)}, u32[]{:S(2)}) copy-start(bf16[16,8,128]{2,1,0:T(8,128)(2,1)} %prompt_grad.1) | copy-start | bytes 98308
  61.3 3.9 %copy-start.14 = (bf16[8,128]{1,0:T(8,128)(2,1)S(1)}, bf16[8,128]{1,0:T(8,128)(2,1)}, u32[]{:S(2)}) copy-start(bf16[8,128]{1,0:T(8,128)(2,1)} %gain.1) | copy-start | bytes 6148
  61.3 22.6 %all-to-all-start.2 = ((f32[16,72,128]{2,1,0:T(8,128)}), f32[16,72,128]{2,1,0:T(8,128)S(1)}, u32[]{:S(2)}, u32[]{:S(2)}) async-start(f32[16,72,128]{2,1,0:T(8,128)} %get-tuple-element.50), calls=%async_computation.2 | async-start | bytes 1179648 | tf_op jit(solution)/shard_map/all_to_all | solution.py:467
  94.0 4.6 %copy-start.13 = (f32[8,128]{1,0:T(8,128)S(1)}, f32[8,128]{1,0:T(8,128)}, u32[]{:S(2)}) copy-start(f32[8,128]{1,0:T(8,128)} %get-tuple-element.65.totals) | copy-start | bytes 12292
  94.0 23.3 %all-to-all-start.4 = ((f32[16,72,128]{2,1,0:T(8,128)}), f32[16,72,128]{2,1,0:T(8,128)S(1)}, u32[]{:S(2)}, u32[]{:S(2)}) async-start(f32[16,72,128]{2,1,0:T(8,128)} %get-tuple-element.62), calls=%async_computation.4 | async-start | bytes 1179648 | tf_op jit(solution)/shard_map/all_to_all | solution.py:467
  98.6 1.0 copy-start.1
  102.2 0.6 copy-start.4
  102.9 0.6 copy-start.11
  117.3 0.7 copy-start.12
  119.0 3.6 %copy-start.3 = (bf16[256,64]{1,0:T(8,128)(2,1)S(1)}, bf16[256,64]{1,0:T(8,128)(2,1)}, u32[]{:S(2)}) copy-start(bf16[256,64]{1,0:T(8,128)(2,1)} %copy-done.2) | copy-start | bytes 98308
  119.0 3.6 %copy-start.8 = (f32[64,128]{1,0:T(8,128)S(1)}, f32[64,128]{1,0:T(8,128)}, u32[]{:S(2)}) copy-start(f32[64,128]{1,0:T(8,128)} %get-tuple-element.67.start) | copy-start | bytes 98308
  119.0 3.6 %copy-start.10 = (f32[8,256]{1,0:T(8,128)S(1)}, f32[8,256]{1,0:T(8,128)}, u32[]{:S(2)}) copy-start(f32[8,256]{1,0:T(8,128)} %copy-done.9) | copy-start | bytes 24580
  119.0 14.7 %all-to-all-start.5 = ((f32[8,64,128]{2,1,0:T(8,128)}), f32[8,64,128]{2,1,0:T(8,128)S(1)}, u32[]{:S(2)}, u32[]{:S(2)}) async-start(f32[8,64,128]{2,1,0:T(8,128)} %back_fold_kernel.1), calls=%async_computation.5 | async-start | bytes 524288 | tf_op jit(solution)/shard_map/all_to_all | solution.py:467
  123.5 0.9 copy-start
  124.4 3.1 %collective-permute-start.1 = (f32[16,8,128]{2,1,0:T(8,128)S(1)}, f32[16,8,128]{2,1,0:T(8,128)S(1)}, u32[]{:S(2)}, u32[]{:S(2)}) collective-permute-start(f32[16,8,128]{2,1,0:T(8,128)S(1)} %get-tuple-element.71), channel_id=1, source_target_pairs={{0,4},{4,0},{8,12},{12,8},{16,20},{20,16},{24,28},{28,24},{32,36},... | collective-permute-start | bytes 196616 | tf_op jit(solution)/shard_map/ppermute | solution.py:471
  135.5 27.2 %copy-start.5 = (f32[128,128]{1,0:T(8,128)S(1)}, f32[128,128]{1,0:T(8,128)}, u32[]{:S(2)}) copy-start(f32[128,128]{1,0:T(8,128)} %copy-done.4) | copy-start | bytes 196612

commit v4 on v3

--- a/solution.py
+++ b/solution.py
@@ -253,15 +253,15 @@
     local_out[...] = sum(dot(part, v, 1, 0) for part in weights)
 
 
-def fold_kernel(rows_received, received, query, local, column, out, start_out, total_out):
+def fold_kernel(rows_received, received, query, local, column, after_reply, out, start_out, factors_out):
+    del after_reply
     place = lax.axis_index("sample")
+    totals = [rows_received[s, 64:65, :] for s in range(SAMPLE)]
     end = jnp.zeros((HALF, D), F32)
     start = end
     for s in range(SAMPLE):
         start = jnp.where(place == s, end, start)
-        total = rows_received[s, 64:65, :]
-        total_out[s : s + 1, :] = total
-        end = jnp.exp(total) * end + rows_received[s, 0:64, :]
+        end = jnp.exp(totals[s]) * end + rows_received[s, 0:64, :]
     start_out[...] = start
     state = end
     for b in range(CTX):
@@ -269,6 +269,14 @@
         state = jnp.exp(received[b, 89:90, :]) * state + received[b, 0:64, :]
     outputs = local[...] + jnp.exp(column[:, 0:1]) * dot_right(query[...], start, 1, 1)
     out[:, 64:72, :] = packed_half(outputs)
+    for s in range(SAMPLE):
+        after = jnp.zeros((1, D), F32)
+        between = after
+        for other in range(s + 1, SAMPLE):
+            after = after + totals[other]
+            between = between + jnp.where(other < place, totals[other], 0.0)
+        factors_out[s : s + 1, :] = jnp.exp(after)
+        factors_out[SAMPLE + s : SAMPLE + s + 1, :] = jnp.where(place > s, jnp.exp(between), 0.0)
 
 
 def output_kernel(
@@ -325,22 +333,14 @@
 
 
 def reply_back_kernel(
-    received, out_grad, query, key, value, weights, decay, totals,
-    query_grad, key_local, value_local, to_end_out, factors_out, rows,
-):
+    received, out_grad, query, key, value, weights, decay, after_fold,
+    query_grad, key_local, value_local, to_end_out, rows,
+):
+    del after_fold
     lines = running_rows(decay[0])
     columns = running_columns(decay[0])
     scales = jnp.exp(columns)
     to_end_out[...] = wide_columns(jnp.exp(columns[T - 1 : T, :] - columns))
-    place = lax.axis_index("sample")
-    for s in range(SAMPLE):
-        after = jnp.zeros((1, D), F32)
-        between = after
-        for other in range(s + 1, SAMPLE):
-            after = after + totals[other : other + 1, :]
-            between = between + jnp.where(other < place, totals[other : other + 1, :], 0.0)
-        factors_out[s : s + 1, :] = jnp.exp(after)
-        factors_out[SAMPLE + s : SAMPLE + s + 1, :] = jnp.where(place > s, jnp.exp(between), 0.0)
     for h in range(HEADS):
         state = jnp.concatenate([received[2 * h, 0:64, :], received[2 * h + 1, 0:64, :]], axis=0)
         og = out_grad[h]
@@ -352,7 +352,7 @@
     query_grad[0] = rows[...].reshape(T, HEADS, D).astype(BF16)
 
 
-def back_fold_kernel(received, blocks, factors, query, column, rows_out):
+def back_fold_kernel(received, blocks, factors, query, column, rows_out, ready_out):
     adjoint = jnp.zeros((HALF, D), F32)
     for b in range(CTX - 1, -1, -1):
         adjoint = jnp.exp(blocks[b : b + 1, :]) * adjoint + received[b, 0:64, :]
@@ -360,6 +360,7 @@
     back = dot_right(og, query[...].astype(F32) * jnp.exp(column[:, 0:1]), 0, 0)
     for s in range(SAMPLE):
         rows_out[s] = factors[s : s + 1, :] * adjoint + factors[SAMPLE + s : SAMPLE + s + 1, :] * back
+    ready_out[...] = adjoint[0:8]
 
 
 def prompt_mid_kernel(received, blocks, start, query, key, value, column, line, out, swap_out):
@@ -383,9 +384,8 @@
     out[:, 88:96, :] = jnp.where(second, query_grad[:, 8:16], query_grad[:, 0:8])
 
 
-def prompt_back_kernel(rows_received, swapped, key, value, column, message, out, part, sems):
-    arrive = pltpu.make_async_copy(message.at[:, 64:96, :], part, sems.at[0])
-    arrive.start()
+def prompt_back_kernel(rows_received, swapped, key, value, column, message, after_reply, out):
+    del after_reply
     adjoint = rows_received[0]
     for s in range(1, SAMPLE):
         adjoint = adjoint + rows_received[s]
@@ -393,13 +393,10 @@
     to_end = jnp.exp(running[ROW - 1 : ROW] - running)
     key_grad = to_end * dot_right(value[...], adjoint, 1, 0)
     value_grad = to_end * dot_right(key[...], adjoint, 1, 1)
-    arrive.wait()
-    part[:, 0:16, :] += key_grad.reshape(CTX, PT, D)
-    part[:, 16:24, :] += packed_half(value_grad)
-    part[:, 24:32, :] += swapped[...]
-    leave = pltpu.make_async_copy(part, out.at[:, 64:96, :], sems.at[1])
-    leave.start()
-    leave.wait()
+    out[:, 0:64, :] = message[:, 0:64, :]
+    out[:, 64:80, :] = message[:, 64:80, :] + key_grad.reshape(CTX, PT, D)
+    out[:, 80:88, :] = message[:, 80:88, :] + packed_half(value_grad)
+    out[:, 88:96, :] = message[:, 88:96, :] + swapped[...]
 
 
 def end_kernel(
@@ -434,7 +431,7 @@
 PROMPT = ((PT, HEADS, D), BF16)
 
 
-def run(kernel, outs, scratch, *operands, hbm=(), hbm_outs=(), kept=(), far=(), aliases=None, flops=0):
+def run(kernel, outs, scratch, *operands, hbm=(), kept=(), flops=0):
     operands = [
         pltpu.with_memory_space_constraint(operand, pltpu.HBM) if i in hbm else operand
         for i, operand in enumerate(operands)
@@ -446,17 +443,12 @@
     return pl.pallas_call(
         kernel,
         out_shape=[
-            pltpu.VMEM(shape, kind)
-            if i in kept
-            else pltpu.HBM(shape, kind)
-            if i in far
-            else jax.ShapeDtypeStruct(shape, kind)
+            pltpu.VMEM(shape, kind) if i in kept else jax.ShapeDtypeStruct(shape, kind)
             for i, (shape, kind) in enumerate(outs)
         ],
         in_specs=specs,
-        out_specs=[HBM if i in hbm_outs else VMEM for i in range(len(outs))],
+        out_specs=[VMEM] * len(outs),
         scratch_shapes=scratch,
-        input_output_aliases=aliases or {},
         compiler_params=pltpu.CompilerParams(vmem_limit_bytes=8 * 1024 * 1024),
         cost_estimate=pl.CostEstimate(flops=flops, bytes_accessed=2 * moved, transcendentals=0),
         name=kernel.__name__,
@@ -548,16 +540,17 @@
         flops=work,
         kept=range(5),
     )
-    sent, start, totals = run(
+    sent, start, factors = run(
         fold_kernel,
-        [((CTX, 72, D), F32), ((HALF, D), F32), ((SAMPLE, D), F32)],
+        [((CTX, 72, D), F32), ((HALF, D), F32), ((2 * SAMPLE, D), F32)],
         [],
         rows,
         first,
         row_query,
         row_local,
         column,
-        far=(1, 2),
+        scale,
+        kept=(1, 2),
     )
     states = exchange(sent, "ctx")
     sent, outputs, prompt_outputs = run(
@@ -589,12 +582,24 @@
         scale,
         prompt_upstream,
         flops=2 * work,
-        far=(1,),
+        kept=(1,),
     )
     backs = exchange(sent, "ctx")
-    reply_query_grad, key_local, value_local, to_end, factors = run(
+    sent, ready = run(
+        back_fold_kernel,
+        [((SAMPLE, HALF, D), F32), ((8, D), F32)],
+        [],
+        backs,
+        blocks,
+        factors,
+        row_query,
+        column,
+        kept=(1,),
+    )
+    rows = exchange(sent, "sample")
+    reply_query_grad, key_local, value_local, to_end = run(
         reply_back_kernel,
-        [REPLY, BY_HEAD_WIDE, BY_HEAD_WIDE, ((T, D), F32), ((2 * SAMPLE, D), F32)],
+        [REPLY, BY_HEAD_WIDE, BY_HEAD_WIDE, ((T, D), F32)],
         [REPLY_ROWS],
         states,
         out_grad,
@@ -603,14 +608,10 @@
         value,
         weights,
         reply_decay,
-        totals,
+        ready,
         flops=6 * work,
-        kept=(1, 2, 3, 4),
-    )
-    (sent,) = run(
-        back_fold_kernel, [((SAMPLE, HALF, D), F32)], [], backs, blocks, factors, row_query, column
-    )
-    rows = exchange(sent, "sample")
+        kept=(1, 2, 3),
+    )
     message, swap = run(
         prompt_mid_kernel,
         [((CTX, 96, D), F32), ((CTX, 8, D), F32)],
@@ -624,20 +625,19 @@
         column,
         line,
         flops=work,
+        kept=(0,),
     )
     (sent,) = run(
         prompt_back_kernel,
         [((CTX, 96, D), F32)],
-        [pltpu.VMEM((CTX, 32, D), F32), pltpu.SemaphoreType.DMA((2,))],
+        [],
         rows,
         swap_cores(swap),
         row_key,
         row_value,
         column,
         message,
-        hbm=(5,),
-        hbm_outs=(0,),
-        aliases={5: 0},
+        to_end,
     )
     received = exchange(sent, "ctx")
     reply_key_grad, reply_value_grad, prompt_query_grad, prompt_key_grad, prompt_value_grad = run(

time: 165 us -> 161 us (0.976)
  blocking collectives: 69.1 us -> 113 us
  waiting for transfers between devices: 48.5 us -> 11.6 us
  starting transfers between devices: 24.8 us -> 16.4 us
  Pallas kernels: 16 us -> 12.8 us
    all_to_all x3 -> x5, blocking collectives: 69.1 us -> 113 us  [exchange(): return lax.all_to_all(x, axis, 0, 0, tiled=True)]
    all_to_all x4 -> x2, waiting for transfers between devices: 46 us -> 11.6 us  [exchange(): return lax.all_to_all(x, axis, 0, 0, tiled=True)]
    all_to_all x4 -> x2, starting transfers between devices: 21 us -> 12.5 us  [exchange(): return lax.all_to_all(x, axis, 0, 0, tiled=True)]
    pallas_call x12, Pallas kernels: 16 us -> 12.8 us  [run(): pl.pallas_call(kernel, out_shape=[pltpu.VMEM(shape, kind) if i in kept el...]
    ppermute x2, waiting for transfers between devices: 2.44 us -> 0.01 us  [swap_cores(): return lax.ppermute(x, 'ctx', [(i, i ^ 1) for i in range(CTX)])]
    unnamed x30 -> x32, local copies, waits for them, and re-layouts: 4.44 us -> 5.23 us
  transfers between devices with their start and end apart: 6 -> 4, of which waited for: 6 -> 2; matrix products, arithmetic and copies ran while one was open for 0% -> 0% of each run, Pallas kernels for 3% -> 3%
where the time goes in v4:
time: 161 us; the launch traced here: 160 us
  blocking collectives  113 us (70%)
  starting transfers between devices  16.4 us (10%)
  Pallas kernels  12.8 us (8%)
  waiting for transfers between devices  11.6 us (7%)
  local copies, waits for them, and re-layouts  5.23 us (3%)
    all_to_all x5, blocking collectives, exchange(): return lax.all_to_all(x, axis, 0, 0, tiled=True)  113 us
    pallas_call x12, Pallas kernels, run(): pl.pallas_call(kernel, out_shape=[pltpu.VMEM(shape, kind) if i in kept el...  12.8 us
    all_to_all x2, starting transfers between devices, exchange(): return lax.all_to_all(x, axis, 0, 0, tiled=True)  12.5 us
    all_to_all x2, waiting for transfers between devices, exchange(): return lax.all_to_all(x, axis, 0, 0, tiled=True)  11.6 us
    unnamed x32, local copies, waits for them, and re-layouts  5.23 us
    ppermute x2, starting transfers between devices, swap_cores(): return lax.ppermute(x, 'ctx', [(i, i ^ 1) for i in range(CTX)])  3.93 us
  transfers between devices with their start and end apart: 4, of which 2 were waited for; matrix products, arithmetic and copies ran while one was open for 0% of the time, Pallas kernels for 3%

profile of v4, /device:TPU:1, one launch (start us, length us, event | category | flops | bytes accessed | tf_op | source)
XLA Modules:
  0.0 160.4 jit_solution(14116724560142212329)
XLA Ops:
  1.3 1.8 %send_kernel.1 = (f32[16,104,128]{2,1,0:T(8,128)S(1)}, bf16[8,128,128]{2,1,0:T(8,128)(2,1)S(1)}, bf16[8,128,128]{2,1,0:T(8,128)(2,1)S(1)}) custom-call(s32[1]{0:T(128)S(6)} %copy.18.lengths, bf16[1,128,8,128]{3,2,1,0:T(8,128)(2,1)} %key.1, bf16[1,128,8,128]{3,2,1,0:T(8,128)(2,1)} %value.1, f32[1,8,128]{2,1,0:T(8,128)} %decay.5, ...), custom_call_target="tpu_custom_call" | custom-call | flops 67108864 | bytes 1254408 | tf_op jit(solution)/shard_map/send_kernel/pallas_call | solution.py:443
  3.0 33.8 %all_to_all.35.received = f32[16,104,128]{2,1,0:T(8,128)S(1)} all-to-all(f32[16,104,128]{2,1,0:T(8,128)S(1)} %get-tuple-element.45), channel_id=1, replica_groups=mesh['sample'=8,'ctx'=16,'head'=4] {'ctx'}, dimensions={0} | all-to-all | bytes 1703936 | tf_op jit(solution)/shard_map/all_to_all | solution.py:459
  36.9 1.2 prompt_row_kernel.1
  38.1 0.0 copy-start.9
  38.1 9.1 %all-to-all-start.1 = ((f32[8,72,128]{2,1,0:T(8,128)}), f32[8,72,128]{2,1,0:T(8,128)S(1)}, u32[]{:S(2)}, u32[]{:S(2)}) async-start(f32[8,72,128]{2,1,0:T(8,128)} %get-tuple-element.46), calls=%async_computation.1 | async-start | bytes 589824 | tf_op jit(solution)/shard_map/all_to_all | solution.py:459
  47.2 1.9 %collective-permute-start = (f32[16,8,128]{2,1,0:T(8,128)S(1)}, f32[16,8,128]{2,1,0:T(8,128)S(1)}, u32[]{:S(2)}, u32[]{:S(2)}) collective-permute-start(f32[16,8,128]{2,1,0:T(8,128)S(1)} %get-tuple-element.47), channel_id=1, source_target_pairs={{0,4},{4,0},{8,12},{12,8},{16,20},{20,16},{24,28},{28,24},{32,36},... | collective-permute-start | bytes 196616 | tf_op jit(solution)/shard_map/ppermute | solution.py:463
  49.1 0.0 copy-done.9
  49.1 0.0 copy-done.10
  49.2 0.0 copy-done.15
  49.2 1.5 reply_local_kernel.1
  50.7 0.0 collective-permute-done.other
  50.7 0.4 prompt_local_kernel.1
  51.1 0.0 copy-start.4
  51.1 0.6 copy-done.4
  51.7 8.6 %all-to-all-done.1.rows_received = f32[8,72,128]{2,1,0:T(8,128)S(1)} async-done(((f32[8,72,128]{2,1,0:T(8,128)}), f32[8,72,128]{2,1,0:T(8,128)S(1)}, u32[]{:S(2)}, u32[]{:S(2)}) %all-to-all-start.1) | async-done | bytes 294944 | tf_op jit(solution)/shard_map/all_to_all | solution.py:459
  60.3 0.3 fold_kernel.1
  60.6 0.0 copy-done.13
  60.7 0.0 copy-start.11
  60.7 21.9 %all_to_all.36.received = f32[16,72,128]{2,1,0:T(8,128)S(1)} all-to-all(f32[16,72,128]{2,1,0:T(8,128)S(1)} %get-tuple-element.53), channel_id=1, replica_groups=mesh['sample'=8,'ctx'=16,'head'=4] {'ctx'}, dimensions={0} | all-to-all | bytes 1179648 | tf_op jit(solution)/shard_map/all_to_all | solution.py:459
  82.6 0.0 copy-done.11
  82.6 0.6 output_kernel.1
  83.2 8.1 %all_to_all.37.sums = f32[4,8,128]{2,1,0:T(8,128)S(1)} all-to-all(f32[4,8,128]{2,1,0:T(8,128)S(1)} %get-tuple-element.60), channel_id=1, replica_groups=mesh['sample'=8,'ctx'=16,'head'=4] {'head'}, dimensions={0} | all-to-all | bytes 32768 | tf_op jit(solution)/shard_map/all_to_all | solution.py:459
  91.2 0.6 grad_kernel.1
  91.9 0.0 copy-start.2
  91.9 23.0 %all_to_all.38.received = f32[16,72,128]{2,1,0:T(8,128)S(1)} all-to-all(f32[16,72,128]{2,1,0:T(8,128)S(1)} %get-tuple-element.63), channel_id=1, replica_groups=mesh['sample'=8,'ctx'=16,'head'=4] {'ctx'}, dimensions={0} | all-to-all | bytes 1179648 | tf_op jit(solution)/shard_map/all_to_all | solution.py:459
  114.9 0.0 copy-done.2
  114.9 1.0 back_fold_kernel.1
  115.9 3.4 %all-to-all-start.5 = ((f32[8,64,128]{2,1,0:T(8,128)}), f32[8,64,128]{2,1,0:T(8,128)S(1)}, u32[]{:S(2)}, u32[]{:S(2)}) async-start(f32[8,64,128]{2,1,0:T(8,128)} %get-tuple-element.66), calls=%async_computation.5 | async-start | bytes 524288 | tf_op jit(solution)/shard_map/all_to_all | solution.py:459
  119.3 0.0 copy-start.5
  119.3 0.8 copy-done.5
  120.1 0.8 copy-done.12
  120.9 0.7 copy-done.14
  121.6 0.9 prompt_mid_kernel.1
  122.5 2.0 %collective-permute-start.1 = (f32[16,8,128]{2,1,0:T(8,128)S(1)}, f32[16,8,128]{2,1,0:T(8,128)S(1)}, u32[]{:S(2)}, u32[]{:S(2)}) collective-permute-start(f32[16,8,128]{2,1,0:T(8,128)S(1)} %get-tuple-element.71), channel_id=1, source_target_pairs={{0,4},{4,0},{8,12},{12,8},{16,20},{20,16},{24,28},{28,24},{32,36},... | collective-permute-start | bytes 196616 | tf_op jit(solution)/shard_map/ppermute | solution.py:463
  124.5 0.0 copy-done.3
  124.5 0.0 copy-start.6
  124.5 2.6 %reply_back_kernel.1 = (bf16[1,128,8,128]{3,2,1,0:T(8,128)(2,1)}, f32[8,128,128]{2,1,0:T(8,128)S(1)}, f32[8,128,128]{2,1,0:T(8,128)S(1)}, f32[128,128]{1,0:T(8,128)S(1)}) custom-call(f32[16,72,128]{2,1,0:T(8,128)S(1)} %all_to_all.36.received, bf16[8,128,128]{2,1,0:T(8,128)(2,1)S(1)} %copy-done.3, bf16[8,128,128]{2,1,0:T(8,128)(2,1)S(1)} %get-tuple-element.54.query, ...), custom_call_target="tpu_custom_call" | custom-call | flops 201326592 | bytes 3817472 | tf_op jit(solution)/shard_map/reply_back_kernel/pallas_call | solution.py:443
  127.2 0.8 copy-done
  128.0 0.0 collective-permute-done.1.swapped
  128.0 0.6 copy-done.7
  128.6 3.0 %all-to-all-done.5.rows_received = f32[8,64,128]{2,1,0:T(8,128)S(1)} async-done(((f32[8,64,128]{2,1,0:T(8,128)}), f32[8,64,128]{2,1,0:T(8,128)S(1)}, u32[]{:S(2)}, u32[]{:S(2)}) %all-to-all-start.5) | async-done | bytes 262176 | tf_op jit(solution)/shard_map/all_to_all | solution.py:459
  131.6 0.0 copy-done.6
  131.6 0.8 copy-done.8
  132.4 0.3 prompt_back_kernel.1
  132.7 0.0 copy-start.1
  132.7 26.2 %all_to_all.39.received = f32[16,96,128]{2,1,0:T(8,128)S(1)} all-to-all(f32[16,96,128]{2,1,0:T(8,128)S(1)} %prompt_back_kernel.1), channel_id=1, replica_groups=mesh['sample'=8,'ctx'=16,'head'=4] {'ctx'}, dimensions={0} | all-to-all | bytes 1572864 | tf_op jit(solution)/shard_map/all_to_all | solution.py:459
  158.9 0.0 copy-done.1
  158.9 1.5 end_kernel.1
  (9 shorter events, 0.0 us)
Async XLA Ops:
  38.1 11.0 %copy-start.9 = (f32[1,8,128]{2,1,0:T(8,128)S(1)}, f32[1,8,128]{2,1,0:T(8,128)}, u32[]{:S(2)}) copy-start(f32[1,8,128]{2,1,0:T(8,128)} %decay.5) | copy-start | bytes 12292
  38.1 11.0 %copy-start.10 = (bf16[16,8,128]{2,1,0:T(8,128)(2,1)S(1)}, bf16[16,8,128]{2,1,0:T(8,128)(2,1)}, u32[]{:S(2)}) copy-start(bf16[16,8,128]{2,1,0:T(8,128)(2,1)} %prompt_grad.1) | copy-start | bytes 98308
  38.1 22.2 %all-to-all-start.1 = ((f32[8,72,128]{2,1,0:T(8,128)}), f32[8,72,128]{2,1,0:T(8,128)S(1)}, u32[]{:S(2)}, u32[]{:S(2)}) async-start(f32[8,72,128]{2,1,0:T(8,128)} %get-tuple-element.46), calls=%async_computation.1 | async-start | bytes 589824 | tf_op jit(solution)/shard_map/all_to_all | solution.py:459
  47.2 2.0 %copy-start.15 = (bf16[8,128]{1,0:T(8,128)(2,1)S(1)}, bf16[8,128]{1,0:T(8,128)(2,1)}, u32[]{:S(2)}) copy-start(bf16[8,128]{1,0:T(8,128)(2,1)} %gain.1) | copy-start | bytes 6148
  47.2 3.5 %collective-permute-start = (f32[16,8,128]{2,1,0:T(8,128)S(1)}, f32[16,8,128]{2,1,0:T(8,128)S(1)}, u32[]{:S(2)}, u32[]{:S(2)}) collective-permute-start(f32[16,8,128]{2,1,0:T(8,128)S(1)} %get-tuple-element.47), channel_id=1, source_target_pairs={{0,4},{4,0},{8,12},{12,8},{16,20},{20,16},{24,28},{28,24},{32,36},... | collective-permute-start | bytes 196616 | tf_op jit(solution)/shard_map/ppermute | solution.py:463
  51.1 0.6 copy-start.4
  51.7 8.9 %copy-start.13 = (f32[8,256]{1,0:T(8,128)}, f32[8,256]{1,0:T(8,128)S(1)}, u32[]{:S(2)}) copy-start(f32[8,256]{1,0:T(8,128)S(1)} %get-tuple-element.70.line) | copy-start | bytes 24580
  60.7 21.9 %copy-start.11 = (f32[64,128]{1,0:T(8,128)}, f32[64,128]{1,0:T(8,128)S(1)}, u32[]{:S(2)}) copy-start(f32[64,128]{1,0:T(8,128)S(1)} %get-tuple-element.67.start) | copy-start | bytes 98308
  91.9 23.0 %copy-start.2 = (bf16[8,128,128]{2,1,0:T(8,128)(2,1)}, bf16[8,128,128]{2,1,0:T(8,128)(2,1)S(1)}, u32[]{:S(2)}) copy-start(bf16[8,128,128]{2,1,0:T(8,128)(2,1)S(1)} %get-tuple-element.73.out_grad) | copy-start | bytes 786436
  115.9 15.7 %all-to-all-start.5 = ((f32[8,64,128]{2,1,0:T(8,128)}), f32[8,64,128]{2,1,0:T(8,128)S(1)}, u32[]{:S(2)}, u32[]{:S(2)}) async-start(f32[8,64,128]{2,1,0:T(8,128)} %get-tuple-element.66), calls=%async_computation.5 | async-start | bytes 524288 | tf_op jit(solution)/shard_map/all_to_all | solution.py:459
  119.3 0.8 copy-start.5
  120.1 0.8 copy-start.12
  120.9 0.7 copy-start.14
  121.6 3.0 %copy-start.3 = (bf16[8,128,128]{2,1,0:T(8,128)(2,1)S(1)}, bf16[8,128,128]{2,1,0:T(8,128)(2,1)}, u32[]{:S(2)}) copy-start(bf16[8,128,128]{2,1,0:T(8,128)(2,1)} %copy-done.2) | copy-start | bytes 786436
  122.5 5.5 %collective-permute-start.1 = (f32[16,8,128]{2,1,0:T(8,128)S(1)}, f32[16,8,128]{2,1,0:T(8,128)S(1)}, u32[]{:S(2)}, u32[]{:S(2)}) collective-permute-start(f32[16,8,128]{2,1,0:T(8,128)S(1)} %get-tuple-element.71), channel_id=1, source_target_pairs={{0,4},{4,0},{8,12},{12,8},{16,20},{20,16},{24,28},{28,24},{32,36},... | collective-permute-start | bytes 196616 | tf_op jit(solution)/shard_map/ppermute | solution.py:463
  124.5 7.1 %copy-start.6 = (bf16[256,64]{1,0:T(8,128)(2,1)S(1)}, bf16[256,64]{1,0:T(8,128)(2,1)}, u32[]{:S(2)}) copy-start(bf16[256,64]{1,0:T(8,128)(2,1)} %copy-done.4) | copy-start | bytes 98308
  127.2 0.8 copy-start
  128.0 0.6 copy-start.7
  131.6 0.8 copy-start.8
  132.7 26.2 %copy-start.1 = (f32[8,128,128]{2,1,0:T(8,128)S(1)}, f32[8,128,128]{2,1,0:T(8,128)}, u32[]{:S(2)}) copy-start(f32[8,128,128]{2,1,0:T(8,128)} %copy-done) | copy-start | bytes 1572868

commit v5 on v4

--- a/solution.py
+++ b/solution.py
@@ -14,6 +14,7 @@
 T = 128
 PT = 16
 CTX = 16
+CHIPS = 8
 SAMPLE = 8
 HEAD_AXIS = 4
 ROW = CTX * PT
@@ -107,6 +108,19 @@
     return lax.axis_index("ctx") * T + iota((T, 1), 0) < lengths[0]
 
 
+def second_core():
+    return lax.axis_index("ctx") % 2 == 1
+
+
+def in_order(mine, other):
+    second = second_core()
+    return jnp.where(second, other, mine), jnp.where(second, mine, other)
+
+
+def choose(first, last):
+    return in_order(first, last)
+
+
 def start_copies(pairs, sems):
     copies = [pltpu.make_async_copy(source, target, sems.at[i]) for i, (source, target) in enumerate(pairs)]
     for copy in copies:
@@ -115,7 +129,8 @@
 
 
 def send_kernel(
-    lengths, key, value, decay, prompt_query, prompt_key, prompt_value, prompt_decay, out, key_out, value_out,
+    lengths, key, value, decay, prompt_query, prompt_key, prompt_value, prompt_decay,
+    mine, theirs, query_out, key_out, value_out,
     key_in, value_in, decay_in, query_in, prompt_key_in, prompt_value_in, prompt_decay_in,
     rows_k, rows_v, prompt_q, prompt_k, prompt_v, sems,
 ):
@@ -144,14 +159,13 @@
     prompt_v[...] = prompt_value_in[...].astype(F32).reshape(PT * HEADS, D)
     for h in range(HEADS):
         tail = jnp.where(at == 0, wide[h : h + 1], jnp.where(at == 1, totals[h : h + 1], 0.0))
-        q = prompt_q[pl.ds(h, PT, HEADS), :]
+        query_out[h] = prompt_q[pl.ds(h, PT, HEADS), :]
         k = prompt_k[pl.ds(h, PT, HEADS), :]
         v = prompt_v[pl.ds(h, PT, HEADS), :]
-        for half in range(2):
-            out[2 * h + half, 64:80, :] = k
-            out[2 * h + half, 80:88, :] = pack(v, half)
-            out[2 * h + half, 88:96, :] = tail
-            out[2 * h + half, 96:104, :] = q[8 * half : 8 * half + 8]
+        for ref, half in zip((mine, theirs), choose(pack(v, 0), pack(v, 1))):
+            ref[h, 64:80, :] = k
+            ref[h, 80:88, :] = half
+            ref[h, 88:96, :] = tail
     for copy in copies[5:]:
         copy.wait()
     rows_v[...] = value_in[0].astype(F32).reshape(T * HEADS, D)
@@ -162,8 +176,25 @@
         key_out[h] = k.astype(BF16)
         value_out[h] = v
         state = dot_right(v, k * to_end[:, h : h + 1], 0, 0)
-        for half in range(2):
-            out[2 * h + half, 0:64, :] = state[half * HALF : (half + 1) * HALF]
+        for ref, half in zip((mine, theirs), choose(state[0:64], state[64:128])):
+            ref[h, 0:64, :] = half
+
+
+def merge_kernel(mine, other, query, out, first_out, totals_out):
+    at = iota((8, D), 0)
+    for h in range(HEADS):
+        first, last = in_order(mine[h], other[h])
+        totals_out[h : h + 1, :] = first[89:90]
+        totals_out[HEADS + h : HEADS + h + 1, :] = last[89:90]
+        first_out[h] = first[0:64]
+        out[h, 0:64, :] = jnp.exp(last[89:90]) * first[0:64] + last[0:64]
+        out[h, 64:80, :] = first[64:80]
+        out[h, 80:96, :] = last[64:80]
+        out[h, 96:104, :] = first[80:88]
+        out[h, 104:112, :] = last[80:88]
+        tile = jnp.where(at == 0, first[88:89], jnp.where(at == 1, first[89:90], 0.0))
+        out[h, 112:120, :] = jnp.where(at == 2, last[88:89], jnp.where(at == 3, last[89:90], tile))
+        out[h, 120:136, :] = query[h]
 
 
 def wide_columns(columns):
@@ -198,24 +229,25 @@
 
 
 def prompt_row_kernel(received, out, column_out, query_out, blocks_out):
-    decay = received[:, 88, :]
+    decay = jnp.concatenate([received[:, 112, :], received[:, 114, :]], axis=0)
     token_block, token_place = iota((ROW, CTX), 0) // PT, iota((ROW, D), 0) % PT
-    block = iota((ROW, CTX), 1)
+    at = iota((ROW, CTX), 1)
+    block = jnp.where(at < CHIPS, 2 * at, 2 * (at - CHIPS) + 1)
     parts = split3(decay)
     own = sum(dot((block == token_block).astype(BF16), part, 1, 0) for part in parts)
     before = sum(dot((block < token_block).astype(BF16), part, 1, 0) for part in parts)
     running = jnp.sum(before + jnp.where(iota((ROW, D), 1) <= token_place, own, 0.0), axis=1, keepdims=True)
     last = running[ROW - 1 : ROW]
-    k = received[:, 64:80, :].reshape(ROW, D)
-    v = rows_of_half(received[:, 80:88, :]).astype(BF16)
+    k = received[:, 64:96, :].reshape(ROW, D)
+    v = rows_of_half(received[:, 96:112, :].reshape(CTX, 8, D)).astype(BF16)
     state = dot_right(v, k * jnp.exp(last - running), 0, 0)
     total = jnp.broadcast_to(last, (8, D))
     for s in range(SAMPLE):
         out[s, 0:64, :] = state
         out[s, 64:72, :] = total
     column_out[...] = jnp.broadcast_to(running, (ROW, D))
-    query_out[...] = received[:, 96:104, :]
-    blocks_out[...] = received[:, 89, :]
+    query_out[...] = received[:, 120:136, :]
+    blocks_out[...] = received[:, 113, :] + received[:, 115, :]
 
 
 def same_block():
@@ -229,20 +261,13 @@
     return high, low
 
 
-def second_core():
-    return lax.axis_index("ctx") % 2 == 1
-
-
 def prompt_local_kernel(
     received, other, column, query_out, key_out, value_out, line_out, local_out
 ):
-    own = received[:, 96:104, :]
-    second = second_core()
-    first_half = jnp.where(second, other[...], own)
-    second_half = jnp.where(second, own, other[...])
-    q = jnp.concatenate([first_half, second_half], axis=1).reshape(ROW, D).astype(BF16)
-    k = received[:, 64:80, :].reshape(ROW, D).astype(BF16)
-    v = rows_of_half(received[:, 80:88, :]).astype(BF16)
+    both = in_order(received[:, 120:136, :], other[...])
+    q = jnp.concatenate(both, axis=1).reshape(ROW, D).astype(BF16)
+    k = received[:, 64:96, :].reshape(ROW, D).astype(BF16)
+    v = rows_of_half(received[:, 96:112, :].reshape(CTX, 8, D)).astype(BF16)
     running = column[:, 0:1]
     line = column_to_row(running)
     query_out[...] = q
@@ -253,7 +278,9 @@
     local_out[...] = sum(dot(part, v, 1, 0) for part in weights)
 
 
-def fold_kernel(rows_received, received, query, local, column, after_reply, out, start_out, factors_out):
+def fold_kernel(
+    rows_received, received, blocks, query, local, column, after_reply, out, start_out, factors_out
+):
     del after_reply
     place = lax.axis_index("sample")
     totals = [rows_received[s, 64:65, :] for s in range(SAMPLE)]
@@ -264,11 +291,11 @@
         end = jnp.exp(totals[s]) * end + rows_received[s, 0:64, :]
     start_out[...] = start
     state = end
-    for b in range(CTX):
-        out[b, 0:64, :] = state
-        state = jnp.exp(received[b, 89:90, :]) * state + received[b, 0:64, :]
+    for y in range(CHIPS):
+        out[y, 0:64, :] = state
+        state = jnp.exp(blocks[y : y + 1, :]) * state + received[y, 0:64, :]
     outputs = local[...] + jnp.exp(column[:, 0:1]) * dot_right(query[...], start, 1, 1)
-    out[:, 64:72, :] = packed_half(outputs)
+    out[:, 64:80, :] = packed_half(outputs).reshape(CHIPS, PT, D)
     for s in range(SAMPLE):
         after = jnp.zeros((1, D), F32)
         between = after
@@ -279,21 +306,30 @@
         factors_out[SAMPLE + s : SAMPLE + s + 1, :] = jnp.where(place > s, jnp.exp(between), 0.0)
 
 
+def spread_kernel(received, first_state, totals, mine, theirs):
+    for h in range(HEADS):
+        before = received[h, 0:64, :]
+        after = jnp.exp(totals[h : h + 1, :]) * before + first_state[h]
+        mine[h, 0:64, :], theirs[h, 0:64, :] = choose(before, after)
+        mine[h, 64:72, :], theirs[h, 64:72, :] = choose(received[h, 64:72, :], received[h, 72:80, :])
+
+
 def output_kernel(
-    received, query, weights, value, grad, growth, scale, prompt_upstream, out, output_out, prompt_out
+    mine, other, query, weights, value, grad, growth, scale, prompt_upstream, out, output_out, prompt_out
 ):
     squares = jnp.zeros((T, D), F32)
     crossed = jnp.zeros((T, D), F32)
     prompt_squares = jnp.zeros((PT, D), F32)
     prompt_crossed = jnp.zeros((PT, D), F32)
     for h in range(HEADS):
-        state = jnp.concatenate([received[2 * h, 0:64, :], received[2 * h + 1, 0:64, :]], axis=0)
+        low, high = in_order(mine[h], other[h])
+        state = jnp.concatenate([low[0:64], high[0:64]], axis=0)
         outputs = dot(weights[h], value[h], 1, 0) + growth[:, h : h + 1] * dot_right(query[h], state, 1, 1)
         output_out[h] = outputs
         upstream = grad[h].astype(F32) * scale[h : h + 1, :]
         squares = squares + outputs * outputs
         crossed = crossed + upstream * outputs
-        outputs = unpack(received[2 * h, 64:72, :], received[2 * h + 1, 64:72, :])
+        outputs = unpack(low[64:72], high[64:72])
         prompt_out[h] = outputs
         prompt_squares = prompt_squares + outputs * outputs
         prompt_crossed = prompt_crossed + prompt_upstream[h] * outputs
@@ -315,7 +351,7 @@
 
 
 def grad_kernel(
-    sums, outputs, prompt_outputs, query, grad, growth, scale, prompt_upstream, out, grad_out
+    sums, outputs, prompt_outputs, query, grad, growth, scale, prompt_upstream, mine, theirs, grad_out
 ):
     total = sums[0] + sums[1] + sums[2] + sums[3]
     inverse, project = norm_terms(row_to_column(total[0:1], T), row_to_column(total[1:2], T))
@@ -327,13 +363,21 @@
         back = dot_right(out_grad, query[h].astype(F32) * growth[:, h : h + 1], 0, 0)
         prompt_out_grad = (prompt_upstream[h] - prompt_outputs[h] * prompt_project) * prompt_inverse
         prompt_out_grad = prompt_out_grad.astype(BF16).astype(F32)
-        for half in range(2):
-            out[2 * h + half, 0:64, :] = back[half * HALF : (half + 1) * HALF]
-            out[2 * h + half, 64:72, :] = pack(prompt_out_grad, half)
+        mine[h, 0:64, :], theirs[h, 0:64, :] = choose(back[0:64], back[64:128])
+        mine[h, 64:72, :], theirs[h, 64:72, :] = choose(pack(prompt_out_grad, 0), pack(prompt_out_grad, 1))
+
+
+def back_merge_kernel(mine, other, totals, out, last_out):
+    for h in range(HEADS):
+        first, last = in_order(mine[h], other[h])
+        last_out[h] = last[0:64]
+        out[h, 0:64, :] = first[0:64] + jnp.exp(totals[h : h + 1, :]) * last[0:64]
+        out[h, 64:72, :] = first[64:72]
+        out[h, 72:80, :] = last[64:72]
 
 
 def reply_back_kernel(
-    received, out_grad, query, key, value, weights, decay, after_fold,
+    mine, other, out_grad, query, key, value, weights, decay, after_fold,
     query_grad, key_local, value_local, to_end_out, rows,
 ):
     del after_fold
@@ -342,7 +386,7 @@
     scales = jnp.exp(columns)
     to_end_out[...] = wide_columns(jnp.exp(columns[T - 1 : T, :] - columns))
     for h in range(HEADS):
-        state = jnp.concatenate([received[2 * h, 0:64, :], received[2 * h + 1, 0:64, :]], axis=0)
+        state = jnp.concatenate(in_order(mine[h, 0:64, :], other[h, 0:64, :]), axis=0)
         og = out_grad[h]
         mask = masking(columns[:, h : h + 1], lines[h : h + 1])
         mix = (dot(og, value[h], 1, 1) * mask).astype(BF16)
@@ -354,9 +398,9 @@
 
 def back_fold_kernel(received, blocks, factors, query, column, rows_out, ready_out):
     adjoint = jnp.zeros((HALF, D), F32)
-    for b in range(CTX - 1, -1, -1):
-        adjoint = jnp.exp(blocks[b : b + 1, :]) * adjoint + received[b, 0:64, :]
-    og = rows_of_half(received[:, 64:72, :]).astype(BF16)
+    for y in range(CHIPS - 1, -1, -1):
+        adjoint = jnp.exp(blocks[y : y + 1, :]) * adjoint + received[y, 0:64, :]
+    og = rows_of_half(received[:, 64:80, :].reshape(CTX, 8, D)).astype(BF16)
     back = dot_right(og, query[...].astype(F32) * jnp.exp(column[:, 0:1]), 0, 0)
     for s in range(SAMPLE):
         rows_out[s] = factors[s : s + 1, :] * adjoint + factors[SAMPLE + s : SAMPLE + s + 1, :] * back
@@ -365,23 +409,21 @@
 
 def prompt_mid_kernel(received, blocks, start, query, key, value, column, line, out, swap_out):
     adjoint = jnp.zeros((HALF, D), F32)
-    for b in range(CTX - 1, -1, -1):
-        out[b, 0:64, :] = adjoint
-        adjoint = jnp.exp(blocks[b : b + 1, :]) * adjoint + received[b, 0:64, :]
-    og = rows_of_half(received[:, 64:72, :]).astype(BF16)
+    for y in range(CHIPS - 1, -1, -1):
+        out[y, 0:64, :] = adjoint
+        adjoint = jnp.exp(blocks[y : y + 1, :]) * adjoint + received[y, 0:64, :]
+    og = rows_of_half(received[:, 64:80, :].reshape(CTX, 8, D)).astype(BF16)
     running = column[:, 0:1]
     mask = masking(running, line[0:1, :])
     mix = split(dot(og, value[...], 1, 1) * mask)
     k, q = key[...], query[...]
     query_grad = sum(dot(part, k, 1, 0) for part in mix) + jnp.exp(running) * dot_right(og, start[...], 1, 0)
-    query_grad = query_grad.reshape(CTX, PT, D)
-    second = second_core()
-    swap_out[...] = jnp.where(second, query_grad[:, 0:8], query_grad[:, 8:16])
+    query_grad = query_grad.reshape(CHIPS, 2 * PT, D)
     key_local = sum(dot(part, q, 0, 0) for part in mix)
     value_local = sum(dot(part, og, 0, 0) for part in prompt_weights(q, k, mask))
-    out[:, 64:80, :] = key_local.reshape(CTX, PT, D)
-    out[:, 80:88, :] = packed_half(value_local)
-    out[:, 88:96, :] = jnp.where(second, query_grad[:, 8:16], query_grad[:, 0:8])
+    out[:, 64:96, :] = key_local.reshape(CHIPS, 2 * PT, D)
+    out[:, 96:112, :] = packed_half(value_local).reshape(CHIPS, PT, D)
+    out[:, 112:128, :], swap_out[...] = choose(query_grad[:, 0:PT], query_grad[:, PT:])
 
 
 def prompt_back_kernel(rows_received, swapped, key, value, column, message, after_reply, out):
@@ -394,25 +436,34 @@
     key_grad = to_end * dot_right(value[...], adjoint, 1, 0)
     value_grad = to_end * dot_right(key[...], adjoint, 1, 1)
     out[:, 0:64, :] = message[:, 0:64, :]
-    out[:, 64:80, :] = message[:, 64:80, :] + key_grad.reshape(CTX, PT, D)
-    out[:, 80:88, :] = message[:, 80:88, :] + packed_half(value_grad)
-    out[:, 88:96, :] = message[:, 88:96, :] + swapped[...]
+    out[:, 64:96, :] = message[:, 64:96, :] + key_grad.reshape(CHIPS, 2 * PT, D)
+    out[:, 96:112, :] = message[:, 96:112, :] + packed_half(value_grad).reshape(CHIPS, PT, D)
+    out[:, 112:128, :] = message[:, 112:128, :] + swapped[...]
+
+
+def back_spread_kernel(received, last_back, totals, mine, theirs):
+    for h in range(HEADS):
+        after = received[h, 0:64, :]
+        before = jnp.exp(totals[HEADS + h : HEADS + h + 1, :]) * after + last_back[h]
+        mine[h, 0:64, :], theirs[h, 0:64, :] = choose(before, after)
+        mine[h, 64:80, :], theirs[h, 64:80, :] = choose(received[h, 64:80, :], received[h, 80:96, :])
+        mine[h, 80:88, :], theirs[h, 80:88, :] = choose(received[h, 96:104, :], received[h, 104:112, :])
 
 
 def end_kernel(
-    received, key, value, key_local, value_local, to_end,
+    received, mine, other, key, value, key_local, value_local, to_end,
     key_grad, value_grad, prompt_query_grad, prompt_key_grad, prompt_value_grad,
     rows_k, rows_v, prompt_q, prompt_k, prompt_v,
 ):
     for h in range(HEADS):
-        low, high = received[2 * h], received[2 * h + 1]
+        low, high = in_order(mine[h], other[h])
         adjoint = jnp.concatenate([low[0:64], high[0:64]], axis=0)
         scale = to_end[:, h : h + 1]
         rows_k[pl.ds(h, T, HEADS), :] = key_local[h] + scale * dot_right(value[h], adjoint, 1, 0)
         rows_v[pl.ds(h, T, HEADS), :] = value_local[h] + scale * dot_right(key[h], adjoint, 1, 1)
         prompt_k[pl.ds(h, PT, HEADS), :] = low[64:80] + high[64:80]
         prompt_v[pl.ds(h, PT, HEADS), :] = unpack(low[80:88], high[80:88])
-        prompt_q[pl.ds(h, PT, HEADS), :] = jnp.concatenate([low[88:96], high[88:96]], axis=0)
+        prompt_q[pl.ds(h, PT, HEADS), :] = received[h, 112:128, :]
     key_grad[0] = rows_k[...].reshape(T, HEADS, D).astype(BF16)
     value_grad[0] = rows_v[...].reshape(T, HEADS, D).astype(BF16)
     prompt_query_grad[...] = prompt_q[...].reshape(PT, HEADS, D).astype(BF16)
@@ -459,6 +510,11 @@
     return lax.all_to_all(x, axis, 0, 0, tiled=True)
 
 
+def exchange_chips(x):
+    groups = [[2 * chip + core for chip in range(CHIPS)] for core in range(2)]
+    return lax.all_to_all(x, "ctx", 0, 0, axis_index_groups=groups, tiled=True)
+
+
 def swap_cores(x):
     return lax.ppermute(x, "ctx", [(i, i ^ 1) for i in range(CTX)])
 
@@ -479,9 +535,9 @@
 ):
     work = 8 * 2 * T * D * D
     reply_in, prompt_in = pltpu.VMEM(*REPLY), pltpu.VMEM(*PROMPT)
-    sent, key, value = run(
+    mine, theirs, own_query, key, value = run(
         send_kernel,
-        [((CTX, 104, D), F32), BY_HEAD, BY_HEAD],
+        [((HEADS, 96, D), F32), ((HEADS, 96, D), F32), ((HEADS, PT, D), F32), BY_HEAD, BY_HEAD],
         [reply_in, reply_in, pltpu.VMEM((1, HEADS, T), F32)]
         + [prompt_in] * 3
         + [pltpu.VMEM((HEADS, PT), F32)]
@@ -498,12 +554,21 @@
         prompt_decay,
         hbm=range(1, 8),
         flops=2 * work,
+        kept=(0, 2, 3, 4),
+    )
+    sent, first_state, block_totals = run(
+        merge_kernel,
+        [((HEADS, 136, D), F32), ((HEADS, HALF, D), F32), ((2 * HEADS, D), F32)],
+        [],
+        mine,
+        swap_cores(theirs),
+        own_query,
         kept=(1, 2),
     )
-    first = exchange(sent, "ctx")
+    first = exchange_chips(sent)
     sent, column, half_query, blocks = run(
         prompt_row_kernel,
-        [((SAMPLE, 72, D), F32), ((ROW, D), F32), ((CTX, 8, D), F32), ((CTX, D), F32)],
+        [((SAMPLE, 72, D), F32), ((ROW, D), F32), ((CHIPS, PT, D), F32), ((CHIPS, D), F32)],
         [],
         first,
         kept=(1, 3),
@@ -542,22 +607,33 @@
     )
     sent, start, factors = run(
         fold_kernel,
-        [((CTX, 72, D), F32), ((HALF, D), F32), ((2 * SAMPLE, D), F32)],
+        [((CHIPS, 80, D), F32), ((HALF, D), F32), ((2 * SAMPLE, D), F32)],
         [],
         rows,
         first,
+        blocks,
         row_query,
         row_local,
         column,
         scale,
         kept=(1, 2),
     )
-    states = exchange(sent, "ctx")
+    mine, theirs = run(
+        spread_kernel,
+        [((HEADS, 72, D), F32), ((HEADS, 72, D), F32)],
+        [],
+        exchange_chips(sent),
+        first_state,
+        block_totals,
+        kept=(0,),
+    )
+    other = swap_cores(theirs)
     sent, outputs, prompt_outputs = run(
         output_kernel,
         [((HEAD_AXIS, 8, D), F32), BY_HEAD_WIDE, ((HEADS, PT, D), F32)],
         [],
-        states,
+        mine,
+        other,
         query,
         weights,
         value,
@@ -569,9 +645,9 @@
         kept=(1, 2),
     )
     sums = exchange(sent, "head")
-    sent, out_grad = run(
+    back_mine, back_theirs, out_grad = run(
         grad_kernel,
-        [((CTX, 72, D), F32), BY_HEAD],
+        [((HEADS, 72, D), F32), ((HEADS, 72, D), F32), BY_HEAD],
         [],
         sums,
         outputs,
@@ -582,9 +658,18 @@
         scale,
         prompt_upstream,
         flops=2 * work,
+        kept=(0, 2),
+    )
+    sent, last_back = run(
+        back_merge_kernel,
+        [((HEADS, 80, D), F32), ((HEADS, HALF, D), F32)],
+        [],
+        back_mine,
+        swap_cores(back_theirs),
+        block_totals,
         kept=(1,),
     )
-    backs = exchange(sent, "ctx")
+    backs = exchange_chips(sent)
     sent, ready = run(
         back_fold_kernel,
         [((SAMPLE, HALF, D), F32), ((8, D), F32)],
@@ -601,7 +686,8 @@
         reply_back_kernel,
         [REPLY, BY_HEAD_WIDE, BY_HEAD_WIDE, ((T, D), F32)],
         [REPLY_ROWS],
-        states,
+        mine,
+        other,
         out_grad,
         query,
         key,
@@ -614,7 +700,7 @@
     )
     message, swap = run(
         prompt_mid_kernel,
-        [((CTX, 96, D), F32), ((CTX, 8, D), F32)],
+        [((CHIPS, 128, D), F32), ((CHIPS, PT, D), F32)],
         [],
         backs,
         blocks,
@@ -629,7 +715,7 @@
     )
     (sent,) = run(
         prompt_back_kernel,
-        [((CTX, 96, D), F32)],
+        [((CHIPS, 128, D), F32)],
         [],
         rows,
         swap_cores(swap),
@@ -639,12 +725,23 @@
         message,
         to_end,
     )
-    received = exchange(sent, "ctx")
+    received = exchange_chips(sent)
+    end_mine, end_theirs = run(
+        back_spread_kernel,
+        [((HEADS, 88, D), F32), ((HEADS, 88, D), F32)],
+        [],
+        received,
+        last_back,
+        block_totals,
+        kept=(0,),
+    )
     reply_key_grad, reply_value_grad, prompt_query_grad, prompt_key_grad, prompt_value_grad = run(
         end_kernel,
         [REPLY, REPLY, PROMPT, PROMPT, PROMPT],
         [REPLY_ROWS] * 2 + [PROMPT_ROWS] * 3,
         received,
+        end_mine,
+        swap_cores(end_theirs),
         key,
         value,
         key_local,

time: 161 us -> 151 us (0.938)
  blocking collectives: 113 us -> 76.9 us
  starting transfers between devices: 16.4 us -> 39.9 us
  waiting for transfers between devices: 11.6 us -> 14 us
    all_to_all x5 -> x1, blocking collectives: 113 us -> 8.02 us  [exchange(): return lax.all_to_all(x, axis, 0, 0, tiled=True)]
    all_to_all x0 -> x4, blocking collectives: none -> 68.8 us  [exchange_chips(): return lax.all_to_all(x, 'ctx', 0, 0, axis_index_groups=groups, tiled=True)]
    ppermute x2 -> x6, starting transfers between devices: 3.93 us -> 27.8 us  [swap_cores(): return lax.ppermute(x, 'ctx', [(i, i ^ 1) for i in range(CTX)])]
    ppermute x2 -> x6, waiting for transfers between devices: 0.01 us -> 4.99 us  [swap_cores(): return lax.ppermute(x, 'ctx', [(i, i ^ 1) for i in range(CTX)])]
    all_to_all x2, waiting for transfers between devices: 11.6 us -> 9.04 us  [exchange(): return lax.all_to_all(x, axis, 0, 0, tiled=True)]
    unnamed x32 -> x28, local copies, waits for them, and re-layouts: 5.23 us -> 4.45 us
    pallas_call x12 -> x16, Pallas kernels: 12.8 us -> 13.2 us  [run(): pl.pallas_call(kernel, out_shape=[pltpu.VMEM(shape, kind) if i in kept el...]
  transfers between devices with their start and end apart: 4 -> 8, of which waited for: 2 -> 6; matrix products, arithmetic and copies ran while one was open for 0% -> 0% of each run, Pallas kernels for 3% -> 4%
where the time goes in v5:
time: 151 us; the launch traced here: 150 us
  blocking collectives  76.9 us (51%)
  starting transfers between devices  39.9 us (26%)
  waiting for transfers between devices  14 us (9%)
  Pallas kernels  13.2 us (9%)
  local copies, waits for them, and re-layouts  4.45 us (3%)
    all_to_all x4, blocking collectives, exchange_chips(): return lax.all_to_all(x, 'ctx', 0, 0, axis_index_groups=groups, tiled=True)  68.8 us
    ppermute x6, starting transfers between devices, swap_cores(): return lax.ppermute(x, 'ctx', [(i, i ^ 1) for i in range(CTX)])  27.8 us
    pallas_call x16, Pallas kernels, run(): pl.pallas_call(kernel, out_shape=[pltpu.VMEM(shape, kind) if i in kept el...  13.2 us
    all_to_all x2, starting transfers between devices, exchange(): return lax.all_to_all(x, axis, 0, 0, tiled=True)  12 us
    all_to_all x2, waiting for transfers between devices, exchange(): return lax.all_to_all(x, axis, 0, 0, tiled=True)  9.04 us
    all_to_all x1, blocking collectives, exchange(): return lax.all_to_all(x, axis, 0, 0, tiled=True)  8.02 us
    ppermute x6, waiting for transfers between devices, swap_cores(): return lax.ppermute(x, 'ctx', [(i, i ^ 1) for i in range(CTX)])  4.99 us
    unnamed x28, local copies, waits for them, and re-layouts  4.45 us
  transfers between devices with their start and end apart: 8, of which 6 were waited for; matrix products, arithmetic and copies ran while one was open for 0% of the time, Pallas kernels for 4%

profile of v5, /device:TPU:1, one launch (start us, length us, event | category | flops | bytes accessed | tf_op | source)
XLA Modules:
  0.0 149.9 jit_solution(10817573142656219265)
XLA Ops:
  1.3 1.8 %send_kernel.1 = (f32[8,96,128]{2,1,0:T(8,128)S(1)}, f32[8,96,128]{2,1,0:T(8,128)S(1)}, f32[8,16,128]{2,1,0:T(8,128)S(1)}, bf16[8,128,128]{2,1,0:T(8,128)(2,1)S(1)}, bf16[8,128,128]{2,1,0:T(8,128)(2,1)S(1)}) custom-call(s32[1]{0:T(128)S(6)} %copy.18.lengths, bf16[1,128,8,128]{3,2,1,0:T(8,128)(2,1)} %key.1, bf16[1,128,8,128]{3,2,1,0:T(8,128)(2,1)} %value.1, ...), custom_call_target="tpu_custom_call" | custom-call | flops 67108864 | bytes 1254408 | tf_op jit(solution)/shard_map/send_kernel/pallas_call | solution.py:494
  3.0 8.8 %collective-permute-start = (f32[8,96,128]{2,1,0:T(8,128)S(1)}, f32[8,96,128]{2,1,0:T(8,128)S(1)}, u32[]{:S(2)}, u32[]{:S(2)}) collective-permute-start(f32[8,96,128]{2,1,0:T(8,128)S(1)} %get-tuple-element.58), channel_id=1, source_target_pairs={{0,4},{4,0},{8,12},{12,8},{16,20},{20,16},{24,28},{28,24},{32,36},... | collective-permute-start | bytes 1179656 | tf_op jit(solution)/shard_map/ppermute | solution.py:519
  11.8 1.3 collective-permute-done.other
  13.2 0.1 merge_kernel.1
  13.3 20.7 %all_to_all.35.received = f32[8,136,128]{2,1,0:T(8,128)S(1)} all-to-all(f32[8,136,128]{2,1,0:T(8,128)S(1)} %get-tuple-element.60), channel_id=1, replica_groups={{0,8,16,24,32,40,48,56},{4,12,20,28,36,44,52,60},{1,9,17,25,33,41,49,57..., dimensions={0} | all-to-all | bytes 1114112 | tf_op jit(solution)/shard_map/all_to_all | solution.py:515
  33.9 1.2 prompt_row_kernel.1
  35.2 8.5 %all-to-all-start.1 = ((f32[8,72,128]{2,1,0:T(8,128)}), f32[8,72,128]{2,1,0:T(8,128)S(1)}, u32[]{:S(2)}, u32[]{:S(2)}) async-start(f32[8,72,128]{2,1,0:T(8,128)} %get-tuple-element.61), calls=%async_computation.1 | async-start | bytes 589824 | tf_op jit(solution)/shard_map/all_to_all | solution.py:510
  43.6 3.6 %collective-permute-start.1 = (f32[8,16,128]{2,1,0:T(8,128)S(1)}, f32[8,16,128]{2,1,0:T(8,128)S(1)}, u32[]{:S(2)}, u32[]{:S(2)}) collective-permute-start(f32[8,16,128]{2,1,0:T(8,128)S(1)} %get-tuple-element.63), channel_id=1, source_target_pairs={{0,4},{4,0},{8,12},{12,8},{16,20},{20,16},{24,28},{28,24},{32,36},... | collective-permute-start | bytes 196616 | tf_op jit(solution)/shard_map/ppermute | solution.py:519
  47.3 0.0 copy-done.9
  47.3 0.0 copy-done.10
  47.3 1.5 reply_local_kernel.1
  48.8 0.0 collective-permute-done.1.other
  48.8 0.4 prompt_local_kernel.1
  49.2 0.6 copy-done.4
  49.9 4.3 %all-to-all-done.1.rows_received = f32[8,72,128]{2,1,0:T(8,128)S(1)} async-done(((f32[8,72,128]{2,1,0:T(8,128)}), f32[8,72,128]{2,1,0:T(8,128)S(1)}, u32[]{:S(2)}, u32[]{:S(2)}) %all-to-all-start.1) | async-done | bytes 294944 | tf_op jit(solution)/shard_map/all_to_all | solution.py:510
  54.2 0.3 fold_kernel.1
  54.5 12.4 %all_to_all.36.received = f32[8,80,128]{2,1,0:T(8,128)S(1)} all-to-all(f32[8,80,128]{2,1,0:T(8,128)S(1)} %get-tuple-element.69), channel_id=1, replica_groups={{0,8,16,24,32,40,48,56},{4,12,20,28,36,44,52,60},{1,9,17,25,33,41,49,57..., dimensions={0} | all-to-all | bytes 655360 | tf_op jit(solution)/shard_map/all_to_all | solution.py:515
  66.9 0.1 spread_kernel.1
  66.9 6.2 %collective-permute-start.2 = (f32[8,72,128]{2,1,0:T(8,128)S(1)}, f32[8,72,128]{2,1,0:T(8,128)S(1)}, u32[]{:S(2)}, u32[]{:S(2)}) collective-permute-start(f32[8,72,128]{2,1,0:T(8,128)S(1)} %get-tuple-element.73), channel_id=1, source_target_pairs={{0,4},{4,0},{8,12},{12,8},{16,20},{20,16},{24,28},{28,24},{32,36},... | collective-permute-start | bytes 884744 | tf_op jit(solution)/shard_map/ppermute | solution.py:519
  73.1 1.2 collective-permute-done.2.other
  74.3 0.7 output_kernel.1
  75.0 8.0 %all_to_all.37.sums = f32[4,8,128]{2,1,0:T(8,128)S(1)} all-to-all(f32[4,8,128]{2,1,0:T(8,128)S(1)} %get-tuple-element.80), channel_id=1, replica_groups=mesh['sample'=8,'ctx'=16,'head'=4] {'head'}, dimensions={0} | all-to-all | bytes 32768 | tf_op jit(solution)/shard_map/all_to_all | solution.py:510
  83.0 0.6 grad_kernel.1
  83.7 0.0 copy-start.2
  83.7 0.7 copy-done.2
  84.4 3.7 %collective-permute-start.3 = (f32[8,72,128]{2,1,0:T(8,128)S(1)}, f32[8,72,128]{2,1,0:T(8,128)S(1)}, u32[]{:S(2)}, u32[]{:S(2)}) collective-permute-start(f32[8,72,128]{2,1,0:T(8,128)S(1)} %get-tuple-element.84), channel_id=1, source_target_pairs={{0,4},{4,0},{8,12},{12,8},{16,20},{20,16},{24,28},{28,24},{32,36},... | collective-permute-start | bytes 884744 | tf_op jit(solution)/shard_map/ppermute | solution.py:519
  88.1 1.2 collective-permute-done.3.other
  89.3 0.1 back_merge_kernel.1
  89.4 16.1 %all_to_all.38.received = f32[8,80,128]{2,1,0:T(8,128)S(1)} all-to-all(f32[8,80,128]{2,1,0:T(8,128)S(1)} %get-tuple-element.85), channel_id=1, replica_groups={{0,8,16,24,32,40,48,56},{4,12,20,28,36,44,52,60},{1,9,17,25,33,41,49,57..., dimensions={0} | all-to-all | bytes 655360 | tf_op jit(solution)/shard_map/all_to_all | solution.py:515
  105.5 1.0 back_fold_kernel.1
  106.5 3.5 %all-to-all-start.5 = ((f32[8,64,128]{2,1,0:T(8,128)}), f32[8,64,128]{2,1,0:T(8,128)S(1)}, u32[]{:S(2)}, u32[]{:S(2)}) async-start(f32[8,64,128]{2,1,0:T(8,128)} %get-tuple-element.87), calls=%async_computation.5 | async-start | bytes 524288 | tf_op jit(solution)/shard_map/all_to_all | solution.py:510
  110.1 0.0 copy-start.3
  110.1 0.9 prompt_mid_kernel.1
  111.0 2.4 %collective-permute-start.4 = (f32[8,16,128]{2,1,0:T(8,128)S(1)}, f32[8,16,128]{2,1,0:T(8,128)S(1)}, u32[]{:S(2)}, u32[]{:S(2)}) collective-permute-start(f32[8,16,128]{2,1,0:T(8,128)S(1)} %get-tuple-element.92), channel_id=1, source_target_pairs={{0,4},{4,0},{8,12},{12,8},{16,20},{20,16},{24,28},{28,24},{32,36},... | collective-permute-start | bytes 196616 | tf_op jit(solution)/shard_map/ppermute | solution.py:519
  113.4 2.7 %reply_back_kernel.1 = (bf16[1,128,8,128]{3,2,1,0:T(8,128)(2,1)}, f32[8,128,128]{2,1,0:T(8,128)S(1)}, f32[8,128,128]{2,1,0:T(8,128)S(1)}, f32[128,128]{1,0:T(8,128)S(1)}) custom-call(f32[8,72,128]{2,1,0:T(8,128)S(1)} %get-tuple-element.72.mine, f32[8,72,128]{2,1,0:T(8,128)S(1)} %collective-permute-done.2.other, bf16[8,128,128]{2,1,0:T(8,128)(2,1)S(1)} %copy-done.3, ...), custom_call_target="tpu_custom_call" | custom-call | flops 201326592 | bytes 3817472 | tf_op jit(solution)/shard_map/reply_back_kernel/pallas_call | solution.py:494
  116.1 0.8 copy-done
  116.9 0.0 collective-permute-done.4.swapped
  116.9 0.6 copy-done.7
  117.5 4.7 %all-to-all-done.5.rows_received = f32[8,64,128]{2,1,0:T(8,128)S(1)} async-done(((f32[8,64,128]{2,1,0:T(8,128)}), f32[8,64,128]{2,1,0:T(8,128)S(1)}, u32[]{:S(2)}, u32[]{:S(2)}) %all-to-all-start.5) | async-done | bytes 262176 | tf_op jit(solution)/shard_map/all_to_all | solution.py:510
  122.2 0.8 copy-done.6
  123.0 0.8 copy-done.8
  123.9 0.3 prompt_back_kernel.1
  124.2 19.7 %all_to_all.39.received = f32[8,128,128]{2,1,0:T(8,128)S(1)} all-to-all(f32[8,128,128]{2,1,0:T(8,128)S(1)} %prompt_back_kernel.1), channel_id=1, replica_groups={{0,8,16,24,32,40,48,56},{4,12,20,28,36,44,52,60},{1,9,17,25,33,41,49,57..., dimensions={0} | all-to-all | bytes 1048576 | tf_op jit(solution)/shard_map/all_to_all | solution.py:515
  143.8 0.1 back_spread_kernel.1
  143.9 3.2 %collective-permute-start.5 = (f32[8,88,128]{2,1,0:T(8,128)S(1)}, f32[8,88,128]{2,1,0:T(8,128)S(1)}, u32[]{:S(2)}, u32[]{:S(2)}) collective-permute-start(f32[8,88,128]{2,1,0:T(8,128)S(1)} %get-tuple-element.99), channel_id=1, source_target_pairs={{0,4},{4,0},{8,12},{12,8},{16,20},{20,16},{24,28},{28,24},{32,36},... | collective-permute-start | bytes 1081352 | tf_op jit(solution)/shard_map/ppermute | solution.py:519
  147.1 1.3 collective-permute-done.5.other
  148.4 0.0 copy-done.1
  148.4 1.5 %end_kernel.1 = (bf16[1,128,8,128]{3,2,1,0:T(8,128)(2,1)}, bf16[1,128,8,128]{3,2,1,0:T(8,128)(2,1)}, bf16[16,8,128]{2,1,0:T(8,128)(2,1)}, bf16[16,8,128]{2,1,0:T(8,128)(2,1)}, bf16[16,8,128]{2,1,0:T(8,128)(2,1)}) custom-call(f32[8,128,128]{2,1,0:T(8,128)S(1)} %all_to_all.39.received, f32[8,88,128]{2,1,0:T(8,128)S(1)} %get-tuple-element.98.mine, ...), custom_call_target="tpu_custom_call" | custom-call | flops 134217728 | bytes 5767168 | tf_op jit(solution)/shard_map/end_kernel/pallas_call | solution.py:494
  (17 shorter events, 0.0 us)
Async XLA Ops:
  3.0 10.1 %collective-permute-start = (f32[8,96,128]{2,1,0:T(8,128)S(1)}, f32[8,96,128]{2,1,0:T(8,128)S(1)}, u32[]{:S(2)}, u32[]{:S(2)}) collective-permute-start(f32[8,96,128]{2,1,0:T(8,128)S(1)} %get-tuple-element.58), channel_id=1, source_target_pairs={{0,4},{4,0},{8,12},{12,8},{16,20},{20,16},{24,28},{28,24},{32,36},... | collective-permute-start | bytes 1179656 | tf_op jit(solution)/shard_map/ppermute | solution.py:519
  35.2 12.1 %copy-start.9 = (f32[1,8,128]{2,1,0:T(8,128)S(1)}, f32[1,8,128]{2,1,0:T(8,128)}, u32[]{:S(2)}) copy-start(f32[1,8,128]{2,1,0:T(8,128)} %decay.5) | copy-start | bytes 12292
  35.2 12.1 %copy-start.10 = (bf16[16,8,128]{2,1,0:T(8,128)(2,1)S(1)}, bf16[16,8,128]{2,1,0:T(8,128)(2,1)}, u32[]{:S(2)}) copy-start(bf16[16,8,128]{2,1,0:T(8,128)(2,1)} %prompt_grad.1) | copy-start | bytes 98308
  35.2 19.0 %all-to-all-start.1 = ((f32[8,72,128]{2,1,0:T(8,128)}), f32[8,72,128]{2,1,0:T(8,128)S(1)}, u32[]{:S(2)}, u32[]{:S(2)}) async-start(f32[8,72,128]{2,1,0:T(8,128)} %get-tuple-element.61), calls=%async_computation.1 | async-start | bytes 589824 | tf_op jit(solution)/shard_map/all_to_all | solution.py:510
  43.6 3.6 %copy-start.13 = (bf16[8,128]{1,0:T(8,128)(2,1)S(1)}, bf16[8,128]{1,0:T(8,128)(2,1)}, u32[]{:S(2)}) copy-start(bf16[8,128]{1,0:T(8,128)(2,1)} %gain.1) | copy-start | bytes 6148
  43.6 5.2 %collective-permute-start.1 = (f32[8,16,128]{2,1,0:T(8,128)S(1)}, f32[8,16,128]{2,1,0:T(8,128)S(1)}, u32[]{:S(2)}, u32[]{:S(2)}) collective-permute-start(f32[8,16,128]{2,1,0:T(8,128)S(1)} %get-tuple-element.63), channel_id=1, source_target_pairs={{0,4},{4,0},{8,12},{12,8},{16,20},{20,16},{24,28},{28,24},{32,36},... | collective-permute-start | bytes 196616 | tf_op jit(solution)/shard_map/ppermute | solution.py:519
  49.2 0.6 copy-start.4
  49.9 4.6 %copy-start.11 = (f32[8,256]{1,0:T(8,128)}, f32[8,256]{1,0:T(8,128)S(1)}, u32[]{:S(2)}) copy-start(f32[8,256]{1,0:T(8,128)S(1)} %get-tuple-element.91.line) | copy-start | bytes 24580
  66.9 7.4 %collective-permute-start.2 = (f32[8,72,128]{2,1,0:T(8,128)S(1)}, f32[8,72,128]{2,1,0:T(8,128)S(1)}, u32[]{:S(2)}, u32[]{:S(2)}) collective-permute-start(f32[8,72,128]{2,1,0:T(8,128)S(1)} %get-tuple-element.73), channel_id=1, source_target_pairs={{0,4},{4,0},{8,12},{12,8},{16,20},{20,16},{24,28},{28,24},{32,36},... | collective-permute-start | bytes 884744 | tf_op jit(solution)/shard_map/ppermute | solution.py:519
  83.7 0.7 copy-start.2
  84.4 4.9 %collective-permute-start.3 = (f32[8,72,128]{2,1,0:T(8,128)S(1)}, f32[8,72,128]{2,1,0:T(8,128)S(1)}, u32[]{:S(2)}, u32[]{:S(2)}) collective-permute-start(f32[8,72,128]{2,1,0:T(8,128)S(1)} %get-tuple-element.84), channel_id=1, source_target_pairs={{0,4},{4,0},{8,12},{12,8},{16,20},{20,16},{24,28},{28,24},{32,36},... | collective-permute-start | bytes 884744 | tf_op jit(solution)/shard_map/ppermute | solution.py:519
  106.5 3.6 %copy-start.5 = (bf16[256,64]{1,0:T(8,128)(2,1)S(1)}, bf16[256,64]{1,0:T(8,128)(2,1)}, u32[]{:S(2)}) copy-start(bf16[256,64]{1,0:T(8,128)(2,1)} %copy-done.4) | copy-start | bytes 98308
  106.5 3.6 %copy-start.12 = (f32[8,256]{1,0:T(8,128)S(1)}, f32[8,256]{1,0:T(8,128)}, u32[]{:S(2)}) copy-start(f32[8,256]{1,0:T(8,128)} %copy-done.11) | copy-start | bytes 24580
  106.5 15.7 %all-to-all-start.5 = ((f32[8,64,128]{2,1,0:T(8,128)}), f32[8,64,128]{2,1,0:T(8,128)S(1)}, u32[]{:S(2)}, u32[]{:S(2)}) async-start(f32[8,64,128]{2,1,0:T(8,128)} %get-tuple-element.87), calls=%async_computation.5 | async-start | bytes 524288 | tf_op jit(solution)/shard_map/all_to_all | solution.py:510
  110.1 3.3 %copy-start.3 = (bf16[8,128,128]{2,1,0:T(8,128)(2,1)S(1)}, bf16[8,128,128]{2,1,0:T(8,128)(2,1)}, u32[]{:S(2)}) copy-start(bf16[8,128,128]{2,1,0:T(8,128)(2,1)} %copy-done.2) | copy-start | bytes 786436
  111.0 5.8 %collective-permute-start.4 = (f32[8,16,128]{2,1,0:T(8,128)S(1)}, f32[8,16,128]{2,1,0:T(8,128)S(1)}, u32[]{:S(2)}, u32[]{:S(2)}) collective-permute-start(f32[8,16,128]{2,1,0:T(8,128)S(1)} %get-tuple-element.92), channel_id=1, source_target_pairs={{0,4},{4,0},{8,12},{12,8},{16,20},{20,16},{24,28},{28,24},{32,36},... | collective-permute-start | bytes 196616 | tf_op jit(solution)/shard_map/ppermute | solution.py:519
  116.1 0.8 copy-start
  116.9 0.6 copy-start.7
  122.2 0.8 copy-start.6
  123.0 0.8 copy-start.8
  143.8 4.6 %copy-start.1 = (f32[8,128,128]{2,1,0:T(8,128)S(1)}, f32[8,128,128]{2,1,0:T(8,128)}, u32[]{:S(2)}) copy-start(f32[8,128,128]{2,1,0:T(8,128)} %copy-done) | copy-start | bytes 1572868
  143.9 4.5 %collective-permute-start.5 = (f32[8,88,128]{2,1,0:T(8,128)S(1)}, f32[8,88,128]{2,1,0:T(8,128)S(1)}, u32[]{:S(2)}, u32[]{:S(2)}) collective-permute-start(f32[8,88,128]{2,1,0:T(8,128)S(1)} %get-tuple-element.99), channel_id=1, source_target_pairs={{0,4},{4,0},{8,12},{12,8},{16,20},{20,16},{24,28},{28,24},{32,36},... | collective-permute-start | bytes 1081352 | tf_op jit(solution)/shard_map/ppermute | solution.py:519

commit v6 on v5

--- a/solution.py
+++ b/solution.py
@@ -367,7 +367,8 @@
         mine[h, 64:72, :], theirs[h, 64:72, :] = choose(pack(prompt_out_grad, 0), pack(prompt_out_grad, 1))
 
 
-def back_merge_kernel(mine, other, totals, out, last_out):
+def back_merge_kernel(mine, other, totals, after_reply, out, last_out):
+    del after_reply
     for h in range(HEADS):
         first, last = in_order(mine[h], other[h])
         last_out[h] = last[0:64]
@@ -377,10 +378,8 @@
 
 
 def reply_back_kernel(
-    mine, other, out_grad, query, key, value, weights, decay, after_fold,
-    query_grad, key_local, value_local, to_end_out, rows,
-):
-    del after_fold
+    mine, other, out_grad, query, key, value, weights, decay, query_grad, key_local, value_local, to_end_out
+):
     lines = running_rows(decay[0])
     columns = running_columns(decay[0])
     scales = jnp.exp(columns)
@@ -390,13 +389,12 @@
         og = out_grad[h]
         mask = masking(columns[:, h : h + 1], lines[h : h + 1])
         mix = (dot(og, value[h], 1, 1) * mask).astype(BF16)
-        rows[pl.ds(h, T, HEADS), :] = dot(mix, key[h], 1, 0) + scales[:, h : h + 1] * dot_right(og, state, 1, 0)
+        query_grad[h] = dot(mix, key[h], 1, 0) + scales[:, h : h + 1] * dot_right(og, state, 1, 0)
         key_local[h] = dot(mix, query[h], 0, 0)
         value_local[h] = dot(weights[h], og, 0, 0)
-    query_grad[0] = rows[...].reshape(T, HEADS, D).astype(BF16)
-
-
-def back_fold_kernel(received, blocks, factors, query, column, rows_out, ready_out):
+
+
+def back_fold_kernel(received, blocks, factors, query, column, rows_out):
     adjoint = jnp.zeros((HALF, D), F32)
     for y in range(CHIPS - 1, -1, -1):
         adjoint = jnp.exp(blocks[y : y + 1, :]) * adjoint + received[y, 0:64, :]
@@ -404,10 +402,14 @@
     back = dot_right(og, query[...].astype(F32) * jnp.exp(column[:, 0:1]), 0, 0)
     for s in range(SAMPLE):
         rows_out[s] = factors[s : s + 1, :] * adjoint + factors[SAMPLE + s : SAMPLE + s + 1, :] * back
-    ready_out[...] = adjoint[0:8]
-
-
-def prompt_mid_kernel(received, blocks, start, query, key, value, column, line, out, swap_out):
+
+
+def prompt_mid_kernel(
+    received, blocks, start, query, key, value, column, line, reply_query, out, swap_out, reply_query_grad, rows
+):
+    for h in range(HEADS):
+        rows[pl.ds(h, T, HEADS), :] = reply_query[h]
+    reply_query_grad[0] = rows[...].reshape(T, HEADS, D).astype(BF16)
     adjoint = jnp.zeros((HALF, D), F32)
     for y in range(CHIPS - 1, -1, -1):
         out[y, 0:64, :] = adjoint
@@ -426,8 +428,7 @@
     out[:, 112:128, :], swap_out[...] = choose(query_grad[:, 0:PT], query_grad[:, PT:])
 
 
-def prompt_back_kernel(rows_received, swapped, key, value, column, message, after_reply, out):
-    del after_reply
+def prompt_back_kernel(rows_received, swapped, key, value, column, message, out):
     adjoint = rows_received[0]
     for s in range(1, SAMPLE):
         adjoint = adjoint + rows_received[s]
@@ -660,32 +661,11 @@
         flops=2 * work,
         kept=(0, 2),
     )
-    sent, last_back = run(
-        back_merge_kernel,
-        [((HEADS, 80, D), F32), ((HEADS, HALF, D), F32)],
-        [],
-        back_mine,
-        swap_cores(back_theirs),
-        block_totals,
-        kept=(1,),
-    )
-    backs = exchange_chips(sent)
-    sent, ready = run(
-        back_fold_kernel,
-        [((SAMPLE, HALF, D), F32), ((8, D), F32)],
-        [],
-        backs,
-        blocks,
-        factors,
-        row_query,
-        column,
-        kept=(1,),
-    )
-    rows = exchange(sent, "sample")
-    reply_query_grad, key_local, value_local, to_end = run(
+    back_other = swap_cores(back_theirs)
+    reply_query_wide, key_local, value_local, to_end = run(
         reply_back_kernel,
-        [REPLY, BY_HEAD_WIDE, BY_HEAD_WIDE, ((T, D), F32)],
-        [REPLY_ROWS],
+        [BY_HEAD_WIDE, BY_HEAD_WIDE, BY_HEAD_WIDE, ((T, D), F32)],
+        [],
         mine,
         other,
         out_grad,
@@ -694,14 +674,35 @@
         value,
         weights,
         reply_decay,
-        ready,
         flops=6 * work,
-        kept=(1, 2, 3),
-    )
-    message, swap = run(
+        kept=(0, 1, 2, 3),
+    )
+    sent, last_back = run(
+        back_merge_kernel,
+        [((HEADS, 80, D), F32), ((HEADS, HALF, D), F32)],
+        [],
+        back_mine,
+        back_other,
+        block_totals,
+        to_end,
+        kept=(1,),
+    )
+    backs = exchange_chips(sent)
+    (sent,) = run(
+        back_fold_kernel,
+        [((SAMPLE, HALF, D), F32)],
+        [],
+        backs,
+        blocks,
+        factors,
+        row_query,
+        column,
+    )
+    rows = exchange(sent, "sample")
+    message, swap, reply_query_grad = run(
         prompt_mid_kernel,
-        [((CHIPS, 128, D), F32), ((CHIPS, PT, D), F32)],
-        [],
+        [((CHIPS, 128, D), F32), ((CHIPS, PT, D), F32), REPLY],
+        [REPLY_ROWS],
         backs,
         blocks,
         start,
@@ -710,6 +711,7 @@
         row_value,
         column,
         line,
+        reply_query_wide,
         flops=work,
         kept=(0,),
     )
@@ -723,7 +725,6 @@
         row_value,
         column,
         message,
-        to_end,
     )
     received = exchange_chips(sent)
     end_mine, end_theirs = run(

time: 151 us -> 149 us (0.987)
  local copies, waits for them, and re-layouts: 4.45 us -> 0.72 us
  waiting for transfers between devices: 14 us -> 16.2 us
    unnamed x28 -> x18, local copies, waits for them, and re-layouts: 4.45 us -> 0.72 us
    all_to_all x2, waiting for transfers between devices: 9.04 us -> 11.5 us  [exchange(): return lax.all_to_all(x, axis, 0, 0, tiled=True)]
where the time goes in v6:
time: 149 us; the launch traced here: 148 us
  blocking collectives  77 us (52%)
  starting transfers between devices  39.7 us (27%)
  waiting for transfers between devices  16.2 us (11%)
  Pallas kernels  13.3 us (9%)
  between operations  1.49 us (1%)
    all_to_all x4, blocking collectives, exchange_chips(): return lax.all_to_all(x, 'ctx', 0, 0, axis_index_groups=groups, tiled=True)  69 us
    ppermute x6, starting transfers between devices, swap_cores(): return lax.ppermute(x, 'ctx', [(i, i ^ 1) for i in range(CTX)])  27.7 us
    pallas_call x16, Pallas kernels, run(): pl.pallas_call(kernel, out_shape=[pltpu.VMEM(shape, kind) if i in kept el...  13.3 us
    all_to_all x2, starting transfers between devices, exchange(): return lax.all_to_all(x, axis, 0, 0, tiled=True)  12 us
    all_to_all x2, waiting for transfers between devices, exchange(): return lax.all_to_all(x, axis, 0, 0, tiled=True)  11.5 us
    all_to_all x1, blocking collectives, exchange(): return lax.all_to_all(x, axis, 0, 0, tiled=True)  8.02 us
    ppermute x6, waiting for transfers between devices, swap_cores(): return lax.ppermute(x, 'ctx', [(i, i ^ 1) for i in range(CTX)])  4.68 us
  transfers between devices with their start and end apart: 8, of which 6 were waited for; matrix products, arithmetic and copies ran while one was open for 0% of the time, Pallas kernels for 4%

profile of v6, /device:TPU:1, one launch (start us, length us, event | category | flops | bytes accessed | tf_op | source)
XLA Modules:
  0.0 148.4 jit_solution(14093014515479528743)
XLA Ops:
  1.3 1.8 %send_kernel.1 = (f32[8,96,128]{2,1,0:T(8,128)S(1)}, f32[8,96,128]{2,1,0:T(8,128)S(1)}, f32[8,16,128]{2,1,0:T(8,128)S(1)}, bf16[8,128,128]{2,1,0:T(8,128)(2,1)S(1)}, bf16[8,128,128]{2,1,0:T(8,128)(2,1)S(1)}) custom-call(s32[1]{0:T(128)S(6)} %copy.18.lengths, bf16[1,128,8,128]{3,2,1,0:T(8,128)(2,1)} %key.1, bf16[1,128,8,128]{3,2,1,0:T(8,128)(2,1)} %value.1, ...), custom_call_target="tpu_custom_call" | custom-call | flops 67108864 | bytes 1254408 | tf_op jit(solution)/shard_map/send_kernel/pallas_call | solution.py:495
  3.0 8.8 %collective-permute-start = (f32[8,96,128]{2,1,0:T(8,128)S(1)}, f32[8,96,128]{2,1,0:T(8,128)S(1)}, u32[]{:S(2)}, u32[]{:S(2)}) collective-permute-start(f32[8,96,128]{2,1,0:T(8,128)S(1)} %get-tuple-element.57), channel_id=1, source_target_pairs={{0,4},{4,0},{8,12},{12,8},{16,20},{20,16},{24,28},{28,24},{32,36},... | collective-permute-start | bytes 1179656 | tf_op jit(solution)/shard_map/ppermute | solution.py:520
  11.8 1.3 collective-permute-done.other
  13.2 0.1 merge_kernel.1
  13.3 20.7 %all_to_all.35.received = f32[8,136,128]{2,1,0:T(8,128)S(1)} all-to-all(f32[8,136,128]{2,1,0:T(8,128)S(1)} %get-tuple-element.59), channel_id=1, replica_groups={{0,8,16,24,32,40,48,56},{4,12,20,28,36,44,52,60},{1,9,17,25,33,41,49,57..., dimensions={0} | all-to-all | bytes 1114112 | tf_op jit(solution)/shard_map/all_to_all | solution.py:516
  33.9 1.2 prompt_row_kernel.1
  35.2 8.5 %all-to-all-start.1 = ((f32[8,72,128]{2,1,0:T(8,128)}), f32[8,72,128]{2,1,0:T(8,128)S(1)}, u32[]{:S(2)}, u32[]{:S(2)}) async-start(f32[8,72,128]{2,1,0:T(8,128)} %get-tuple-element.60), calls=%async_computation.1 | async-start | bytes 589824 | tf_op jit(solution)/shard_map/all_to_all | solution.py:511
  43.6 3.6 %collective-permute-start.1 = (f32[8,16,128]{2,1,0:T(8,128)S(1)}, f32[8,16,128]{2,1,0:T(8,128)S(1)}, u32[]{:S(2)}, u32[]{:S(2)}) collective-permute-start(f32[8,16,128]{2,1,0:T(8,128)S(1)} %get-tuple-element.62), channel_id=1, source_target_pairs={{0,4},{4,0},{8,12},{12,8},{16,20},{20,16},{24,28},{28,24},{32,36},... | collective-permute-start | bytes 196616 | tf_op jit(solution)/shard_map/ppermute | solution.py:520
  47.3 0.0 copy-done.2
  47.3 0.0 copy-done.3
  47.3 0.0 copy-done.8
  47.3 1.5 %reply_local_kernel.1 = (bf16[8,128,128]{2,1,0:T(8,128)(2,1)S(1)}, bf16[8,128,128]{2,1,0:T(8,128)(2,1)S(1)}, bf16[8,128,128]{2,1,0:T(8,128)(2,1)S(1)}, f32[128,1...) custom-call(s32[1]{0:T(128)S(6)} %copy.18.lengths, bf16[1,128,8,128]{3,2,1,0:T(8,128)(2,1)} %query.1, ...), custom_call_target="tpu_custom_call" | custom-call | flops 67108864 | bytes 1650696 | tf_op jit(solution)/shard_map/reply_local_kernel/pallas_call | solution.py:495
  48.8 0.0 collective-permute-done.1.other
  48.8 0.4 prompt_local_kernel.1
  49.2 0.0 copy-start.6
  49.2 5.0 %all-to-all-done.1.rows_received = f32[8,72,128]{2,1,0:T(8,128)S(1)} async-done(((f32[8,72,128]{2,1,0:T(8,128)}), f32[8,72,128]{2,1,0:T(8,128)S(1)}, u32[]{:S(2)}, u32[]{:S(2)}) %all-to-all-start.1) | async-done | bytes 294944 | tf_op jit(solution)/shard_map/all_to_all | solution.py:511
  54.2 0.3 fold_kernel.1
  54.5 0.0 copy-done.6
  54.5 0.0 copy-start.4
  54.5 12.4 %all_to_all.36.received = f32[8,80,128]{2,1,0:T(8,128)S(1)} all-to-all(f32[8,80,128]{2,1,0:T(8,128)S(1)} %get-tuple-element.68), channel_id=1, replica_groups={{0,8,16,24,32,40,48,56},{4,12,20,28,36,44,52,60},{1,9,17,25,33,41,49,57..., dimensions={0} | all-to-all | bytes 655360 | tf_op jit(solution)/shard_map/all_to_all | solution.py:516
  66.9 0.0 copy-done.4
  66.9 0.1 spread_kernel.1
  66.9 6.2 %collective-permute-start.2 = (f32[8,72,128]{2,1,0:T(8,128)S(1)}, f32[8,72,128]{2,1,0:T(8,128)S(1)}, u32[]{:S(2)}, u32[]{:S(2)}) collective-permute-start(f32[8,72,128]{2,1,0:T(8,128)S(1)} %get-tuple-element.72), channel_id=1, source_target_pairs={{0,4},{4,0},{8,12},{12,8},{16,20},{20,16},{24,28},{28,24},{32,36},... | collective-permute-start | bytes 884744 | tf_op jit(solution)/shard_map/ppermute | solution.py:520
  73.1 1.2 collective-permute-done.2.other
  74.3 0.7 output_kernel.1
  75.0 8.0 %all_to_all.37.sums = f32[4,8,128]{2,1,0:T(8,128)S(1)} all-to-all(f32[4,8,128]{2,1,0:T(8,128)S(1)} %get-tuple-element.79), channel_id=1, replica_groups=mesh['sample'=8,'ctx'=16,'head'=4] {'head'}, dimensions={0} | all-to-all | bytes 32768 | tf_op jit(solution)/shard_map/all_to_all | solution.py:511
  83.1 0.6 grad_kernel.1
  83.7 3.7 %collective-permute-start.3 = (f32[8,72,128]{2,1,0:T(8,128)S(1)}, f32[8,72,128]{2,1,0:T(8,128)S(1)}, u32[]{:S(2)}, u32[]{:S(2)}) collective-permute-start(f32[8,72,128]{2,1,0:T(8,128)S(1)} %get-tuple-element.83), channel_id=1, source_target_pairs={{0,4},{4,0},{8,12},{12,8},{16,20},{20,16},{24,28},{28,24},{32,36},... | collective-permute-start | bytes 884744 | tf_op jit(solution)/shard_map/ppermute | solution.py:520
  87.4 1.9 %reply_back_kernel.1 = (f32[8,128,128]{2,1,0:T(8,128)S(1)}, f32[8,128,128]{2,1,0:T(8,128)S(1)}, f32[8,128,128]{2,1,0:T(8,128)S(1)}, f32[128,128]{1,0:T(8,128)S(1)}) custom-call(f32[8,72,128]{2,1,0:T(8,128)S(1)} %get-tuple-element.71.mine, f32[8,72,128]{2,1,0:T(8,128)S(1)} %collective-permute-done.2.other, ...), custom_call_target="tpu_custom_call" | custom-call | flops 201326592 | bytes 3809280 | tf_op jit(solution)/shard_map/reply_back_kernel/pallas_call | solution.py:495
  89.4 0.0 copy-start
  89.4 0.0 collective-permute-done.3.other
  89.4 0.1 back_merge_kernel.1
  89.5 16.2 %all_to_all.38.received = f32[8,80,128]{2,1,0:T(8,128)S(1)} all-to-all(f32[8,80,128]{2,1,0:T(8,128)S(1)} %get-tuple-element.86), channel_id=1, replica_groups={{0,8,16,24,32,40,48,56},{4,12,20,28,36,44,52,60},{1,9,17,25,33,41,49,57..., dimensions={0} | all-to-all | bytes 655360 | tf_op jit(solution)/shard_map/all_to_all | solution.py:516
  105.6 0.0 copy-done
  105.6 1.0 back_fold_kernel.1
  106.6 3.5 %all-to-all-start.5 = ((f32[8,64,128]{2,1,0:T(8,128)}), f32[8,64,128]{2,1,0:T(8,128)S(1)}, u32[]{:S(2)}, u32[]{:S(2)}) async-start(f32[8,64,128]{2,1,0:T(8,128)} %back_fold_kernel.1), calls=%async_computation.5 | async-start | bytes 524288 | tf_op jit(solution)/shard_map/all_to_all | solution.py:511
  110.2 0.0 copy-start.7
  110.2 0.7 copy-done.7
  110.9 1.7 %prompt_mid_kernel.1 = (f32[8,128,128]{2,1,0:T(8,128)S(1)}, f32[8,16,128]{2,1,0:T(8,128)S(1)}, bf16[1,128,8,128]{3,2,1,0:T(8,128)(2,1)}) custom-call(f32[8,80,128]{2,1,0:T(8,128)S(1)} %all_to_all.38.received, f32[8,128]{1,0:T(8,128)S(1)} %get-tuple-element.61.blocks, f32[64,128]{1,0:T(8,128)S(1)} %copy-done.5, bf16[256,128]{1,0:T(8,128)(2,1)S(1)} %get-tuple-element.64.query, ...), custom_call_target="tpu_custom_call" | custom-call | flops 33554432 | bytes 2383872 | tf_op jit(solution)/shard_map/prompt_mid_kernel/pallas_call | solution.py:495
  112.6 2.3 %collective-permute-start.4 = (f32[8,16,128]{2,1,0:T(8,128)S(1)}, f32[8,16,128]{2,1,0:T(8,128)S(1)}, u32[]{:S(2)}, u32[]{:S(2)}) collective-permute-start(f32[8,16,128]{2,1,0:T(8,128)S(1)} %get-tuple-element.93), channel_id=1, source_target_pairs={{0,4},{4,0},{8,12},{12,8},{16,20},{20,16},{24,28},{28,24},{32,36},... | collective-permute-start | bytes 196616 | tf_op jit(solution)/shard_map/ppermute | solution.py:520
  114.9 0.9 collective-permute-done.4.swapped
  115.8 6.6 %all-to-all-done.5.rows_received = f32[8,64,128]{2,1,0:T(8,128)S(1)} async-done(((f32[8,64,128]{2,1,0:T(8,128)}), f32[8,64,128]{2,1,0:T(8,128)S(1)}, u32[]{:S(2)}, u32[]{:S(2)}) %all-to-all-start.5) | async-done | bytes 262176 | tf_op jit(solution)/shard_map/all_to_all | solution.py:511
  122.4 0.3 prompt_back_kernel.1
  122.7 19.8 %all_to_all.39.received = f32[8,128,128]{2,1,0:T(8,128)S(1)} all-to-all(f32[8,128,128]{2,1,0:T(8,128)S(1)} %prompt_back_kernel.1), channel_id=1, replica_groups={{0,8,16,24,32,40,48,56},{4,12,20,28,36,44,52,60},{1,9,17,25,33,41,49,57..., dimensions={0} | all-to-all | bytes 1048576 | tf_op jit(solution)/shard_map/all_to_all | solution.py:516
  142.5 0.1 back_spread_kernel.1
  142.6 3.1 %collective-permute-start.5 = (f32[8,88,128]{2,1,0:T(8,128)S(1)}, f32[8,88,128]{2,1,0:T(8,128)S(1)}, u32[]{:S(2)}, u32[]{:S(2)}) collective-permute-start(f32[8,88,128]{2,1,0:T(8,128)S(1)} %get-tuple-element.97), channel_id=1, source_target_pairs={{0,4},{4,0},{8,12},{12,8},{16,20},{20,16},{24,28},{28,24},{32,36},... | collective-permute-start | bytes 1081352 | tf_op jit(solution)/shard_map/ppermute | solution.py:520
  145.7 1.3 collective-permute-done.5.other
  146.9 1.5 %end_kernel.1 = (bf16[1,128,8,128]{3,2,1,0:T(8,128)(2,1)}, bf16[1,128,8,128]{3,2,1,0:T(8,128)(2,1)}, bf16[16,8,128]{2,1,0:T(8,128)(2,1)}, bf16[16,8,128]{2,1,0:T(8,128)(2,1)}, bf16[16,8,128]{2,1,0:T(8,128)(2,1)}) custom-call(f32[8,128,128]{2,1,0:T(8,128)S(1)} %all_to_all.39.received, f32[8,88,128]{2,1,0:T(8,128)S(1)} %get-tuple-element.96.mine, ...), custom_call_target="tpu_custom_call" | custom-call | flops 134217728 | bytes 5767168 | tf_op jit(solution)/shard_map/end_kernel/pallas_call | solution.py:495
  (7 shorter events, 0.0 us)
Async XLA Ops:
  3.0 10.1 %collective-permute-start = (f32[8,96,128]{2,1,0:T(8,128)S(1)}, f32[8,96,128]{2,1,0:T(8,128)S(1)}, u32[]{:S(2)}, u32[]{:S(2)}) collective-permute-start(f32[8,96,128]{2,1,0:T(8,128)S(1)} %get-tuple-element.57), channel_id=1, source_target_pairs={{0,4},{4,0},{8,12},{12,8},{16,20},{20,16},{24,28},{28,24},{32,36},... | collective-permute-start | bytes 1179656 | tf_op jit(solution)/shard_map/ppermute | solution.py:520
  35.1 12.1 %copy-start.2 = (f32[1,8,128]{2,1,0:T(8,128)S(1)}, f32[1,8,128]{2,1,0:T(8,128)}, u32[]{:S(2)}) copy-start(f32[1,8,128]{2,1,0:T(8,128)} %decay.5) | copy-start | bytes 12292
  35.2 12.1 %copy-start.3 = (bf16[16,8,128]{2,1,0:T(8,128)(2,1)S(1)}, bf16[16,8,128]{2,1,0:T(8,128)(2,1)}, u32[]{:S(2)}) copy-start(bf16[16,8,128]{2,1,0:T(8,128)(2,1)} %prompt_grad.1) | copy-start | bytes 98308
  35.2 19.0 %all-to-all-start.1 = ((f32[8,72,128]{2,1,0:T(8,128)}), f32[8,72,128]{2,1,0:T(8,128)S(1)}, u32[]{:S(2)}, u32[]{:S(2)}) async-start(f32[8,72,128]{2,1,0:T(8,128)} %get-tuple-element.60), calls=%async_computation.1 | async-start | bytes 589824 | tf_op jit(solution)/shard_map/all_to_all | solution.py:511
  43.6 3.6 %copy-start.8 = (bf16[8,128]{1,0:T(8,128)(2,1)S(1)}, bf16[8,128]{1,0:T(8,128)(2,1)}, u32[]{:S(2)}) copy-start(bf16[8,128]{1,0:T(8,128)(2,1)} %gain.1) | copy-start | bytes 6148
  43.6 5.2 %collective-permute-start.1 = (f32[8,16,128]{2,1,0:T(8,128)S(1)}, f32[8,16,128]{2,1,0:T(8,128)S(1)}, u32[]{:S(2)}, u32[]{:S(2)}) collective-permute-start(f32[8,16,128]{2,1,0:T(8,128)S(1)} %get-tuple-element.62), channel_id=1, source_target_pairs={{0,4},{4,0},{8,12},{12,8},{16,20},{20,16},{24,28},{28,24},{32,36},... | collective-permute-start | bytes 196616 | tf_op jit(solution)/shard_map/ppermute | solution.py:520
  49.2 5.3 %copy-start.6 = (f32[8,256]{1,0:T(8,128)}, f32[8,256]{1,0:T(8,128)S(1)}, u32[]{:S(2)}) copy-start(f32[8,256]{1,0:T(8,128)S(1)} %get-tuple-element.91.line) | copy-start | bytes 24580
  54.5 12.4 %copy-start.4 = (f32[64,128]{1,0:T(8,128)}, f32[64,128]{1,0:T(8,128)S(1)}, u32[]{:S(2)}) copy-start(f32[64,128]{1,0:T(8,128)S(1)} %get-tuple-element.88.start) | copy-start | bytes 98308
  66.9 7.3 %collective-permute-start.2 = (f32[8,72,128]{2,1,0:T(8,128)S(1)}, f32[8,72,128]{2,1,0:T(8,128)S(1)}, u32[]{:S(2)}, u32[]{:S(2)}) collective-permute-start(f32[8,72,128]{2,1,0:T(8,128)S(1)} %get-tuple-element.72), channel_id=1, source_target_pairs={{0,4},{4,0},{8,12},{12,8},{16,20},{20,16},{24,28},{28,24},{32,36},... | collective-permute-start | bytes 884744 | tf_op jit(solution)/shard_map/ppermute | solution.py:520
  83.7 5.7 %collective-permute-start.3 = (f32[8,72,128]{2,1,0:T(8,128)S(1)}, f32[8,72,128]{2,1,0:T(8,128)S(1)}, u32[]{:S(2)}, u32[]{:S(2)}) collective-permute-start(f32[8,72,128]{2,1,0:T(8,128)S(1)} %get-tuple-element.83), channel_id=1, source_target_pairs={{0,4},{4,0},{8,12},{12,8},{16,20},{20,16},{24,28},{28,24},{32,36},... | collective-permute-start | bytes 884744 | tf_op jit(solution)/shard_map/ppermute | solution.py:520
  89.4 16.3 %copy-start = (f32[8,128,128]{2,1,0:T(8,128)}, f32[8,128,128]{2,1,0:T(8,128)S(1)}, u32[]{:S(2)}) copy-start(f32[8,128,128]{2,1,0:T(8,128)S(1)} %get-tuple-element.99.value_local) | copy-start | bytes 1572868
  106.6 3.6 %copy-start.5 = (f32[64,128]{1,0:T(8,128)S(1)}, f32[64,128]{1,0:T(8,128)}, u32[]{:S(2)}) copy-start(f32[64,128]{1,0:T(8,128)} %copy-done.4) | copy-start | bytes 98308
  106.6 15.8 %all-to-all-start.5 = ((f32[8,64,128]{2,1,0:T(8,128)}), f32[8,64,128]{2,1,0:T(8,128)S(1)}, u32[]{:S(2)}, u32[]{:S(2)}) async-start(f32[8,64,128]{2,1,0:T(8,128)} %back_fold_kernel.1), calls=%async_computation.5 | async-start | bytes 524288 | tf_op jit(solution)/shard_map/all_to_all | solution.py:511
  110.2 0.7 copy-start.7
  112.6 3.2 %collective-permute-start.4 = (f32[8,16,128]{2,1,0:T(8,128)S(1)}, f32[8,16,128]{2,1,0:T(8,128)S(1)}, u32[]{:S(2)}, u32[]{:S(2)}) collective-permute-start(f32[8,16,128]{2,1,0:T(8,128)S(1)} %get-tuple-element.93), channel_id=1, source_target_pairs={{0,4},{4,0},{8,12},{12,8},{16,20},{20,16},{24,28},{28,24},{32,36},... | collective-permute-start | bytes 196616 | tf_op jit(solution)/shard_map/ppermute | solution.py:520
  142.5 4.4 %copy-start.1 = (f32[8,128,128]{2,1,0:T(8,128)S(1)}, f32[8,128,128]{2,1,0:T(8,128)}, u32[]{:S(2)}) copy-start(f32[8,128,128]{2,1,0:T(8,128)} %copy-done) | copy-start | bytes 1572868
  142.6 4.4 %collective-permute-start.5 = (f32[8,88,128]{2,1,0:T(8,128)S(1)}, f32[8,88,128]{2,1,0:T(8,128)S(1)}, u32[]{:S(2)}, u32[]{:S(2)}) collective-permute-start(f32[8,88,128]{2,1,0:T(8,128)S(1)} %get-tuple-element.97), channel_id=1, source_target_pairs={{0,4},{4,0},{8,12},{12,8},{16,20},{20,16},{24,28},{28,24},{32,36},... | collective-permute-start | bytes 1081352 | tf_op jit(solution)/shard_map/ppermute | solution.py:520

commit v7 on v6

--- a/solution.py
+++ b/solution.py
@@ -121,6 +121,16 @@
     return in_order(first, last)
 
 
+def half_lanes(x, other_core):
+    x = x.astype(F32)
+    own, other = choose(x[:, 0:HALF], x[:, HALF:D])
+    return (other if other_core else own).astype(BF16)
+
+
+def wide_columns(columns):
+    return jnp.concatenate([columns, jnp.zeros((T, D - HEADS), F32)], axis=1)
+
+
 def start_copies(pairs, sems):
     copies = [pltpu.make_async_copy(source, target, sems.at[i]) for i, (source, target) in enumerate(pairs)]
     for copy in copies:
@@ -130,7 +140,7 @@
 
 def send_kernel(
     lengths, key, value, decay, prompt_query, prompt_key, prompt_value, prompt_decay,
-    mine, theirs, query_out, key_out, value_out,
+    mine_prompt, theirs, query_out, key_out, value_out, to_end_out,
     key_in, value_in, decay_in, query_in, prompt_key_in, prompt_value_in, prompt_decay_in,
     rows_k, rows_v, prompt_q, prompt_k, prompt_v, sems,
 ):
@@ -162,10 +172,11 @@
         query_out[h] = prompt_q[pl.ds(h, PT, HEADS), :]
         k = prompt_k[pl.ds(h, PT, HEADS), :]
         v = prompt_v[pl.ds(h, PT, HEADS), :]
-        for ref, half in zip((mine, theirs), choose(pack(v, 0), pack(v, 1))):
-            ref[h, 64:80, :] = k
-            ref[h, 80:88, :] = half
-            ref[h, 88:96, :] = tail
+        own, sent = choose(pack(v, 0), pack(v, 1))
+        for ref, row, half in ((mine_prompt, 0, own), (theirs, 64, sent)):
+            ref[h, row : row + 16, :] = k
+            ref[h, row + 16 : row + 24, :] = half
+            ref[h, row + 24 : row + 32, :] = tail
     for copy in copies[5:]:
         copy.wait()
     rows_v[...] = value_in[0].astype(F32).reshape(T * HEADS, D)
@@ -175,15 +186,30 @@
         v = jnp.where(live, rows_v[pl.ds(h, T, HEADS), :], 0.0).astype(BF16)
         key_out[h] = k.astype(BF16)
         value_out[h] = v
-        state = dot_right(v, k * to_end[:, h : h + 1], 0, 0)
-        for ref, half in zip((mine, theirs), choose(state[0:64], state[64:128])):
-            ref[h, 0:64, :] = half
-
-
-def merge_kernel(mine, other, query, out, first_out, totals_out):
+        theirs[h, 0:64, :] = dot_right(half_lanes(v, other_core=True), k * to_end[:, h : h + 1], 0, 0)
+    to_end_out[...] = wide_columns(to_end)
+
+
+def own_half_kernel(key, value, to_end, mine):
+    for h in range(HEADS):
+        weighted = key[h].astype(F32) * to_end[:, h : h + 1]
+        mine[h] = dot_right(half_lanes(value[h], other_core=False), weighted, 0, 0)
+
+
+def reply_masks_kernel(weights, value, decay, after_fold, mask_out, local_out):
+    del after_fold
+    lines = running_rows(decay[0])
+    columns = running_columns(decay[0])
+    for h in range(HEADS):
+        mask_out[h] = masking(columns[:, h : h + 1], lines[h : h + 1])
+        local_out[h] = dot(weights[h], value[h], 1, 0)
+
+
+def merge_kernel(mine_state, mine_prompt, other, query, out, first_out, totals_out):
     at = iota((8, D), 0)
     for h in range(HEADS):
-        first, last = in_order(mine[h], other[h])
+        mine = jnp.concatenate([mine_state[h], mine_prompt[h]], axis=0)
+        first, last = in_order(mine, other[h])
         totals_out[h : h + 1, :] = first[89:90]
         totals_out[HEADS + h : HEADS + h + 1, :] = last[89:90]
         first_out[h] = first[0:64]
@@ -195,10 +221,6 @@
         tile = jnp.where(at == 0, first[88:89], jnp.where(at == 1, first[89:90], 0.0))
         out[h, 112:120, :] = jnp.where(at == 2, last[88:89], jnp.where(at == 3, last[89:90], tile))
         out[h, 120:136, :] = query[h]
-
-
-def wide_columns(columns):
-    return jnp.concatenate([columns, jnp.zeros((T, D - HEADS), F32)], axis=1)
 
 
 def reply_local_kernel(
@@ -315,7 +337,7 @@
 
 
 def output_kernel(
-    mine, other, query, weights, value, grad, growth, scale, prompt_upstream, out, output_out, prompt_out
+    mine, other, query, local, grad, growth, scale, prompt_upstream, out, output_out, prompt_out
 ):
     squares = jnp.zeros((T, D), F32)
     crossed = jnp.zeros((T, D), F32)
@@ -324,7 +346,7 @@
     for h in range(HEADS):
         low, high = in_order(mine[h], other[h])
         state = jnp.concatenate([low[0:64], high[0:64]], axis=0)
-        outputs = dot(weights[h], value[h], 1, 0) + growth[:, h : h + 1] * dot_right(query[h], state, 1, 1)
+        outputs = local[h] + growth[:, h : h + 1] * dot_right(query[h], state, 1, 1)
         output_out[h] = outputs
         upstream = grad[h].astype(F32) * scale[h : h + 1, :]
         squares = squares + outputs * outputs
@@ -378,18 +400,13 @@
 
 
 def reply_back_kernel(
-    mine, other, out_grad, query, key, value, weights, decay, query_grad, key_local, value_local, to_end_out
-):
-    lines = running_rows(decay[0])
-    columns = running_columns(decay[0])
-    scales = jnp.exp(columns)
-    to_end_out[...] = wide_columns(jnp.exp(columns[T - 1 : T, :] - columns))
+    mine, other, out_grad, query, key, value, weights, masks, growth, query_grad, key_local, value_local
+):
     for h in range(HEADS):
         state = jnp.concatenate(in_order(mine[h, 0:64, :], other[h, 0:64, :]), axis=0)
         og = out_grad[h]
-        mask = masking(columns[:, h : h + 1], lines[h : h + 1])
-        mix = (dot(og, value[h], 1, 1) * mask).astype(BF16)
-        query_grad[h] = dot(mix, key[h], 1, 0) + scales[:, h : h + 1] * dot_right(og, state, 1, 0)
+        mix = (dot(og, value[h], 1, 1) * masks[h]).astype(BF16)
+        query_grad[h] = dot(mix, key[h], 1, 0) + growth[:, h : h + 1] * dot_right(og, state, 1, 0)
         key_local[h] = dot(mix, query[h], 0, 0)
         value_local[h] = dot(weights[h], og, 0, 0)
 
@@ -536,9 +553,16 @@
 ):
     work = 8 * 2 * T * D * D
     reply_in, prompt_in = pltpu.VMEM(*REPLY), pltpu.VMEM(*PROMPT)
-    mine, theirs, own_query, key, value = run(
+    own_prompt, theirs, own_query, key, value, to_end = run(
         send_kernel,
-        [((HEADS, 96, D), F32), ((HEADS, 96, D), F32), ((HEADS, PT, D), F32), BY_HEAD, BY_HEAD],
+        [
+            ((HEADS, 32, D), F32),
+            ((HEADS, 96, D), F32),
+            ((HEADS, PT, D), F32),
+            BY_HEAD,
+            BY_HEAD,
+            ((T, D), F32),
+        ],
         [reply_in, reply_in, pltpu.VMEM((1, HEADS, T), F32)]
         + [prompt_in] * 3
         + [pltpu.VMEM((HEADS, PT), F32)]
@@ -555,14 +579,19 @@
         prompt_decay,
         hbm=range(1, 8),
         flops=2 * work,
-        kept=(0, 2, 3, 4),
+        kept=(0, 2, 3, 4, 5),
+    )
+    other = swap_cores(theirs)
+    (own_state,) = run(
+        own_half_kernel, [((HEADS, HALF, D), F32)], [], key, value, to_end, flops=work, kept=(0,)
     )
     sent, first_state, block_totals = run(
         merge_kernel,
         [((HEADS, 136, D), F32), ((HEADS, HALF, D), F32), ((2 * HEADS, D), F32)],
         [],
-        mine,
-        swap_cores(theirs),
+        own_state,
+        own_prompt,
+        other,
         own_query,
         kept=(1, 2),
     )
@@ -629,6 +658,17 @@
         kept=(0,),
     )
     other = swap_cores(theirs)
+    masks, local = run(
+        reply_masks_kernel,
+        [BY_HEAD_WIDE, BY_HEAD_WIDE],
+        [],
+        weights,
+        value,
+        reply_decay,
+        mine,
+        flops=work,
+        kept=(0, 1),
+    )
     sent, outputs, prompt_outputs = run(
         output_kernel,
         [((HEAD_AXIS, 8, D), F32), BY_HEAD_WIDE, ((HEADS, PT, D), F32)],
@@ -636,8 +676,7 @@
         mine,
         other,
         query,
-        weights,
-        value,
+        local,
         grad,
         growth,
         scale,
@@ -662,9 +701,9 @@
         kept=(0, 2),
     )
     back_other = swap_cores(back_theirs)
-    reply_query_wide, key_local, value_local, to_end = run(
+    reply_query_wide, key_local, value_local = run(
         reply_back_kernel,
-        [BY_HEAD_WIDE, BY_HEAD_WIDE, BY_HEAD_WIDE, ((T, D), F32)],
+        [BY_HEAD_WIDE, BY_HEAD_WIDE, BY_HEAD_WIDE],
         [],
         mine,
         other,
@@ -673,9 +712,10 @@
         key,
         value,
         weights,
-        reply_decay,
+        masks,
+        growth,
         flops=6 * work,
-        kept=(0, 1, 2, 3),
+        kept=(0, 1, 2),
     )
     sent, last_back = run(
         back_merge_kernel,
@@ -684,7 +724,7 @@
         back_mine,
         back_other,
         block_totals,
-        to_end,
+        reply_query_wide,
         kept=(1,),
     )
     backs = exchange_chips(sent)

time: 149 us -> 150 us (level)
    pallas_call x16 -> x18, Pallas kernels: 13.3 us -> 14.6 us  [run(): pl.pallas_call(kernel, out_shape=[pltpu.VMEM(shape, kind) if i in kept el...]
  transfers between devices with their start and end apart: 8 -> 8, of which waited for: 6 -> 6; matrix products, arithmetic and copies ran while one was open for 0% -> 0% of each run, Pallas kernels for 4% -> 5%
where the time goes in v7:
time: 150 us; the launch traced here: 149 us
  blocking collectives  77 us (51%)
  starting transfers between devices  39.7 us (26%)
  waiting for transfers between devices  14.9 us (10%)
  Pallas kernels  14.6 us (10%)
  between operations  1.51 us (1%)
    all_to_all x4, blocking collectives, exchange_chips(): return lax.all_to_all(x, 'ctx', 0, 0, axis_index_groups=groups, tiled=True)  69 us
    ppermute x6, starting transfers between devices, swap_cores(): return lax.ppermute(x, 'ctx', [(i, i ^ 1) for i in range(CTX)])  27.7 us
    pallas_call x18, Pallas kernels, run(): pl.pallas_call(kernel, out_shape=[pltpu.VMEM(shape, kind) if i in kept el...  14.6 us
    all_to_all x2, starting transfers between devices, exchange(): return lax.all_to_all(x, axis, 0, 0, tiled=True)  12 us
    all_to_all x2, waiting for transfers between devices, exchange(): return lax.all_to_all(x, axis, 0, 0, tiled=True)  11.6 us
    all_to_all x1, blocking collectives, exchange(): return lax.all_to_all(x, axis, 0, 0, tiled=True)  8.03 us
    ppermute x6, waiting for transfers between devices, swap_cores(): return lax.ppermute(x, 'ctx', [(i, i ^ 1) for i in range(CTX)])  3.32 us
  transfers between devices with their start and end apart: 8, of which 6 were waited for; matrix products, arithmetic and copies ran while one was open for 0% of the time, Pallas kernels for 5%

profile of v7, /device:TPU:1, one launch (start us, length us, event | category | flops | bytes accessed | tf_op | source)
XLA Modules:
  0.0 149.1 jit_solution(13744509160285387892)
XLA Ops:
  1.3 1.9 %send_kernel.1 = (f32[8,32,128]{2,1,0:T(8,128)S(1)}, f32[8,96,128]{2,1,0:T(8,128)S(1)}, f32[8,16,128]{2,1,0:T(8,128)S(1)}, bf16[8,128,128]{2,1,0:T(8,128)(2,1)S(...) custom-call(s32[1]{0:T(128)S(6)} %copy.18.lengths, bf16[1,128,8,128]{3,2,1,0:T(8,128)(2,1)} %key.1, ...), custom_call_target="tpu_custom_call" | custom-call | flops 67108864 | bytes 1254408 | tf_op jit(solution)/shard_map/send_kernel/pallas_call | solution.py:512
  3.2 0.0 copy-start.4
  3.2 8.8 %collective-permute-start = (f32[8,96,128]{2,1,0:T(8,128)S(1)}, f32[8,96,128]{2,1,0:T(8,128)S(1)}, u32[]{:S(2)}, u32[]{:S(2)}) collective-permute-start(f32[8,96,128]{2,1,0:T(8,128)S(1)} %get-tuple-element.62), channel_id=1, source_target_pairs={{0,4},{4,0},{8,12},{12,8},{16,20},{20,16},{24,28},{28,24},{32,36},... | collective-permute-start | bytes 1179656 | tf_op jit(solution)/shard_map/ppermute | solution.py:537
  12.0 0.9 own_half_kernel.1.mine_state
  12.9 0.0 copy-done.4
  13.0 0.4 collective-permute-done.other
  13.4 0.1 merge_kernel.1
  13.5 20.7 %all_to_all.35.received = f32[8,136,128]{2,1,0:T(8,128)S(1)} all-to-all(f32[8,136,128]{2,1,0:T(8,128)S(1)} %get-tuple-element.64), channel_id=1, replica_groups={{0,8,16,24,32,40,48,56},{4,12,20,28,36,44,52,60},{1,9,17,25,33,41,49,57..., dimensions={0} | all-to-all | bytes 1114112 | tf_op jit(solution)/shard_map/all_to_all | solution.py:533
  34.1 1.2 prompt_row_kernel.1
  35.4 8.5 %all-to-all-start.1 = ((f32[8,72,128]{2,1,0:T(8,128)}), f32[8,72,128]{2,1,0:T(8,128)S(1)}, u32[]{:S(2)}, u32[]{:S(2)}) async-start(f32[8,72,128]{2,1,0:T(8,128)} %get-tuple-element.65), calls=%async_computation.1 | async-start | bytes 589824 | tf_op jit(solution)/shard_map/all_to_all | solution.py:528
  43.8 3.6 %collective-permute-start.1 = (f32[8,16,128]{2,1,0:T(8,128)S(1)}, f32[8,16,128]{2,1,0:T(8,128)S(1)}, u32[]{:S(2)}, u32[]{:S(2)}) collective-permute-start(f32[8,16,128]{2,1,0:T(8,128)S(1)} %get-tuple-element.67), channel_id=1, source_target_pairs={{0,4},{4,0},{8,12},{12,8},{16,20},{20,16},{24,28},{28,24},{32,36},... | collective-permute-start | bytes 196616 | tf_op jit(solution)/shard_map/ppermute | solution.py:537
  47.4 0.0 copy-done.6
  47.4 0.0 copy-done.7
  47.5 0.0 copy-done.10
  47.5 1.5 %reply_local_kernel.1 = (bf16[8,128,128]{2,1,0:T(8,128)(2,1)S(1)}, bf16[8,128,128]{2,1,0:T(8,128)(2,1)S(1)}, bf16[8,128,128]{2,1,0:T(8,128)(2,1)S(1)}, f32[128,1...) custom-call(s32[1]{0:T(128)S(6)} %copy.18.lengths, bf16[1,128,8,128]{3,2,1,0:T(8,128)(2,1)} %query.1, ...), custom_call_target="tpu_custom_call" | custom-call | flops 67108864 | bytes 1650696 | tf_op jit(solution)/shard_map/reply_local_kernel/pallas_call | solution.py:512
  49.0 0.0 collective-permute-done.1.other
  49.0 0.4 prompt_local_kernel.1
  49.4 0.0 copy-start.2
  49.4 0.6 copy-done.2
  50.0 4.3 %all-to-all-done.1.rows_received = f32[8,72,128]{2,1,0:T(8,128)S(1)} async-done(((f32[8,72,128]{2,1,0:T(8,128)}), f32[8,72,128]{2,1,0:T(8,128)S(1)}, u32[]{:S(2)}, u32[]{:S(2)}) %all-to-all-start.1) | async-done | bytes 294944 | tf_op jit(solution)/shard_map/all_to_all | solution.py:528
  54.4 0.3 fold_kernel.1
  54.7 0.0 copy-done.8
  54.7 12.4 %all_to_all.36.received = f32[8,80,128]{2,1,0:T(8,128)S(1)} all-to-all(f32[8,80,128]{2,1,0:T(8,128)S(1)} %get-tuple-element.72), channel_id=1, replica_groups={{0,8,16,24,32,40,48,56},{4,12,20,28,36,44,52,60},{1,9,17,25,33,41,49,57..., dimensions={0} | all-to-all | bytes 655360 | tf_op jit(solution)/shard_map/all_to_all | solution.py:533
  67.1 0.1 spread_kernel.1
  67.1 6.2 %collective-permute-start.2 = (f32[8,72,128]{2,1,0:T(8,128)S(1)}, f32[8,72,128]{2,1,0:T(8,128)S(1)}, u32[]{:S(2)}, u32[]{:S(2)}) collective-permute-start(f32[8,72,128]{2,1,0:T(8,128)S(1)} %get-tuple-element.76), channel_id=1, source_target_pairs={{0,4},{4,0},{8,12},{12,8},{16,20},{20,16},{24,28},{28,24},{32,36},... | collective-permute-start | bytes 884744 | tf_op jit(solution)/shard_map/ppermute | solution.py:537
  73.3 0.4 reply_masks_kernel.1
  73.7 0.8 collective-permute-done.2.other
  74.5 0.6 output_kernel.1
  75.1 8.0 %all_to_all.37.sums = f32[4,8,128]{2,1,0:T(8,128)S(1)} all-to-all(f32[4,8,128]{2,1,0:T(8,128)S(1)} %get-tuple-element.83), channel_id=1, replica_groups=mesh['sample'=8,'ctx'=16,'head'=4] {'head'}, dimensions={0} | all-to-all | bytes 32768 | tf_op jit(solution)/shard_map/all_to_all | solution.py:528
  83.1 0.7 grad_kernel.1
  83.8 3.7 %collective-permute-start.3 = (f32[8,72,128]{2,1,0:T(8,128)S(1)}, f32[8,72,128]{2,1,0:T(8,128)S(1)}, u32[]{:S(2)}, u32[]{:S(2)}) collective-permute-start(f32[8,72,128]{2,1,0:T(8,128)S(1)} %get-tuple-element.87), channel_id=1, source_target_pairs={{0,4},{4,0},{8,12},{12,8},{16,20},{20,16},{24,28},{28,24},{32,36},... | collective-permute-start | bytes 884744 | tf_op jit(solution)/shard_map/ppermute | solution.py:537
  87.5 1.8 %reply_back_kernel.1 = (f32[8,128,128]{2,1,0:T(8,128)S(1)}, f32[8,128,128]{2,1,0:T(8,128)S(1)}, f32[8,128,128]{2,1,0:T(8,128)S(1)}) custom-call(f32[8,72,128]{2,1,0:T(8,128)S(1)} %get-tuple-element.75.after_fold.mine, f32[8,72,128]{2,1,0:T(8,128)S(1)} %collective-permute-done.2.other, bf16[8,128,128]{2,1,0:T(8,128)(2,1)S(1)} %get-tuple-element.88.out_grad, ...), custom_call_target="tpu_custom_call" | custom-call | flops 201326592 | bytes 4980736 | tf_op jit(solution)/shard_map/reply_back_kernel/pallas_call | solution.py:512
  89.4 0.0 collective-permute-done.3.other
  89.4 0.1 back_merge_kernel.1
  89.5 0.7 copy-done
  90.1 16.2 %all_to_all.38.received = f32[8,80,128]{2,1,0:T(8,128)S(1)} all-to-all(f32[8,80,128]{2,1,0:T(8,128)S(1)} %get-tuple-element.91), channel_id=1, replica_groups={{0,8,16,24,32,40,48,56},{4,12,20,28,36,44,52,60},{1,9,17,25,33,41,49,57..., dimensions={0} | all-to-all | bytes 655360 | tf_op jit(solution)/shard_map/all_to_all | solution.py:533
  106.3 1.0 back_fold_kernel.1
  107.3 3.5 %all-to-all-start.5 = ((f32[8,64,128]{2,1,0:T(8,128)}), f32[8,64,128]{2,1,0:T(8,128)S(1)}, u32[]{:S(2)}, u32[]{:S(2)}) async-start(f32[8,64,128]{2,1,0:T(8,128)} %back_fold_kernel.1), calls=%async_computation.5 | async-start | bytes 524288 | tf_op jit(solution)/shard_map/all_to_all | solution.py:528
  110.9 1.7 %prompt_mid_kernel.1 = (f32[8,128,128]{2,1,0:T(8,128)S(1)}, f32[8,16,128]{2,1,0:T(8,128)S(1)}, bf16[1,128,8,128]{3,2,1,0:T(8,128)(2,1)}) custom-call(f32[8,80,128]{2,1,0:T(8,128)S(1)} %all_to_all.38.received, f32[8,128]{1,0:T(8,128)S(1)} %get-tuple-element.66.blocks, f32[64,128]{1,0:T(8,128)S(1)} %get-tuple-element.93.start, ...), custom_call_target="tpu_custom_call" | custom-call | flops 33554432 | bytes 2383872 | tf_op jit(solution)/shard_map/prompt_mid_kernel/pallas_call | solution.py:512
  112.6 2.3 %collective-permute-start.4 = (f32[8,16,128]{2,1,0:T(8,128)S(1)}, f32[8,16,128]{2,1,0:T(8,128)S(1)}, u32[]{:S(2)}, u32[]{:S(2)}) collective-permute-start(f32[8,16,128]{2,1,0:T(8,128)S(1)} %get-tuple-element.97), channel_id=1, source_target_pairs={{0,4},{4,0},{8,12},{12,8},{16,20},{20,16},{24,28},{28,24},{32,36},... | collective-permute-start | bytes 196616 | tf_op jit(solution)/shard_map/ppermute | solution.py:537
  114.9 0.9 collective-permute-done.4.swapped
  115.8 7.2 %all-to-all-done.5.rows_received = f32[8,64,128]{2,1,0:T(8,128)S(1)} async-done(((f32[8,64,128]{2,1,0:T(8,128)}), f32[8,64,128]{2,1,0:T(8,128)S(1)}, u32[]{:S(2)}, u32[]{:S(2)}) %all-to-all-start.5) | async-done | bytes 262176 | tf_op jit(solution)/shard_map/all_to_all | solution.py:528
  123.0 0.3 prompt_back_kernel.1
  123.3 19.8 %all_to_all.39.received = f32[8,128,128]{2,1,0:T(8,128)S(1)} all-to-all(f32[8,128,128]{2,1,0:T(8,128)S(1)} %prompt_back_kernel.1), channel_id=1, replica_groups={{0,8,16,24,32,40,48,56},{4,12,20,28,36,44,52,60},{1,9,17,25,33,41,49,57..., dimensions={0} | all-to-all | bytes 1048576 | tf_op jit(solution)/shard_map/all_to_all | solution.py:533
  143.2 0.1 back_spread_kernel.1
  143.2 3.1 %collective-permute-start.5 = (f32[8,88,128]{2,1,0:T(8,128)S(1)}, f32[8,88,128]{2,1,0:T(8,128)S(1)}, u32[]{:S(2)}, u32[]{:S(2)}) collective-permute-start(f32[8,88,128]{2,1,0:T(8,128)S(1)} %get-tuple-element.101), channel_id=1, source_target_pairs={{0,4},{4,0},{8,12},{12,8},{16,20},{20,16},{24,28},{28,24},{32,36},... | collective-permute-start | bytes 1081352 | tf_op jit(solution)/shard_map/ppermute | solution.py:537
  146.3 1.3 collective-permute-done.5.other
  147.6 1.5 %end_kernel.1 = (bf16[1,128,8,128]{3,2,1,0:T(8,128)(2,1)}, bf16[1,128,8,128]{3,2,1,0:T(8,128)(2,1)}, bf16[16,8,128]{2,1,0:T(8,128)(2,1)}, bf16[16,8,128]{2,1,0:T(8,128)(2,1)}, bf16[16,8,128]{2,1,0:T(8,128)(2,1)}) custom-call(f32[8,128,128]{2,1,0:T(8,128)S(1)} %all_to_all.39.received, f32[8,88,128]{2,1,0:T(8,128)S(1)} %get-tuple-element.100.mine, ...), custom_call_target="tpu_custom_call" | custom-call | flops 134217728 | bytes 5767168 | tf_op jit(solution)/shard_map/end_kernel/pallas_call | solution.py:512
  (13 shorter events, 0.0 us)
Async XLA Ops:
  3.2 9.7 %copy-start.4 = (f32[128,128]{1,0:T(8,128)}, f32[128,128]{1,0:T(8,128)S(1)}, u32[]{:S(2)}) copy-start(f32[128,128]{1,0:T(8,128)S(1)} %get-tuple-element.60.to_end) | copy-start | bytes 196612
  3.2 10.1 %collective-permute-start = (f32[8,96,128]{2,1,0:T(8,128)S(1)}, f32[8,96,128]{2,1,0:T(8,128)S(1)}, u32[]{:S(2)}, u32[]{:S(2)}) collective-permute-start(f32[8,96,128]{2,1,0:T(8,128)S(1)} %get-tuple-element.62), channel_id=1, source_target_pairs={{0,4},{4,0},{8,12},{12,8},{16,20},{20,16},{24,28},{28,24},{32,36},... | collective-permute-start | bytes 1179656 | tf_op jit(solution)/shard_map/ppermute | solution.py:537
  35.3 12.1 %copy-start.6 = (f32[1,8,128]{2,1,0:T(8,128)S(1)}, f32[1,8,128]{2,1,0:T(8,128)}, u32[]{:S(2)}) copy-start(f32[1,8,128]{2,1,0:T(8,128)} %decay.5) | copy-start | bytes 12292
  35.4 12.1 %copy-start.7 = (bf16[16,8,128]{2,1,0:T(8,128)(2,1)S(1)}, bf16[16,8,128]{2,1,0:T(8,128)(2,1)}, u32[]{:S(2)}) copy-start(bf16[16,8,128]{2,1,0:T(8,128)(2,1)} %prompt_grad.1) | copy-start | bytes 98308
  35.4 12.1 %copy-start.10 = (bf16[8,128]{1,0:T(8,128)(2,1)S(1)}, bf16[8,128]{1,0:T(8,128)(2,1)}, u32[]{:S(2)}) copy-start(bf16[8,128]{1,0:T(8,128)(2,1)} %gain.1) | copy-start | bytes 6148
  35.4 19.0 %all-to-all-start.1 = ((f32[8,72,128]{2,1,0:T(8,128)}), f32[8,72,128]{2,1,0:T(8,128)S(1)}, u32[]{:S(2)}, u32[]{:S(2)}) async-start(f32[8,72,128]{2,1,0:T(8,128)} %get-tuple-element.65), calls=%async_computation.1 | async-start | bytes 589824 | tf_op jit(solution)/shard_map/all_to_all | solution.py:528
  43.8 5.2 %collective-permute-start.1 = (f32[8,16,128]{2,1,0:T(8,128)S(1)}, f32[8,16,128]{2,1,0:T(8,128)S(1)}, u32[]{:S(2)}, u32[]{:S(2)}) collective-permute-start(f32[8,16,128]{2,1,0:T(8,128)S(1)} %get-tuple-element.67), channel_id=1, source_target_pairs={{0,4},{4,0},{8,12},{12,8},{16,20},{20,16},{24,28},{28,24},{32,36},... | collective-permute-start | bytes 196616 | tf_op jit(solution)/shard_map/ppermute | solution.py:537
  49.4 0.6 copy-start.2
  50.0 4.6 %copy-start.8 = (f32[8,256]{1,0:T(8,128)}, f32[8,256]{1,0:T(8,128)S(1)}, u32[]{:S(2)}) copy-start(f32[8,256]{1,0:T(8,128)S(1)} %get-tuple-element.96.line) | copy-start | bytes 24580
  67.1 7.4 %collective-permute-start.2 = (f32[8,72,128]{2,1,0:T(8,128)S(1)}, f32[8,72,128]{2,1,0:T(8,128)S(1)}, u32[]{:S(2)}, u32[]{:S(2)}) collective-permute-start(f32[8,72,128]{2,1,0:T(8,128)S(1)} %get-tuple-element.76), channel_id=1, source_target_pairs={{0,4},{4,0},{8,12},{12,8},{16,20},{20,16},{24,28},{28,24},{32,36},... | collective-permute-start | bytes 884744 | tf_op jit(solution)/shard_map/ppermute | solution.py:537
  83.8 5.6 %collective-permute-start.3 = (f32[8,72,128]{2,1,0:T(8,128)S(1)}, f32[8,72,128]{2,1,0:T(8,128)S(1)}, u32[]{:S(2)}, u32[]{:S(2)}) collective-permute-start(f32[8,72,128]{2,1,0:T(8,128)S(1)} %get-tuple-element.87), channel_id=1, source_target_pairs={{0,4},{4,0},{8,12},{12,8},{16,20},{20,16},{24,28},{28,24},{32,36},... | collective-permute-start | bytes 884744 | tf_op jit(solution)/shard_map/ppermute | solution.py:537
  89.4 0.8 copy-start
  107.3 3.6 %copy-start.3 = (bf16[256,64]{1,0:T(8,128)(2,1)S(1)}, bf16[256,64]{1,0:T(8,128)(2,1)}, u32[]{:S(2)}) copy-start(bf16[256,64]{1,0:T(8,128)(2,1)} %copy-done.2) | copy-start | bytes 98308
  107.3 3.6 %copy-start.9 = (f32[8,256]{1,0:T(8,128)S(1)}, f32[8,256]{1,0:T(8,128)}, u32[]{:S(2)}) copy-start(f32[8,256]{1,0:T(8,128)} %copy-done.8) | copy-start | bytes 24580
  107.3 15.8 %all-to-all-start.5 = ((f32[8,64,128]{2,1,0:T(8,128)}), f32[8,64,128]{2,1,0:T(8,128)S(1)}, u32[]{:S(2)}, u32[]{:S(2)}) async-start(f32[8,64,128]{2,1,0:T(8,128)} %back_fold_kernel.1), calls=%async_computation.5 | async-start | bytes 524288 | tf_op jit(solution)/shard_map/all_to_all | solution.py:528
  112.6 3.2 %collective-permute-start.4 = (f32[8,16,128]{2,1,0:T(8,128)S(1)}, f32[8,16,128]{2,1,0:T(8,128)S(1)}, u32[]{:S(2)}, u32[]{:S(2)}) collective-permute-start(f32[8,16,128]{2,1,0:T(8,128)S(1)} %get-tuple-element.97), channel_id=1, source_target_pairs={{0,4},{4,0},{8,12},{12,8},{16,20},{20,16},{24,28},{28,24},{32,36},... | collective-permute-start | bytes 196616 | tf_op jit(solution)/shard_map/ppermute | solution.py:537
  143.2 4.4 %copy-start.1 = (f32[8,128,128]{2,1,0:T(8,128)S(1)}, f32[8,128,128]{2,1,0:T(8,128)}, u32[]{:S(2)}) copy-start(f32[8,128,128]{2,1,0:T(8,128)} %copy-done) | copy-start | bytes 1572868
  143.2 4.4 %copy-start.5 = (f32[128,128]{1,0:T(8,128)S(1)}, f32[128,128]{1,0:T(8,128)}, u32[]{:S(2)}) copy-start(f32[128,128]{1,0:T(8,128)} %copy-done.4) | copy-start | bytes 196612
  143.2 4.4 %collective-permute-start.5 = (f32[8,88,128]{2,1,0:T(8,128)S(1)}, f32[8,88,128]{2,1,0:T(8,128)S(1)}, u32[]{:S(2)}, u32[]{:S(2)}) collective-permute-start(f32[8,88,128]{2,1,0:T(8,128)S(1)} %get-tuple-element.101), channel_id=1, source_target_pairs={{0,4},{4,0},{8,12},{12,8},{16,20},{20,16},{24,28},{28,24},{32,36},... | collective-permute-start | bytes 1081352 | tf_op jit(solution)/shard_map/ppermute | solution.py:537

commit v8 on v6

--- a/solution.py
+++ b/solution.py
@@ -178,6 +178,15 @@
         state = dot_right(v, k * to_end[:, h : h + 1], 0, 0)
         for ref, half in zip((mine, theirs), choose(state[0:64], state[64:128])):
             ref[h, 0:64, :] = half
+
+
+def reply_masks_kernel(weights, value, decay, after_fold, mask_out, local_out):
+    del after_fold
+    lines = running_rows(decay[0])
+    columns = running_columns(decay[0])
+    for h in range(HEADS):
+        mask_out[h] = masking(columns[:, h : h + 1], lines[h : h + 1])
+        local_out[h] = dot(weights[h], value[h], 1, 0)
 
 
 def merge_kernel(mine, other, query, out, first_out, totals_out):
@@ -315,7 +324,7 @@
 
 
 def output_kernel(
-    mine, other, query, weights, value, grad, growth, scale, prompt_upstream, out, output_out, prompt_out
+    mine, other, query, local, grad, growth, scale, prompt_upstream, out, output_out, prompt_out
 ):
     squares = jnp.zeros((T, D), F32)
     crossed = jnp.zeros((T, D), F32)
@@ -324,7 +333,7 @@
     for h in range(HEADS):
         low, high = in_order(mine[h], other[h])
         state = jnp.concatenate([low[0:64], high[0:64]], axis=0)
-        outputs = dot(weights[h], value[h], 1, 0) + growth[:, h : h + 1] * dot_right(query[h], state, 1, 1)
+        outputs = local[h] + growth[:, h : h + 1] * dot_right(query[h], state, 1, 1)
         output_out[h] = outputs
         upstream = grad[h].astype(F32) * scale[h : h + 1, :]
         squares = squares + outputs * outputs
@@ -378,18 +387,16 @@
 
 
 def reply_back_kernel(
-    mine, other, out_grad, query, key, value, weights, decay, query_grad, key_local, value_local, to_end_out
-):
-    lines = running_rows(decay[0])
+    mine, other, out_grad, query, key, value, weights, masks, growth, decay,
+    query_grad, key_local, value_local, to_end_out,
+):
     columns = running_columns(decay[0])
-    scales = jnp.exp(columns)
     to_end_out[...] = wide_columns(jnp.exp(columns[T - 1 : T, :] - columns))
     for h in range(HEADS):
         state = jnp.concatenate(in_order(mine[h, 0:64, :], other[h, 0:64, :]), axis=0)
         og = out_grad[h]
-        mask = masking(columns[:, h : h + 1], lines[h : h + 1])
-        mix = (dot(og, value[h], 1, 1) * mask).astype(BF16)
-        query_grad[h] = dot(mix, key[h], 1, 0) + scales[:, h : h + 1] * dot_right(og, state, 1, 0)
+        mix = (dot(og, value[h], 1, 1) * masks[h]).astype(BF16)
+        query_grad[h] = dot(mix, key[h], 1, 0) + growth[:, h : h + 1] * dot_right(og, state, 1, 0)
         key_local[h] = dot(mix, query[h], 0, 0)
         value_local[h] = dot(weights[h], og, 0, 0)
 
@@ -629,6 +636,17 @@
         kept=(0,),
     )
     other = swap_cores(theirs)
+    masks, local = run(
+        reply_masks_kernel,
+        [BY_HEAD_WIDE, BY_HEAD_WIDE],
+        [],
+        weights,
+        value,
+        reply_decay,
+        mine,
+        flops=work,
+        kept=(0, 1),
+    )
     sent, outputs, prompt_outputs = run(
         output_kernel,
         [((HEAD_AXIS, 8, D), F32), BY_HEAD_WIDE, ((HEADS, PT, D), F32)],
@@ -636,8 +654,7 @@
         mine,
         other,
         query,
-        weights,
-        value,
+        local,
         grad,
         growth,
         scale,
@@ -673,6 +690,8 @@
         key,
         value,
         weights,
+        masks,
+        growth,
         reply_decay,
         flops=6 * work,
         kept=(0, 1, 2, 3),

time: 149 us -> 149 us (level)
    pallas_call x16 -> x17, Pallas kernels: 13.3 us -> 13.6 us  [run(): pl.pallas_call(kernel, out_shape=[pltpu.VMEM(shape, kind) if i in kept el...]
where the time goes in v8:
time: 149 us; the launch traced here: 148 us
  blocking collectives  77 us (52%)
  starting transfers between devices  39.7 us (27%)
  waiting for transfers between devices  15.1 us (10%)
  Pallas kernels  13.6 us (9%)
  between operations  1.51 us (1%)
    all_to_all x4, blocking collectives, exchange_chips(): return lax.all_to_all(x, 'ctx', 0, 0, axis_index_groups=groups, tiled=True)  69 us
    ppermute x6, starting transfers between devices, swap_cores(): return lax.ppermute(x, 'ctx', [(i, i ^ 1) for i in range(CTX)])  27.7 us
    pallas_call x17, Pallas kernels, run(): pl.pallas_call(kernel, out_shape=[pltpu.VMEM(shape, kind) if i in kept el...  13.6 us
    all_to_all x2, starting transfers between devices, exchange(): return lax.all_to_all(x, axis, 0, 0, tiled=True)  12 us
    all_to_all x2, waiting for transfers between devices, exchange(): return lax.all_to_all(x, axis, 0, 0, tiled=True)  10.9 us
    all_to_all x1, blocking collectives, exchange(): return lax.all_to_all(x, axis, 0, 0, tiled=True)  8.02 us
    ppermute x6, waiting for transfers between devices, swap_cores(): return lax.ppermute(x, 'ctx', [(i, i ^ 1) for i in range(CTX)])  4.24 us
  transfers between devices with their start and end apart: 8, of which 6 were waited for; matrix products, arithmetic and copies ran while one was open for 0% of the time, Pallas kernels for 4%

profile of v8, /device:TPU:1, one launch (start us, length us, event | category | flops | bytes accessed | tf_op | source)
XLA Modules:
  0.0 148.3 jit_solution(169424591410613036)
XLA Ops:
  1.3 1.8 %send_kernel.1 = (f32[8,96,128]{2,1,0:T(8,128)S(1)}, f32[8,96,128]{2,1,0:T(8,128)S(1)}, f32[8,16,128]{2,1,0:T(8,128)S(1)}, bf16[8,128,128]{2,1,0:T(8,128)(2,1)S(1)}, bf16[8,128,128]{2,1,0:T(8,128)(2,1)S(1)}) custom-call(s32[1]{0:T(128)S(6)} %copy.18.lengths, bf16[1,128,8,128]{3,2,1,0:T(8,128)(2,1)} %key.1, bf16[1,128,8,128]{3,2,1,0:T(8,128)(2,1)} %value.1, ...), custom_call_target="tpu_custom_call" | custom-call | flops 67108864 | bytes 1254408 | tf_op jit(solution)/shard_map/send_kernel/pallas_call | solution.py:502
  3.0 8.8 %collective-permute-start = (f32[8,96,128]{2,1,0:T(8,128)S(1)}, f32[8,96,128]{2,1,0:T(8,128)S(1)}, u32[]{:S(2)}, u32[]{:S(2)}) collective-permute-start(f32[8,96,128]{2,1,0:T(8,128)S(1)} %get-tuple-element.59), channel_id=1, source_target_pairs={{0,4},{4,0},{8,12},{12,8},{16,20},{20,16},{24,28},{28,24},{32,36},... | collective-permute-start | bytes 1179656 | tf_op jit(solution)/shard_map/ppermute | solution.py:527
  11.8 1.3 collective-permute-done.other
  13.2 0.1 merge_kernel.1
  13.3 20.7 %all_to_all.35.received = f32[8,136,128]{2,1,0:T(8,128)S(1)} all-to-all(f32[8,136,128]{2,1,0:T(8,128)S(1)} %get-tuple-element.61), channel_id=1, replica_groups={{0,8,16,24,32,40,48,56},{4,12,20,28,36,44,52,60},{1,9,17,25,33,41,49,57..., dimensions={0} | all-to-all | bytes 1114112 | tf_op jit(solution)/shard_map/all_to_all | solution.py:523
  33.9 1.2 prompt_row_kernel.1
  35.2 8.5 %all-to-all-start.1 = ((f32[8,72,128]{2,1,0:T(8,128)}), f32[8,72,128]{2,1,0:T(8,128)S(1)}, u32[]{:S(2)}, u32[]{:S(2)}) async-start(f32[8,72,128]{2,1,0:T(8,128)} %get-tuple-element.62), calls=%async_computation.1 | async-start | bytes 589824 | tf_op jit(solution)/shard_map/all_to_all | solution.py:518
  43.6 3.6 %collective-permute-start.1 = (f32[8,16,128]{2,1,0:T(8,128)S(1)}, f32[8,16,128]{2,1,0:T(8,128)S(1)}, u32[]{:S(2)}, u32[]{:S(2)}) collective-permute-start(f32[8,16,128]{2,1,0:T(8,128)S(1)} %get-tuple-element.64), channel_id=1, source_target_pairs={{0,4},{4,0},{8,12},{12,8},{16,20},{20,16},{24,28},{28,24},{32,36},... | collective-permute-start | bytes 196616 | tf_op jit(solution)/shard_map/ppermute | solution.py:527
  47.3 0.0 copy-done.4
  47.3 0.0 copy-done.5
  47.3 0.0 copy-done.10
  47.3 1.5 %reply_local_kernel.1 = (bf16[8,128,128]{2,1,0:T(8,128)(2,1)S(1)}, bf16[8,128,128]{2,1,0:T(8,128)(2,1)S(1)}, bf16[8,128,128]{2,1,0:T(8,128)(2,1)S(1)}, f32[128,1...) custom-call(s32[1]{0:T(128)S(6)} %copy.18.lengths, bf16[1,128,8,128]{3,2,1,0:T(8,128)(2,1)} %query.1, ...), custom_call_target="tpu_custom_call" | custom-call | flops 67108864 | bytes 1650696 | tf_op jit(solution)/shard_map/reply_local_kernel/pallas_call | solution.py:502
  48.8 0.0 collective-permute-done.1.other
  48.8 0.4 prompt_local_kernel.1
  49.2 0.0 copy-start.2
  49.2 0.6 copy-done.2
  49.9 4.3 %all-to-all-done.1.rows_received = f32[8,72,128]{2,1,0:T(8,128)S(1)} async-done(((f32[8,72,128]{2,1,0:T(8,128)}), f32[8,72,128]{2,1,0:T(8,128)S(1)}, u32[]{:S(2)}, u32[]{:S(2)}) %all-to-all-start.1) | async-done | bytes 294944 | tf_op jit(solution)/shard_map/all_to_all | solution.py:518
  54.2 0.3 fold_kernel.1
  54.5 0.0 copy-done.8
  54.5 0.0 copy-start.6
  54.5 12.4 %all_to_all.36.received = f32[8,80,128]{2,1,0:T(8,128)S(1)} all-to-all(f32[8,80,128]{2,1,0:T(8,128)S(1)} %get-tuple-element.70), channel_id=1, replica_groups={{0,8,16,24,32,40,48,56},{4,12,20,28,36,44,52,60},{1,9,17,25,33,41,49,57..., dimensions={0} | all-to-all | bytes 655360 | tf_op jit(solution)/shard_map/all_to_all | solution.py:523
  66.9 0.1 spread_kernel.1
  66.9 6.2 %collective-permute-start.2 = (f32[8,72,128]{2,1,0:T(8,128)S(1)}, f32[8,72,128]{2,1,0:T(8,128)S(1)}, u32[]{:S(2)}, u32[]{:S(2)}) collective-permute-start(f32[8,72,128]{2,1,0:T(8,128)S(1)} %get-tuple-element.74), channel_id=1, source_target_pairs={{0,4},{4,0},{8,12},{12,8},{16,20},{20,16},{24,28},{28,24},{32,36},... | collective-permute-start | bytes 884744 | tf_op jit(solution)/shard_map/ppermute | solution.py:527
  73.1 0.4 reply_masks_kernel.1
  73.5 0.7 collective-permute-done.2.other
  74.3 0.6 output_kernel.1
  74.9 8.0 %all_to_all.37.sums = f32[4,8,128]{2,1,0:T(8,128)S(1)} all-to-all(f32[4,8,128]{2,1,0:T(8,128)S(1)} %get-tuple-element.82), channel_id=1, replica_groups=mesh['sample'=8,'ctx'=16,'head'=4] {'head'}, dimensions={0} | all-to-all | bytes 32768 | tf_op jit(solution)/shard_map/all_to_all | solution.py:518
  83.0 0.7 grad_kernel.1
  83.6 3.7 %collective-permute-start.3 = (f32[8,72,128]{2,1,0:T(8,128)S(1)}, f32[8,72,128]{2,1,0:T(8,128)S(1)}, u32[]{:S(2)}, u32[]{:S(2)}) collective-permute-start(f32[8,72,128]{2,1,0:T(8,128)S(1)} %get-tuple-element.86), channel_id=1, source_target_pairs={{0,4},{4,0},{8,12},{12,8},{16,20},{20,16},{24,28},{28,24},{32,36},... | collective-permute-start | bytes 884744 | tf_op jit(solution)/shard_map/ppermute | solution.py:527
  87.3 1.9 %reply_back_kernel.1 = (f32[8,128,128]{2,1,0:T(8,128)S(1)}, f32[8,128,128]{2,1,0:T(8,128)S(1)}, f32[8,128,128]{2,1,0:T(8,128)S(1)}, f32[128,128]{1,0:T(8,128)S(1)}) custom-call(f32[8,72,128]{2,1,0:T(8,128)S(1)} %get-tuple-element.73.after_fold.mine, f32[8,72,128]{2,1,0:T(8,128)S(1)} %collective-permute-done.2.other, ...), custom_call_target="tpu_custom_call" | custom-call | flops 201326592 | bytes 4988928 | tf_op jit(solution)/shard_map/reply_back_kernel/pallas_call | solution.py:502
  89.2 0.0 collective-permute-done.3.other
  89.2 0.1 back_merge_kernel.1
  89.3 16.2 %all_to_all.38.received = f32[8,80,128]{2,1,0:T(8,128)S(1)} all-to-all(f32[8,80,128]{2,1,0:T(8,128)S(1)} %get-tuple-element.90), channel_id=1, replica_groups={{0,8,16,24,32,40,48,56},{4,12,20,28,36,44,52,60},{1,9,17,25,33,41,49,57..., dimensions={0} | all-to-all | bytes 655360 | tf_op jit(solution)/shard_map/all_to_all | solution.py:523
  105.5 1.0 back_fold_kernel.1
  106.5 3.5 %all-to-all-start.5 = ((f32[8,64,128]{2,1,0:T(8,128)}), f32[8,64,128]{2,1,0:T(8,128)S(1)}, u32[]{:S(2)}, u32[]{:S(2)}) async-start(f32[8,64,128]{2,1,0:T(8,128)} %back_fold_kernel.1), calls=%async_computation.5 | async-start | bytes 524288 | tf_op jit(solution)/shard_map/all_to_all | solution.py:518
  110.0 0.0 copy-start.9
  110.0 0.7 copy-done.9
  110.7 1.7 %prompt_mid_kernel.1 = (f32[8,128,128]{2,1,0:T(8,128)S(1)}, f32[8,16,128]{2,1,0:T(8,128)S(1)}, bf16[1,128,8,128]{3,2,1,0:T(8,128)(2,1)}) custom-call(f32[8,80,128]{2,1,0:T(8,128)S(1)} %all_to_all.38.received, f32[8,128]{1,0:T(8,128)S(1)} %get-tuple-element.63.blocks, f32[64,128]{1,0:T(8,128)S(1)} %copy-done.7, bf16[256,128]{1,0:T(8,128)(2,1)S(1)} %get-tuple-element.66.query, ...), custom_call_target="tpu_custom_call" | custom-call | flops 33554432 | bytes 2383872 | tf_op jit(solution)/shard_map/prompt_mid_kernel/pallas_call | solution.py:502
  112.4 2.3 %collective-permute-start.4 = (f32[8,16,128]{2,1,0:T(8,128)S(1)}, f32[8,16,128]{2,1,0:T(8,128)S(1)}, u32[]{:S(2)}, u32[]{:S(2)}) collective-permute-start(f32[8,16,128]{2,1,0:T(8,128)S(1)} %get-tuple-element.97), channel_id=1, source_target_pairs={{0,4},{4,0},{8,12},{12,8},{16,20},{20,16},{24,28},{28,24},{32,36},... | collective-permute-start | bytes 196616 | tf_op jit(solution)/shard_map/ppermute | solution.py:527
  114.8 0.9 collective-permute-done.4.swapped
  115.7 6.6 %all-to-all-done.5.rows_received = f32[8,64,128]{2,1,0:T(8,128)S(1)} async-done(((f32[8,64,128]{2,1,0:T(8,128)}), f32[8,64,128]{2,1,0:T(8,128)S(1)}, u32[]{:S(2)}, u32[]{:S(2)}) %all-to-all-start.5) | async-done | bytes 262176 | tf_op jit(solution)/shard_map/all_to_all | solution.py:518
  122.2 0.3 prompt_back_kernel.1
  122.5 19.8 %all_to_all.39.received = f32[8,128,128]{2,1,0:T(8,128)S(1)} all-to-all(f32[8,128,128]{2,1,0:T(8,128)S(1)} %prompt_back_kernel.1), channel_id=1, replica_groups={{0,8,16,24,32,40,48,56},{4,12,20,28,36,44,52,60},{1,9,17,25,33,41,49,57..., dimensions={0} | all-to-all | bytes 1048576 | tf_op jit(solution)/shard_map/all_to_all | solution.py:523
  142.3 0.1 back_spread_kernel.1
  142.4 3.1 %collective-permute-start.5 = (f32[8,88,128]{2,1,0:T(8,128)S(1)}, f32[8,88,128]{2,1,0:T(8,128)S(1)}, u32[]{:S(2)}, u32[]{:S(2)}) collective-permute-start(f32[8,88,128]{2,1,0:T(8,128)S(1)} %get-tuple-element.101), channel_id=1, source_target_pairs={{0,4},{4,0},{8,12},{12,8},{16,20},{20,16},{24,28},{28,24},{32,36},... | collective-permute-start | bytes 1081352 | tf_op jit(solution)/shard_map/ppermute | solution.py:527
  145.5 1.3 collective-permute-done.5.other
  146.8 0.0 copy-done.1
  146.8 1.5 %end_kernel.1 = (bf16[1,128,8,128]{3,2,1,0:T(8,128)(2,1)}, bf16[1,128,8,128]{3,2,1,0:T(8,128)(2,1)}, bf16[16,8,128]{2,1,0:T(8,128)(2,1)}, bf16[16,8,128]{2,1,0:T(8,128)(2,1)}, bf16[16,8,128]{2,1,0:T(8,128)(2,1)}) custom-call(f32[8,128,128]{2,1,0:T(8,128)S(1)} %all_to_all.39.received, f32[8,88,128]{2,1,0:T(8,128)S(1)} %get-tuple-element.100.mine, ...), custom_call_target="tpu_custom_call" | custom-call | flops 134217728 | bytes 5767168 | tf_op jit(solution)/shard_map/end_kernel/pallas_call | solution.py:502
  (12 shorter events, 0.0 us)
Async XLA Ops:
  3.0 10.1 %collective-permute-start = (f32[8,96,128]{2,1,0:T(8,128)S(1)}, f32[8,96,128]{2,1,0:T(8,128)S(1)}, u32[]{:S(2)}, u32[]{:S(2)}) collective-permute-start(f32[8,96,128]{2,1,0:T(8,128)S(1)} %get-tuple-element.59), channel_id=1, source_target_pairs={{0,4},{4,0},{8,12},{12,8},{16,20},{20,16},{24,28},{28,24},{32,36},... | collective-permute-start | bytes 1179656 | tf_op jit(solution)/shard_map/ppermute | solution.py:527
  35.2 12.1 %copy-start.4 = (f32[1,8,128]{2,1,0:T(8,128)S(1)}, f32[1,8,128]{2,1,0:T(8,128)}, u32[]{:S(2)}) copy-start(f32[1,8,128]{2,1,0:T(8,128)} %decay.7) | copy-start | bytes 12292
  35.2 12.1 %copy-start.5 = (bf16[16,8,128]{2,1,0:T(8,128)(2,1)S(1)}, bf16[16,8,128]{2,1,0:T(8,128)(2,1)}, u32[]{:S(2)}) copy-start(bf16[16,8,128]{2,1,0:T(8,128)(2,1)} %prompt_grad.1) | copy-start | bytes 98308
  35.2 19.0 %all-to-all-start.1 = ((f32[8,72,128]{2,1,0:T(8,128)}), f32[8,72,128]{2,1,0:T(8,128)S(1)}, u32[]{:S(2)}, u32[]{:S(2)}) async-start(f32[8,72,128]{2,1,0:T(8,128)} %get-tuple-element.62), calls=%async_computation.1 | async-start | bytes 589824 | tf_op jit(solution)/shard_map/all_to_all | solution.py:518
  43.6 3.6 %copy-start.10 = (bf16[8,128]{1,0:T(8,128)(2,1)S(1)}, bf16[8,128]{1,0:T(8,128)(2,1)}, u32[]{:S(2)}) copy-start(bf16[8,128]{1,0:T(8,128)(2,1)} %gain.1) | copy-start | bytes 6148
  43.6 5.2 %collective-permute-start.1 = (f32[8,16,128]{2,1,0:T(8,128)S(1)}, f32[8,16,128]{2,1,0:T(8,128)S(1)}, u32[]{:S(2)}, u32[]{:S(2)}) collective-permute-start(f32[8,16,128]{2,1,0:T(8,128)S(1)} %get-tuple-element.64), channel_id=1, source_target_pairs={{0,4},{4,0},{8,12},{12,8},{16,20},{20,16},{24,28},{28,24},{32,36},... | collective-permute-start | bytes 196616 | tf_op jit(solution)/shard_map/ppermute | solution.py:527
  49.2 0.6 copy-start.2
  49.9 4.6 %copy-start.8 = (f32[8,256]{1,0:T(8,128)}, f32[8,256]{1,0:T(8,128)S(1)}, u32[]{:S(2)}) copy-start(f32[8,256]{1,0:T(8,128)S(1)} %get-tuple-element.95.line) | copy-start | bytes 24580
  54.5 12.4 %copy-start.6 = (f32[64,128]{1,0:T(8,128)}, f32[64,128]{1,0:T(8,128)S(1)}, u32[]{:S(2)}) copy-start(f32[64,128]{1,0:T(8,128)S(1)} %get-tuple-element.92.start) | copy-start | bytes 98308
  66.9 7.3 %collective-permute-start.2 = (f32[8,72,128]{2,1,0:T(8,128)S(1)}, f32[8,72,128]{2,1,0:T(8,128)S(1)}, u32[]{:S(2)}, u32[]{:S(2)}) collective-permute-start(f32[8,72,128]{2,1,0:T(8,128)S(1)} %get-tuple-element.74), channel_id=1, source_target_pairs={{0,4},{4,0},{8,12},{12,8},{16,20},{20,16},{24,28},{28,24},{32,36},... | collective-permute-start | bytes 884744 | tf_op jit(solution)/shard_map/ppermute | solution.py:527
  83.6 5.6 %collective-permute-start.3 = (f32[8,72,128]{2,1,0:T(8,128)S(1)}, f32[8,72,128]{2,1,0:T(8,128)S(1)}, u32[]{:S(2)}, u32[]{:S(2)}) collective-permute-start(f32[8,72,128]{2,1,0:T(8,128)S(1)} %get-tuple-element.86), channel_id=1, source_target_pairs={{0,4},{4,0},{8,12},{12,8},{16,20},{20,16},{24,28},{28,24},{32,36},... | collective-permute-start | bytes 884744 | tf_op jit(solution)/shard_map/ppermute | solution.py:527
  89.2 16.3 %copy-start = (f32[8,128,128]{2,1,0:T(8,128)}, f32[8,128,128]{2,1,0:T(8,128)S(1)}, u32[]{:S(2)}) copy-start(f32[8,128,128]{2,1,0:T(8,128)S(1)} %get-tuple-element.103.value_local) | copy-start | bytes 1572868
  106.5 3.6 %copy-start.3 = (bf16[256,64]{1,0:T(8,128)(2,1)S(1)}, bf16[256,64]{1,0:T(8,128)(2,1)}, u32[]{:S(2)}) copy-start(bf16[256,64]{1,0:T(8,128)(2,1)} %copy-done.2) | copy-start | bytes 98308
  106.5 3.6 %copy-start.7 = (f32[64,128]{1,0:T(8,128)S(1)}, f32[64,128]{1,0:T(8,128)}, u32[]{:S(2)}) copy-start(f32[64,128]{1,0:T(8,128)} %copy-done.6) | copy-start | bytes 98308
  106.5 15.8 %all-to-all-start.5 = ((f32[8,64,128]{2,1,0:T(8,128)}), f32[8,64,128]{2,1,0:T(8,128)S(1)}, u32[]{:S(2)}, u32[]{:S(2)}) async-start(f32[8,64,128]{2,1,0:T(8,128)} %back_fold_kernel.1), calls=%async_computation.5 | async-start | bytes 524288 | tf_op jit(solution)/shard_map/all_to_all | solution.py:518
  110.0 0.7 copy-start.9
  112.4 3.2 %collective-permute-start.4 = (f32[8,16,128]{2,1,0:T(8,128)S(1)}, f32[8,16,128]{2,1,0:T(8,128)S(1)}, u32[]{:S(2)}, u32[]{:S(2)}) collective-permute-start(f32[8,16,128]{2,1,0:T(8,128)S(1)} %get-tuple-element.97), channel_id=1, source_target_pairs={{0,4},{4,0},{8,12},{12,8},{16,20},{20,16},{24,28},{28,24},{32,36},... | collective-permute-start | bytes 196616 | tf_op jit(solution)/shard_map/ppermute | solution.py:527
  142.3 4.4 %copy-start.1 = (f32[8,128,128]{2,1,0:T(8,128)S(1)}, f32[8,128,128]{2,1,0:T(8,128)}, u32[]{:S(2)}) copy-start(f32[8,128,128]{2,1,0:T(8,128)} %copy-done) | copy-start | bytes 1572868
  142.4 4.4 %collective-permute-start.5 = (f32[8,88,128]{2,1,0:T(8,128)S(1)}, f32[8,88,128]{2,1,0:T(8,128)S(1)}, u32[]{:S(2)}, u32[]{:S(2)}) collective-permute-start(f32[8,88,128]{2,1,0:T(8,128)S(1)} %get-tuple-element.101), channel_id=1, source_target_pairs={{0,4},{4,0},{8,12},{12,8},{16,20},{20,16},{24,28},{28,24},{32,36},... | collective-permute-start | bytes 1081352 | tf_op jit(solution)/shard_map/ppermute | solution.py:527

commit v9 on v8

--- a/solution.py
+++ b/solution.py
@@ -180,10 +180,11 @@
             ref[h, 0:64, :] = half
 
 
-def reply_masks_kernel(weights, value, decay, after_fold, mask_out, local_out):
+def reply_masks_kernel(weights, value, decay, after_fold, mask_out, local_out, to_end_out):
     del after_fold
     lines = running_rows(decay[0])
     columns = running_columns(decay[0])
+    to_end_out[...] = wide_columns(jnp.exp(columns[T - 1 : T, :] - columns))
     for h in range(HEADS):
         mask_out[h] = masking(columns[:, h : h + 1], lines[h : h + 1])
         local_out[h] = dot(weights[h], value[h], 1, 0)
@@ -387,11 +388,8 @@
 
 
 def reply_back_kernel(
-    mine, other, out_grad, query, key, value, weights, masks, growth, decay,
-    query_grad, key_local, value_local, to_end_out,
-):
-    columns = running_columns(decay[0])
-    to_end_out[...] = wide_columns(jnp.exp(columns[T - 1 : T, :] - columns))
+    mine, other, out_grad, query, key, value, weights, masks, growth, query_grad, key_local, value_local
+):
     for h in range(HEADS):
         state = jnp.concatenate(in_order(mine[h, 0:64, :], other[h, 0:64, :]), axis=0)
         og = out_grad[h]
@@ -636,16 +634,16 @@
         kept=(0,),
     )
     other = swap_cores(theirs)
-    masks, local = run(
+    masks, local, to_end = run(
         reply_masks_kernel,
-        [BY_HEAD_WIDE, BY_HEAD_WIDE],
+        [BY_HEAD_WIDE, BY_HEAD_WIDE, ((T, D), F32)],
         [],
         weights,
         value,
         reply_decay,
         mine,
         flops=work,
-        kept=(0, 1),
+        kept=(0, 1, 2),
     )
     sent, outputs, prompt_outputs = run(
         output_kernel,
@@ -679,9 +677,9 @@
         kept=(0, 2),
     )
     back_other = swap_cores(back_theirs)
-    reply_query_wide, key_local, value_local, to_end = run(
+    reply_query_wide, key_local, value_local = run(
         reply_back_kernel,
-        [BY_HEAD_WIDE, BY_HEAD_WIDE, BY_HEAD_WIDE, ((T, D), F32)],
+        [BY_HEAD_WIDE, BY_HEAD_WIDE, BY_HEAD_WIDE],
         [],
         mine,
         other,
@@ -692,9 +690,8 @@
         weights,
         masks,
         growth,
-        reply_decay,
         flops=6 * work,
-        kept=(0, 1, 2, 3),
+        kept=(0, 1, 2),
     )
     sent, last_back = run(
         back_merge_kernel,
@@ -703,7 +700,7 @@
         back_mine,
         back_other,
         block_totals,
-        to_end,
+        reply_query_wide,
         kept=(1,),
     )
     backs = exchange_chips(sent)

time: 149 us -> 150 us (level)
  no operation moved by 1% of the time
where the time goes in v9:
time: 150 us; the launch traced here: 149 us
  blocking collectives  77 us (51%)
  starting transfers between devices  39.7 us (26%)
  waiting for transfers between devices  15.8 us (11%)
  Pallas kernels  13.5 us (9%)
  between operations  1.5 us (1%)
    all_to_all x4, blocking collectives, exchange_chips(): return lax.all_to_all(x, 'ctx', 0, 0, axis_index_groups=groups, tiled=True)  69 us
    ppermute x6, starting transfers between devices, swap_cores(): return lax.ppermute(x, 'ctx', [(i, i ^ 1) for i in range(CTX)])  27.7 us
    pallas_call x17, Pallas kernels, run(): pl.pallas_call(kernel, out_shape=[pltpu.VMEM(shape, kind) if i in kept el...  13.5 us
    all_to_all x2, starting transfers between devices, exchange(): return lax.all_to_all(x, axis, 0, 0, tiled=True)  12 us
    all_to_all x2, waiting for transfers between devices, exchange(): return lax.all_to_all(x, axis, 0, 0, tiled=True)  11.6 us
    all_to_all x1, blocking collectives, exchange(): return lax.all_to_all(x, axis, 0, 0, tiled=True)  8.02 us
    ppermute x6, waiting for transfers between devices, swap_cores(): return lax.ppermute(x, 'ctx', [(i, i ^ 1) for i in range(CTX)])  4.24 us
  transfers between devices with their start and end apart: 8, of which 6 were waited for; matrix products, arithmetic and copies ran while one was open for 0% of the time, Pallas kernels for 4%

profile of v9, /device:TPU:1, one launch (start us, length us, event | category | flops | bytes accessed | tf_op | source)
XLA Modules:
  0.0 148.9 jit_solution(17786748070180828121)
XLA Ops:
  1.3 1.8 %send_kernel.1 = (f32[8,96,128]{2,1,0:T(8,128)S(1)}, f32[8,96,128]{2,1,0:T(8,128)S(1)}, f32[8,16,128]{2,1,0:T(8,128)S(1)}, bf16[8,128,128]{2,1,0:T(8,128)(2,1)S(1)}, bf16[8,128,128]{2,1,0:T(8,128)(2,1)S(1)}) custom-call(s32[1]{0:T(128)S(6)} %copy.18.lengths, bf16[1,128,8,128]{3,2,1,0:T(8,128)(2,1)} %key.1, bf16[1,128,8,128]{3,2,1,0:T(8,128)(2,1)} %value.1, ...), custom_call_target="tpu_custom_call" | custom-call | flops 67108864 | bytes 1254408 | tf_op jit(solution)/shard_map/send_kernel/pallas_call | solution.py:500
  3.0 8.8 %collective-permute-start = (f32[8,96,128]{2,1,0:T(8,128)S(1)}, f32[8,96,128]{2,1,0:T(8,128)S(1)}, u32[]{:S(2)}, u32[]{:S(2)}) collective-permute-start(f32[8,96,128]{2,1,0:T(8,128)S(1)} %get-tuple-element.59), channel_id=1, source_target_pairs={{0,4},{4,0},{8,12},{12,8},{16,20},{20,16},{24,28},{28,24},{32,36},... | collective-permute-start | bytes 1179656 | tf_op jit(solution)/shard_map/ppermute | solution.py:525
  11.8 1.3 collective-permute-done.other
  13.2 0.1 merge_kernel.1
  13.3 20.7 %all_to_all.35.received = f32[8,136,128]{2,1,0:T(8,128)S(1)} all-to-all(f32[8,136,128]{2,1,0:T(8,128)S(1)} %get-tuple-element.61), channel_id=1, replica_groups={{0,8,16,24,32,40,48,56},{4,12,20,28,36,44,52,60},{1,9,17,25,33,41,49,57..., dimensions={0} | all-to-all | bytes 1114112 | tf_op jit(solution)/shard_map/all_to_all | solution.py:521
  33.9 1.2 prompt_row_kernel.1
  35.2 8.5 %all-to-all-start.1 = ((f32[8,72,128]{2,1,0:T(8,128)}), f32[8,72,128]{2,1,0:T(8,128)S(1)}, u32[]{:S(2)}, u32[]{:S(2)}) async-start(f32[8,72,128]{2,1,0:T(8,128)} %get-tuple-element.62), calls=%async_computation.1 | async-start | bytes 589824 | tf_op jit(solution)/shard_map/all_to_all | solution.py:516
  43.6 3.6 %collective-permute-start.1 = (f32[8,16,128]{2,1,0:T(8,128)S(1)}, f32[8,16,128]{2,1,0:T(8,128)S(1)}, u32[]{:S(2)}, u32[]{:S(2)}) collective-permute-start(f32[8,16,128]{2,1,0:T(8,128)S(1)} %get-tuple-element.64), channel_id=1, source_target_pairs={{0,4},{4,0},{8,12},{12,8},{16,20},{20,16},{24,28},{28,24},{32,36},... | collective-permute-start | bytes 196616 | tf_op jit(solution)/shard_map/ppermute | solution.py:525
  47.2 0.0 copy-done.4
  47.3 0.0 copy-done.5
  47.3 0.0 copy-done.8
  47.3 1.5 %reply_local_kernel.1 = (bf16[8,128,128]{2,1,0:T(8,128)(2,1)S(1)}, bf16[8,128,128]{2,1,0:T(8,128)(2,1)S(1)}, bf16[8,128,128]{2,1,0:T(8,128)(2,1)S(1)}, f32[128,1...) custom-call(s32[1]{0:T(128)S(6)} %copy.18.lengths, bf16[1,128,8,128]{3,2,1,0:T(8,128)(2,1)} %query.1, ...), custom_call_target="tpu_custom_call" | custom-call | flops 67108864 | bytes 1650696 | tf_op jit(solution)/shard_map/reply_local_kernel/pallas_call | solution.py:500
  48.8 0.0 collective-permute-done.1.other
  48.8 0.4 prompt_local_kernel.1
  49.2 0.0 copy-start.2
  49.2 0.6 copy-done.2
  49.9 4.3 %all-to-all-done.1.rows_received = f32[8,72,128]{2,1,0:T(8,128)S(1)} async-done(((f32[8,72,128]{2,1,0:T(8,128)}), f32[8,72,128]{2,1,0:T(8,128)S(1)}, u32[]{:S(2)}, u32[]{:S(2)}) %all-to-all-start.1) | async-done | bytes 294944 | tf_op jit(solution)/shard_map/all_to_all | solution.py:516
  54.2 0.3 fold_kernel.1
  54.5 0.0 copy-done.6
  54.5 12.4 %all_to_all.36.received = f32[8,80,128]{2,1,0:T(8,128)S(1)} all-to-all(f32[8,80,128]{2,1,0:T(8,128)S(1)} %get-tuple-element.70), channel_id=1, replica_groups={{0,8,16,24,32,40,48,56},{4,12,20,28,36,44,52,60},{1,9,17,25,33,41,49,57..., dimensions={0} | all-to-all | bytes 655360 | tf_op jit(solution)/shard_map/all_to_all | solution.py:521
  66.9 0.1 spread_kernel.1
  66.9 6.2 %collective-permute-start.2 = (f32[8,72,128]{2,1,0:T(8,128)S(1)}, f32[8,72,128]{2,1,0:T(8,128)S(1)}, u32[]{:S(2)}, u32[]{:S(2)}) collective-permute-start(f32[8,72,128]{2,1,0:T(8,128)S(1)} %get-tuple-element.74), channel_id=1, source_target_pairs={{0,4},{4,0},{8,12},{12,8},{16,20},{20,16},{24,28},{28,24},{32,36},... | collective-permute-start | bytes 884744 | tf_op jit(solution)/shard_map/ppermute | solution.py:525
  73.1 0.4 reply_masks_kernel.1
  73.5 0.7 collective-permute-done.2.other
  74.3 0.6 output_kernel.1
  74.9 8.0 %all_to_all.37.sums = f32[4,8,128]{2,1,0:T(8,128)S(1)} all-to-all(f32[4,8,128]{2,1,0:T(8,128)S(1)} %get-tuple-element.82), channel_id=1, replica_groups=mesh['sample'=8,'ctx'=16,'head'=4] {'head'}, dimensions={0} | all-to-all | bytes 32768 | tf_op jit(solution)/shard_map/all_to_all | solution.py:516
  82.9 0.7 grad_kernel.1
  83.6 3.7 %collective-permute-start.3 = (f32[8,72,128]{2,1,0:T(8,128)S(1)}, f32[8,72,128]{2,1,0:T(8,128)S(1)}, u32[]{:S(2)}, u32[]{:S(2)}) collective-permute-start(f32[8,72,128]{2,1,0:T(8,128)S(1)} %get-tuple-element.86), channel_id=1, source_target_pairs={{0,4},{4,0},{8,12},{12,8},{16,20},{20,16},{24,28},{28,24},{32,36},... | collective-permute-start | bytes 884744 | tf_op jit(solution)/shard_map/ppermute | solution.py:525
  87.3 1.8 %reply_back_kernel.1 = (f32[8,128,128]{2,1,0:T(8,128)S(1)}, f32[8,128,128]{2,1,0:T(8,128)S(1)}, f32[8,128,128]{2,1,0:T(8,128)S(1)}) custom-call(f32[8,72,128]{2,1,0:T(8,128)S(1)} %get-tuple-element.73.after_fold.mine, f32[8,72,128]{2,1,0:T(8,128)S(1)} %collective-permute-done.2.other, bf16[8,128,128]{2,1,0:T(8,128)(2,1)S(1)} %get-tuple-element.87.out_grad, ...), custom_call_target="tpu_custom_call" | custom-call | flops 201326592 | bytes 4980736 | tf_op jit(solution)/shard_map/reply_back_kernel/pallas_call | solution.py:500
  89.2 0.0 copy-start
  89.2 0.0 collective-permute-done.3.other
  89.2 0.1 back_merge_kernel.1
  89.3 0.7 copy-done
  89.9 16.2 %all_to_all.38.received = f32[8,80,128]{2,1,0:T(8,128)S(1)} all-to-all(f32[8,80,128]{2,1,0:T(8,128)S(1)} %get-tuple-element.90), channel_id=1, replica_groups={{0,8,16,24,32,40,48,56},{4,12,20,28,36,44,52,60},{1,9,17,25,33,41,49,57..., dimensions={0} | all-to-all | bytes 655360 | tf_op jit(solution)/shard_map/all_to_all | solution.py:521
  106.1 1.0 back_fold_kernel.1
  107.1 3.5 %all-to-all-start.5 = ((f32[8,64,128]{2,1,0:T(8,128)}), f32[8,64,128]{2,1,0:T(8,128)S(1)}, u32[]{:S(2)}, u32[]{:S(2)}) async-start(f32[8,64,128]{2,1,0:T(8,128)} %back_fold_kernel.1), calls=%async_computation.5 | async-start | bytes 524288 | tf_op jit(solution)/shard_map/all_to_all | solution.py:516
  110.6 0.0 copy-done.3
  110.7 0.0 copy-done.7
  110.7 1.7 %prompt_mid_kernel.1 = (f32[8,128,128]{2,1,0:T(8,128)S(1)}, f32[8,16,128]{2,1,0:T(8,128)S(1)}, bf16[1,128,8,128]{3,2,1,0:T(8,128)(2,1)}) custom-call(f32[8,80,128]{2,1,0:T(8,128)S(1)} %all_to_all.38.received, f32[8,128]{1,0:T(8,128)S(1)} %get-tuple-element.63.blocks, f32[64,128]{1,0:T(8,128)S(1)} %get-tuple-element.92.start, ...), custom_call_target="tpu_custom_call" | custom-call | flops 33554432 | bytes 2383872 | tf_op jit(solution)/shard_map/prompt_mid_kernel/pallas_call | solution.py:500
  112.4 2.3 %collective-permute-start.4 = (f32[8,16,128]{2,1,0:T(8,128)S(1)}, f32[8,16,128]{2,1,0:T(8,128)S(1)}, u32[]{:S(2)}, u32[]{:S(2)}) collective-permute-start(f32[8,16,128]{2,1,0:T(8,128)S(1)} %get-tuple-element.96), channel_id=1, source_target_pairs={{0,4},{4,0},{8,12},{12,8},{16,20},{20,16},{24,28},{28,24},{32,36},... | collective-permute-start | bytes 196616 | tf_op jit(solution)/shard_map/ppermute | solution.py:525
  114.7 0.9 collective-permute-done.4.swapped
  115.6 7.2 %all-to-all-done.5.rows_received = f32[8,64,128]{2,1,0:T(8,128)S(1)} async-done(((f32[8,64,128]{2,1,0:T(8,128)}), f32[8,64,128]{2,1,0:T(8,128)S(1)}, u32[]{:S(2)}, u32[]{:S(2)}) %all-to-all-start.5) | async-done | bytes 262176 | tf_op jit(solution)/shard_map/all_to_all | solution.py:516
  122.9 0.3 prompt_back_kernel.1
  123.1 19.8 %all_to_all.39.received = f32[8,128,128]{2,1,0:T(8,128)S(1)} all-to-all(f32[8,128,128]{2,1,0:T(8,128)S(1)} %prompt_back_kernel.1), channel_id=1, replica_groups={{0,8,16,24,32,40,48,56},{4,12,20,28,36,44,52,60},{1,9,17,25,33,41,49,57..., dimensions={0} | all-to-all | bytes 1048576 | tf_op jit(solution)/shard_map/all_to_all | solution.py:521
  143.0 0.1 back_spread_kernel.1
  143.0 3.1 %collective-permute-start.5 = (f32[8,88,128]{2,1,0:T(8,128)S(1)}, f32[8,88,128]{2,1,0:T(8,128)S(1)}, u32[]{:S(2)}, u32[]{:S(2)}) collective-permute-start(f32[8,88,128]{2,1,0:T(8,128)S(1)} %get-tuple-element.100), channel_id=1, source_target_pairs={{0,4},{4,0},{8,12},{12,8},{16,20},{20,16},{24,28},{28,24},{32,36},... | collective-permute-start | bytes 1081352 | tf_op jit(solution)/shard_map/ppermute | solution.py:525
  146.1 1.3 collective-permute-done.5.other
  147.4 1.5 %end_kernel.1 = (bf16[1,128,8,128]{3,2,1,0:T(8,128)(2,1)}, bf16[1,128,8,128]{3,2,1,0:T(8,128)(2,1)}, bf16[16,8,128]{2,1,0:T(8,128)(2,1)}, bf16[16,8,128]{2,1,0:T(8,128)(2,1)}, bf16[16,8,128]{2,1,0:T(8,128)(2,1)}) custom-call(f32[8,128,128]{2,1,0:T(8,128)S(1)} %all_to_all.39.received, f32[8,88,128]{2,1,0:T(8,128)S(1)} %get-tuple-element.99.mine, ...), custom_call_target="tpu_custom_call" | custom-call | flops 134217728 | bytes 5767168 | tf_op jit(solution)/shard_map/end_kernel/pallas_call | solution.py:500
  (8 shorter events, 0.0 us)
Async XLA Ops:
  3.0 10.1 %collective-permute-start = (f32[8,96,128]{2,1,0:T(8,128)S(1)}, f32[8,96,128]{2,1,0:T(8,128)S(1)}, u32[]{:S(2)}, u32[]{:S(2)}) collective-permute-start(f32[8,96,128]{2,1,0:T(8,128)S(1)} %get-tuple-element.59), channel_id=1, source_target_pairs={{0,4},{4,0},{8,12},{12,8},{16,20},{20,16},{24,28},{28,24},{32,36},... | collective-permute-start | bytes 1179656 | tf_op jit(solution)/shard_map/ppermute | solution.py:525
  35.1 12.1 %copy-start.4 = (f32[1,8,128]{2,1,0:T(8,128)S(1)}, f32[1,8,128]{2,1,0:T(8,128)}, u32[]{:S(2)}) copy-start(f32[1,8,128]{2,1,0:T(8,128)} %decay.5) | copy-start | bytes 12292
  35.1 12.1 %copy-start.5 = (bf16[16,8,128]{2,1,0:T(8,128)(2,1)S(1)}, bf16[16,8,128]{2,1,0:T(8,128)(2,1)}, u32[]{:S(2)}) copy-start(bf16[16,8,128]{2,1,0:T(8,128)(2,1)} %prompt_grad.1) | copy-start | bytes 98308
  35.2 19.0 %all-to-all-start.1 = ((f32[8,72,128]{2,1,0:T(8,128)}), f32[8,72,128]{2,1,0:T(8,128)S(1)}, u32[]{:S(2)}, u32[]{:S(2)}) async-start(f32[8,72,128]{2,1,0:T(8,128)} %get-tuple-element.62), calls=%async_computation.1 | async-start | bytes 589824 | tf_op jit(solution)/shard_map/all_to_all | solution.py:516
  43.6 3.6 %copy-start.8 = (bf16[8,128]{1,0:T(8,128)(2,1)S(1)}, bf16[8,128]{1,0:T(8,128)(2,1)}, u32[]{:S(2)}) copy-start(bf16[8,128]{1,0:T(8,128)(2,1)} %gain.1) | copy-start | bytes 6148
  43.6 5.2 %collective-permute-start.1 = (f32[8,16,128]{2,1,0:T(8,128)S(1)}, f32[8,16,128]{2,1,0:T(8,128)S(1)}, u32[]{:S(2)}, u32[]{:S(2)}) collective-permute-start(f32[8,16,128]{2,1,0:T(8,128)S(1)} %get-tuple-element.64), channel_id=1, source_target_pairs={{0,4},{4,0},{8,12},{12,8},{16,20},{20,16},{24,28},{28,24},{32,36},... | collective-permute-start | bytes 196616 | tf_op jit(solution)/shard_map/ppermute | solution.py:525
  49.2 0.6 copy-start.2
  49.8 4.6 %copy-start.6 = (f32[8,256]{1,0:T(8,128)}, f32[8,256]{1,0:T(8,128)S(1)}, u32[]{:S(2)}) copy-start(f32[8,256]{1,0:T(8,128)S(1)} %get-tuple-element.95.line) | copy-start | bytes 24580
  66.9 7.4 %collective-permute-start.2 = (f32[8,72,128]{2,1,0:T(8,128)S(1)}, f32[8,72,128]{2,1,0:T(8,128)S(1)}, u32[]{:S(2)}, u32[]{:S(2)}) collective-permute-start(f32[8,72,128]{2,1,0:T(8,128)S(1)} %get-tuple-element.74), channel_id=1, source_target_pairs={{0,4},{4,0},{8,12},{12,8},{16,20},{20,16},{24,28},{28,24},{32,36},... | collective-permute-start | bytes 884744 | tf_op jit(solution)/shard_map/ppermute | solution.py:525
  83.6 5.6 %collective-permute-start.3 = (f32[8,72,128]{2,1,0:T(8,128)S(1)}, f32[8,72,128]{2,1,0:T(8,128)S(1)}, u32[]{:S(2)}, u32[]{:S(2)}) collective-permute-start(f32[8,72,128]{2,1,0:T(8,128)S(1)} %get-tuple-element.86), channel_id=1, source_target_pairs={{0,4},{4,0},{8,12},{12,8},{16,20},{20,16},{24,28},{28,24},{32,36},... | collective-permute-start | bytes 884744 | tf_op jit(solution)/shard_map/ppermute | solution.py:525
  89.2 0.8 copy-start
  107.1 3.6 %copy-start.3 = (bf16[256,64]{1,0:T(8,128)(2,1)S(1)}, bf16[256,64]{1,0:T(8,128)(2,1)}, u32[]{:S(2)}) copy-start(bf16[256,64]{1,0:T(8,128)(2,1)} %copy-done.2) | copy-start | bytes 98308
  107.1 3.6 %copy-start.7 = (f32[8,256]{1,0:T(8,128)S(1)}, f32[8,256]{1,0:T(8,128)}, u32[]{:S(2)}) copy-start(f32[8,256]{1,0:T(8,128)} %copy-done.6) | copy-start | bytes 24580
  107.1 15.8 %all-to-all-start.5 = ((f32[8,64,128]{2,1,0:T(8,128)}), f32[8,64,128]{2,1,0:T(8,128)S(1)}, u32[]{:S(2)}, u32[]{:S(2)}) async-start(f32[8,64,128]{2,1,0:T(8,128)} %back_fold_kernel.1), calls=%async_computation.5 | async-start | bytes 524288 | tf_op jit(solution)/shard_map/all_to_all | solution.py:516
  112.4 3.2 %collective-permute-start.4 = (f32[8,16,128]{2,1,0:T(8,128)S(1)}, f32[8,16,128]{2,1,0:T(8,128)S(1)}, u32[]{:S(2)}, u32[]{:S(2)}) collective-permute-start(f32[8,16,128]{2,1,0:T(8,128)S(1)} %get-tuple-element.96), channel_id=1, source_target_pairs={{0,4},{4,0},{8,12},{12,8},{16,20},{20,16},{24,28},{28,24},{32,36},... | collective-permute-start | bytes 196616 | tf_op jit(solution)/shard_map/ppermute | solution.py:525
  143.0 4.4 %copy-start.1 = (f32[8,128,128]{2,1,0:T(8,128)S(1)}, f32[8,128,128]{2,1,0:T(8,128)}, u32[]{:S(2)}) copy-start(f32[8,128,128]{2,1,0:T(8,128)} %copy-done) | copy-start | bytes 1572868
  143.0 4.4 %collective-permute-start.5 = (f32[8,88,128]{2,1,0:T(8,128)S(1)}, f32[8,88,128]{2,1,0:T(8,128)S(1)}, u32[]{:S(2)}, u32[]{:S(2)}) collective-permute-start(f32[8,88,128]{2,1,0:T(8,128)S(1)} %get-tuple-element.100), channel_id=1, source_target_pairs={{0,4},{4,0},{8,12},{12,8},{16,20},{20,16},{24,28},{28,24},{32,36},... | collective-permute-start | bytes 1081352 | tf_op jit(solution)/shard_map/ppermute | solution.py:525
